TPU v7x, 256 devices: a whole 4x4x8 slice. The times are simulated.
256 devices in a mesh: region: 64 (over z, x, core), sub: 4 (over y).
Axes of the slice: x: 4, y: 4, z: 8, core: 2. Of those that a mesh axis runs over, the one named last changes fastest.
Arguments:
- points: float32 [3, 1024, 512], P(None, 'region'), may hold values from 0 to 64, as said below
- noise_var: float32 [1024, 512], P('region'), may hold values from 0.5 to 4
- right_sides: float32 [1024, 16, 512], P('region'), may hold values from -14 to 14
- pair_list: int32 [64, 4, 2, 80], P('region', 'sub'), may hold values from 0 to 31, as said below
- pair_count: int32 [64, 4], P('region', 'sub'), may hold values from 0 to 80, as said below
Outputs:
- solution: float32 [1024, 16, 512], P(('region', 'sub'))
Inputs may be any that keep to these rules, and one draw needn't show every extreme that they name: `points`: block b is a unit cell of a grid of 64 x 4 x 4 cells: region r holds layer r along the first coordinate, its 16 blocks each layer in Morton order of the other two cell indices; every point of a block lies in its cell. `pair_list`: in each device's slots below its pair_count stand pairs (i, j): i a block of the device's region counted from 0, j a block of the region or 16 plus a block of the next region's first layer. Over the devices of a region, every unordered pair of a block of the region and a block of the region or the next region whose cells differ by at most one in every index is listed exactly once, with its first entry in the region. Other slots hold 0. `pair_count`: in every region but the last one device lists exactly 80 pairs.
All inputs are finite; a program needn't handle non-finite values.
Results may differ from a plain program's by a relative error of at most 0.00036.
Values may be sent and summed in bfloat16 or wider, within the bound.
No kernel may reach another device: no remote copies, remote signals or barrier semaphores. Data moves between devices by JAX's collectives and lax.ppermute only.
A program may use at most 64 MiB of HBM per device.

v0:
```python
import jax
import jax.numpy as jnp
from jax import lax
from jax.sharding import PartitionSpec as P

ITERS = 2


support_radius = 1.0
tile_group = 8


def passed_along(value, axis, steps):
    count = lax.axis_size(axis)
    first, last = (max(0, -steps), min(count, count - steps))
    return lax.ppermute(value, axis, [(source, source + steps) for source in range(first, last)])


def kernel_tile(left_points, right_points):
    squared = jnp.zeros(
        (left_points.shape[0], left_points.shape[2], right_points.shape[2]), jnp.float32
    )
    for component in range(3):
        spread = left_points[:, component, :, None] - right_points[:, component, None, :]
        squared = squared + spread * spread
    radius = jnp.sqrt(squared) / support_radius
    falloff = jnp.maximum(1.0 - radius, 0.0)
    return (falloff**4 * (4.0 * radius + 1.0)).astype(jnp.bfloat16)


def inner_products(left_field, right_field):
    return jnp.einsum("brp,bsp->rs", left_field, right_field, precision=lax.Precision.HIGHEST)


def combine_columns(matrix, vectors):
    return jnp.einsum("rs,brp->bsp", matrix, vectors, precision=lax.Precision.HIGHEST)


def spd_solve(matrix, right_part):
    lower = jnp.linalg.cholesky(matrix)
    middle = lax.linalg.triangular_solve(lower, right_part, left_side=True, lower=True)
    return lax.linalg.triangular_solve(lower, middle, left_side=True, lower=True, transpose_a=True)


def global_sum(matrix):
    summed = lax.psum(matrix, "region")
    return summed


def local(points, noise_var, right_sides, pair_list, pair_count):
    blocks = right_sides.shape[0]
    slots = pair_list.shape[3]
    members = lax.axis_size("sub")
    member = lax.axis_index("sub")
    portion = blocks // members
    pair_rows = pair_list[0, 0]
    pair_total = pair_count[0, 0]
    block_points = jnp.transpose(points, (1, 0, 2))
    next_points = passed_along(block_points, "region", -1)
    all_points = jnp.concatenate([block_points, next_points], axis=0)
    residual = right_sides
    solution = jnp.zeros(residual.shape, jnp.float32)
    directions = residual
    current = global_sum(inner_products(residual, residual))
    for sweep in range(ITERS):
        rounded = directions.astype(jnp.bfloat16)
        following = passed_along(rounded, "region", -1)
        extended = jnp.concatenate([rounded, following], axis=0)
        blank_terms = jnp.zeros(extended.shape, jnp.float32)

        def one_group(group, totals):
            ranks = group * tile_group + jnp.arange(tile_group, dtype=jnp.int32)
            live = ranks < pair_total
            clipped = jnp.minimum(ranks, slots - 1)
            rows_left = pair_rows[0, clipped]
            rows_right = pair_rows[1, clipped]
            tiles = kernel_tile(all_points[rows_left], all_points[rows_right])
            to_left = jnp.einsum(
                "grb,gab->gra", extended[rows_right], tiles, preferred_element_type=jnp.float32
            )
            to_right = jnp.einsum(
                "gra,gab->grb", extended[rows_left], tiles, preferred_element_type=jnp.float32
            )
            weight_left = live.astype(jnp.float32)[:, None, None]
            weight_right = (live & (rows_left != rows_right)).astype(jnp.float32)[:, None, None]
            totals = totals.at[rows_left].add(to_left * weight_left)
            return totals.at[rows_right].add(to_right * weight_right)

        groups = (pair_total + tile_group - 1) // tile_group
        terms = lax.fori_loop(0, groups, one_group, blank_terms)
        earlier = passed_along(terms[blocks:].astype(jnp.bfloat16), "region", 1).astype(jnp.float32)
        summed = lax.psum(terms[:blocks] + earlier, "sub")
        image = summed + noise_var[:, None, :] * directions
        curvature = global_sum(inner_products(directions, image))
        step_size = spd_solve(curvature, current)
        solution = solution + combine_columns(step_size, directions)
        residual = residual - combine_columns(step_size, image)
        if sweep + 1 < ITERS:
            following_norm = global_sum(inner_products(residual, residual))
        if sweep + 1 < ITERS:
            momentum = spd_solve(current, following_norm)
            directions = residual + combine_columns(momentum, directions)
            current = following_norm
    result = lax.dynamic_slice_in_dim(solution, member * portion, portion, 0)
    return result


def solution(mesh):
    return jax.shard_map(
        local,
        mesh=mesh,
        in_specs=(
            P(None, "region", None),
            P("region", None),
            P("region", None, None),
            P("region", "sub", None, None),
            P("region", "sub"),
        ),
        out_specs=P(("region", "sub"), None, None),
        check_vma=False,
    )
```

profile of v0, /device:TPU:8, one launch (start us, length us, event | category | flops | bytes accessed | tf_op | source)
XLA Modules:
  0.0 1103.4 jit_solution(13947209003521113657)
XLA Ops:
  6.5 1.1 convert_element_type.48
  7.6 1.3 collective-permute-start
  8.9 1.0 copy.52
  9.9 1.3 collective-permute-start.1
  11.9 1.9 collective-permute-done.1
  14.5 86.3 %while.20 = (s32[]{:T(128)}, f32[32,16,512]{2,1,0:T(8,128)S(1)}, s32[]{:T(128)}, s32[2,80]{1,0:T(2,128)S(1)}, bf16[32,16,512]{2,1,0:T(8,128)(2,1)S(1)}, /*index=...) while((s32[]{:T(128)}, f32[32,16,512]{2,1,0:T(8,128)S(1)}, s32[]{:T(128)}, ...), condition=%wide.region_3.4_spmd, body=%wide.region_0.3_spmd.sunk | while | flops 201591008 | bytes 3679233 | solution.py:90
  18.4 7.6 fusion.105
  27.5 7.6 fusion.106
  40.0 7.6 fusion.105
  49.1 7.6 fusion.106
  61.6 7.6 fusion.105
  70.7 7.6 fusion.106
  83.1 7.6 fusion.105
  90.8 0.9 scatter_fusion
  92.2 7.6 fusion.106
  99.9 0.9 scatter_fusion.1
  100.8 5.6 collective-permute-start.2
  106.4 1.1 collective-permute-done.2
  107.6 0.9 convert_add_fusion.1
  109.3 184.3 %all-reduce.8.cloned.1.call-done = f32[16,16,512]{2,1,0:T(8,128)} async-done(((f32[16,16,512]{2,1,0:T(8,128)}), f32[16,16,512]{2,1,0:T(8,128)}) %all-reduce.8.cloned.1.call-update) | async-done | bytes 524304 | tf_op jit(solution)/shard_map/psum | solution.py:92
  293.7 1.9 convolution_bitcast_fusion.10
  295.6 249.8 %all-reduce.4 = (f32[16,16]{0,1:T(8,128)S(1)}, f32[16,16]{0,1:T(8,128)S(1)}) all-reduce(f32[16,16]{0,1:T(8,128)S(1)} %convolution_bitcast_fusion.9, f32[16,16]{0,1:T(8,128)S(1)} %convolution_bitcast_fusion.10), channel_id=1, replica_groups=mesh['region'=64,'sub'=4] {'region'}, use_global_device_ids=true, to_apply=%region_8.10 | all-reduce | flops 512 | bytes 4096 | tf_op jit(solution)/shard_map/psum | solution.py:46
  545.5 1.5 cholesky.59
  548.3 1.2 custom-call.21
  551.4 126.1 %psum.45 = f32[16,16]{1,0:T(8,128)S(1)} all-reduce(f32[16,16]{1,0:T(8,128)S(1)} %convolution_bitcast_fusion.7), channel_id=1, replica_groups=mesh['region'=64,'sub'=4] {'region'}, use_global_device_ids=true, to_apply=%region_9.13 | all-reduce | flops 256 | bytes 2048 | tf_op jit(solution)/shard_map/psum | solution.py:46
  677.5 1.4 cholesky.70
  680.3 1.2 custom-call.23
  682.5 1.3 collective-permute-start.3
  683.8 2.1 collective-permute-done.3
  686.1 86.3 %while.21 = (s32[]{:T(128)}, f32[32,16,512]{2,1,0:T(8,128)S(1)}, s32[]{:T(128)}, s32[2,80]{1,0:T(2,128)S(1)}, bf16[32,16,512]{2,1,0:T(8,128)(2,1)S(1)}, /*index=...) while((s32[]{:T(128)}, f32[32,16,512]{2,1,0:T(8,128)S(1)}, s32[]{:T(128)}, ...), condition=%wide.region_13.0_spmd, body=%wide.region_10.16_spmd.sunk | while | flops 201591008 | bytes 3679233 | solution.py:90
  690.1 7.6 fusion.114
  699.2 7.6 fusion.115
  711.7 7.6 fusion.114
  720.8 7.6 fusion.115
  733.2 7.6 fusion.114
  742.3 7.6 fusion.115
  754.8 7.6 fusion.114
  762.5 0.9 scatter_fusion.2
  763.9 7.6 fusion.115
  771.5 0.9 scatter_fusion.3
  772.5 6.0 collective-permute-start.4
  778.5 1.1 collective-permute-done.4
  779.6 0.9 convert_add_fusion
  781.2 178.0 %all-reduce.10.cloned.1.call-done = f32[16,16,512]{2,1,0:T(8,128)} async-done(((f32[16,16,512]{2,1,0:T(8,128)}), f32[16,16,512]{2,1,0:T(8,128)}) %all-reduce.10.cloned.1.call-update) | async-done | bytes 524304 | tf_op jit(solution)/shard_map/psum | solution.py:92
  959.2 1.8 convolution_bitcast_fusion.5
  961.0 129.7 %psum.47 = f32[16,16]{0,1:T(8,128)S(1)} all-reduce(f32[16,16]{0,1:T(8,128)S(1)} %convolution_bitcast_fusion.5), channel_id=1, replica_groups=mesh['region'=64,'sub'=4] {'region'}, use_global_device_ids=true, to_apply=%region_15.19 | all-reduce | flops 256 | bytes 2048 | tf_op jit(solution)/shard_map/psum | solution.py:46
  1090.9 1.5 cholesky.81
  1093.7 1.2 custom-call.25
  (203 shorter events, 56.9 us)
Async XLA Ops:
  6.5 287.1 %all-reduce.8.cloned.1.call-start = ((), (), s32[]{:S(2)}) async-start(), calls=%async_computation | async-start | bytes 1048576 | tf_op jit(solution)/shard_map/psum | solution.py:92
  7.6 6.2 collective-permute-start
  9.9 3.9 collective-permute-start.1
  13.8 0.7 copy-start
  100.8 7.7 copy-start.1
  100.8 6.7 collective-permute-start.2
  108.5 185.2 %copy-start.3 = (f32[16,512]{1,0:T(8,128)S(1)}, f32[16,512]{1,0:T(8,128)}, u32[]{:S(2)}) copy-start(f32[16,512]{1,0:T(8,128)} %param.15) | copy-start | bytes 98308
  108.5 850.7 %all-reduce.10.cloned.1.call-start = ((), (), s32[]{:S(2)}) async-start(), calls=%async_computation.1 | async-start | bytes 1048576 | tf_op jit(solution)/shard_map/psum | solution.py:92
  293.7 256.3 %copy-start.2 = (f32[16,16,512]{2,1,0:T(8,128)S(1)}, f32[16,16,512]{2,1,0:T(8,128)}, u32[]{:S(2)}) copy-start(f32[16,16,512]{2,1,0:T(8,128)} %all-reduce.8.cloned.1.call-done) | copy-start | bytes 1572868
  682.5 3.4 collective-permute-start.3
  772.5 7.1 collective-permute-start.4
Sparse Core Ops, SparseCore 0:
  108.6 184.9 all-reduce.7
  780.7 178.4 all-reduce.9
where the time goes:
time: 1100 us
  blocking collectives  506 us (46%)
  waiting for transfers between devices  369 us (34%)
  matrix products  131 us (12%)
  other arithmetic  35.7 us (3%)
  local copies, waits for them, and re-layouts  31.4 us (3%)
  starting transfers between devices  15.5 us (1%)
  between operations  14.3 us (1%)
    psum x3, blocking collectives, global_sum(): summed = lax.psum(matrix, 'region')  506 us
    psum x2, waiting for transfers between devices, local(): summed = lax.psum(terms[:blocks] + earlier, 'sub')  362 us
    dot_general x8, matrix products, one_group(): jnp.einsum('grb,gab->gra', extended[rows_right], tiles, preferred_element...  61.1 us
    dot_general x8, matrix products, one_group(): jnp.einsum('gra,gab->grb', extended[rows_left], tiles, preferred_element_...  61 us
  transfers between devices with their start and end apart: 7, of which 6 were waited for; matrix products, arithmetic and copies ran while one was open for 0% of the time, Pallas kernels for 0%

commit v1 on v0

v1 whole, which is shorter than its diff:
```python
import functools
import jax
import jax.numpy as jnp
from jax import lax
from jax.experimental import pallas as pl
from jax.experimental.pallas import tpu as pltpu
from jax.sharding import PartitionSpec as P

OWN = ((0, 0), (0, 1), (1, 0), (1, 1))
BORDER = ((0, 2), (1, 2), (2, 0), (2, 1), (2, 2))
WINDOW = OWN + BORDER
PAIRED = tuple((i, j) for j in range(4) for i in range(j))
CROSS = tuple(
    (i, j)
    for j in range(4, 9)
    for i in range(4)
    if max(abs(OWN[i][0] - WINDOW[j][0]), abs(OWN[i][1] - WINDOW[j][1])) <= 1
)
BLOCK = 512
RHS = 16
FEATURES = 64
f32, bf16 = jnp.float32, jnp.bfloat16
VMEM = pl.BlockSpec(memory_space=pltpu.VMEM)


def lookup(values, step):
    result = jnp.int32(0)
    for start in range(0, len(values), 8):
        code = 0
        for place, value in enumerate(values[start:start + 8]):
            code |= value << (4 * place)
        if code >= 1 << 31:
            code -= 1 << 32
        part = lax.shift_right_logical(jnp.int32(code), 4 * (step - start)) & 15
        result = part if start == 0 else jnp.where(step >= start, part, result)
    return result


def call(kernel, name, out_shape, args, flops, aliases=None):
    return pl.pallas_call(
        kernel,
        name=name,
        out_shape=out_shape,
        in_specs=[VMEM] * len(args),
        out_specs=jax.tree.map(lambda _: VMEM, out_shape),
        input_output_aliases=aliases or {},
        compiler_params=pltpu.CompilerParams(vmem_limit_bytes=16 << 20),
        cost_estimate=pl.CostEstimate(flops=flops, bytes_accessed=1 << 20, transcendentals=0),
    )(*args)


def split(value):
    high = value.astype(bf16).astype(f32)
    rest = value - high
    middle = rest.astype(bf16).astype(f32)
    return high, middle, rest - middle


def feature_rows(place):
    rows = lax.broadcasted_iota(jnp.int32, place.shape, 0)
    parts = split(place)
    norms = split(16.0 * jnp.sum(place * place, axis=0, keepdims=True))
    left, right = [], []
    for group, (a, b) in enumerate(((0, 0), (0, 1), (1, 0), (1, 1), (0, 2), (2, 0), (1, 2), (2, 1))):
        one_left, one_right = -32.0 * parts[a], parts[b]
        if group < 3:
            norm = jnp.broadcast_to(norms[group], place.shape)
            one_left = jnp.where(rows == 3, norm, jnp.where(rows == 4, 1.0, one_left))
            one_right = jnp.where(rows == 4, norm, jnp.where(rows == 3, 1.0, one_right))
        left.append(one_left)
        right.append(one_right)
    return jnp.concatenate(left, axis=0), jnp.concatenate(right, axis=0)


def prepare(points, noise_var, right_sides, sent, left, right, own_sides, own_noise):
    region = lax.axis_index("region")
    member = lax.axis_index("sub")
    row_half, column_half = member & 1, member >> 1
    rows = lax.broadcasted_iota(jnp.int32, (8, BLOCK), 0)
    centers = (
        region.astype(f32) + 0.5,
        row_half.astype(f32) + 1.5,
        column_half.astype(f32) + 1.5,
    )
    for index, (row, column) in enumerate(WINDOW):
        row = jnp.where(row_half == 1, 3 - row, row)
        column = jnp.where(column_half == 1, 3 - column, column)
        block = (row & 1) + 2 * (column & 1) + 4 * (row >> 1) + 8 * (column >> 1)
        place = jnp.zeros((8, BLOCK), f32)
        for axis in range(3):
            line = points[axis, pl.ds(block, 1), :] - centers[axis]
            place = jnp.where(rows == axis, jnp.broadcast_to(line, place.shape), place)
        side = right_sides[block]
        sent[index, 0:16, :] = side.astype(bf16)
        high, middle, low = split(place)
        sent[index, 16:32, :] = jnp.concatenate(
            [high + pltpu.roll(low, 3, 0), middle], axis=0
        ).astype(bf16)
        left_rows, right_rows = feature_rows(place)
        left[index] = jnp.transpose(left_rows).astype(bf16)
        if index < 4:
            right[index] = right_rows.astype(bf16)
            own_sides[index] = side
            own_noise[index] = noise_var[pl.ds(block, 1), :]


def neighbour_left(packed, shift):
    rows = lax.broadcasted_iota(jnp.int32, (8, BLOCK), 0)
    packed = packed.astype(f32)
    top, middle = packed[0:8], packed[8:16]
    place = jnp.where(rows < 3, top + middle + pltpu.roll(top, 5, 0), 0.0)
    place = jnp.where(rows == 0, place + shift, place)
    return jnp.transpose(feature_rows(place)[0]).astype(bf16)


def tile_of(left, right):
    squared = jnp.dot(left, right, preferred_element_type=f32)
    squared = jnp.maximum(squared, 1e-30)
    falloff = jnp.maximum(4.0 - squared * lax.rsqrt(squared), 0.0)
    second = falloff * falloff
    return ((second * second) * (5.0 - falloff)).astype(bf16)


def times(vectors, tile):
    return jnp.dot(vectors, tile, preferred_element_type=f32)


def times_transposed(vectors, tile):
    return lax.dot_general(vectors, tile, (((1,), (1,)), ((), ())), preferred_element_type=f32)


def within_layer(sent, left, right, totals, tiles):
    totals[...] = jnp.zeros_like(totals)

    def one_self(step, carry):
        tile = tile_of(left[step], right[step])
        tiles[step] = tile
        totals[step] += times(sent[step, 0:16, :], tile)
        return carry

    def one_pair(step, carry):
        i = lookup([p[0] for p in PAIRED], step)
        j = lookup([p[1] for p in PAIRED], step)
        tile = tile_of(left[j], right[i])
        tiles[4 + step] = tile
        totals[i] += times(sent[j, 0:16, :], tile)
        totals[j] += times_transposed(sent[i, 0:16, :], tile)
        return carry

    def one_cross(step, carry):
        i = lookup([p[0] for p in CROSS], step)
        j = lookup([p[1] for p in CROSS], step)
        tile = tile_of(left[j], right[i])
        tiles[10 + step] = tile
        totals[i] += times(sent[j, 0:16, :], tile)
        return carry

    lax.fori_loop(0, 4, one_self, 0, unroll=4)
    lax.fori_loop(0, 6, one_pair, 0, unroll=3)
    lax.fori_loop(0, 9, one_cross, 0, unroll=3)


def above_own(sent, right, above, before, totals, passed, tiles):
    totals[...] = before[...]
    passed[...] = jnp.zeros_like(passed)

    def one_block(j, carry):
        left = neighbour_left(above[j, 16:32, :], 1.0)
        for i in range(4):
            tile = tile_of(left, right[i])
            tiles[4 * j + i] = tile
            totals[i] += times(above[j, 0:16, :], tile)
            passed[j] += times_transposed(sent[i, 0:16, :], tile)
        return carry

    lax.fori_loop(0, 4, one_block, 0)


def across(right, above, below, before, totals, tiles, left_above, left_below):
    totals[...] = before[...]
    for j in range(5):
        left_above[j] = neighbour_left(above[4 + j, 16:32, :], 1.0)
        left_below[j] = neighbour_left(below[j, 16:32, :], -1.0)

    def one_above(step, carry):
        i = lookup([p[0] for p in CROSS], step)
        j = lookup([p[1] for p in CROSS], step)
        tile = tile_of(left_above[j - 4], right[i])
        tiles[step] = tile
        totals[i] += times(above[j, 0:16, :], tile)
        tile = tile_of(left_below[j - 4], right[i])
        totals[i] += times(below[j - 4, 0:16, :], tile)
        return carry

    lax.fori_loop(0, 9, one_above, 0, unroll=3)


def finish_image(totals, arrived, own_noise, own_sides, image, rounded):
    value = (totals[...] + arrived[...]) * (1.0 / 256.0) + own_noise[...] * own_sides[...]
    image[...] = value
    rounded[...] = value.astype(bf16)


def gram(first, second):
    return lax.dot_general(
        first, second, (((1,), (1,)), ((), ())),
        precision=lax.Precision.HIGHEST, preferred_element_type=f32,
    )


def inside(own_sides, image, rounded, own_noise, tiles, products, partial):
    total = jnp.zeros((32, 32), f32)
    for i in range(4):
        both = jnp.concatenate([image[i], own_sides[i]], axis=0)
        total += gram(both, both)
    products[...] = total
    partial[...] = own_noise[...] * image[...] * 256.0

    def one_self(step, carry):
        partial[step] += times(rounded[step], tiles[step])
        return carry

    def one_pair(step, carry):
        i = lookup([p[0] for p in PAIRED], step)
        j = lookup([p[1] for p in PAIRED], step)
        partial[i] += 2.0 * times(rounded[j], tiles[4 + step])
        return carry

    lax.fori_loop(0, 4, one_self, 0, unroll=4)
    lax.fori_loop(0, 6, one_pair, 0, unroll=6)


def upward(above, tiles, before, partial):
    partial[...] = before[...]

    def one_block(i, carry):
        total = jnp.zeros((RHS, BLOCK), f32)
        for j in range(4):
            total += times(above[j], tiles[4 * j + i])
        partial[i] += 2.0 * total
        return carry

    lax.fori_loop(0, 4, one_block, 0, unroll=2)


def sideways(from_row, from_column, from_corner, tiles_here, tiles_above, before, image, products, system):
    partial = [before[i] for i in range(4)]
    sources = {4: (from_column, 0), 5: (from_column, 1), 6: (from_row, 0), 7: (from_row, 1), 8: (from_corner, 0)}
    for step, (i, j) in enumerate(CROSS):
        ref, place = sources[j]
        partial[i] += times(ref[0, place], tiles_here[10 + step])
        partial[i] += 2.0 * times(ref[1, place], tiles_above[step])
    third = jnp.zeros((RHS, RHS), f32)
    for i in range(4):
        third += gram(image[i], partial[i])
    known = products[...]
    second, mixed = known[0:16, 0:16], known[0:16, 16:32]
    crossed, start = known[16:32, 0:16], known[16:32, 16:32]
    third = third * (1.0 / 256.0)
    top = jnp.concatenate([crossed, second, start, jnp.zeros((RHS, 80), f32)], axis=1)
    bottom = jnp.concatenate([second, third, mixed, jnp.zeros((RHS, 80), f32)], axis=1)
    system[...] = jnp.concatenate([top, bottom], axis=0)


def conclude(system, own_sides, image, result):
    value = system[...]
    lanes = lax.broadcasted_iota(jnp.int32, (32, 128), 1)
    rows = lax.broadcasted_iota(jnp.int32, (32, 128), 0)
    flipped = jnp.transpose(jnp.concatenate([value, jnp.zeros((96, 128), f32)], axis=0))[0:32]
    value = jnp.where(lanes < 32, 0.5 * (value + flipped), value)
    for k in range(32):
        pivot = value[k:k + 1, :]
        scaled = pivot * (1.0 / pivot[:, k:k + 1])
        value = jnp.where(rows == k, scaled, value - value[:, k:k + 1] * scaled)
    weights = jnp.transpose(jnp.concatenate([value, jnp.zeros((96, 128), f32)], axis=0))[32:48, 0:32]
    member = lax.axis_index("sub")
    for i, (row, column) in enumerate(OWN):
        both = jnp.concatenate([own_sides[i], image[i]], axis=0)
        place = (row ^ (member & 1)) + 2 * (column ^ (member >> 1))
        result[place] = jnp.dot(
            weights, both, precision=lax.Precision.HIGHEST, preferred_element_type=f32
        )


def local(regions, members, points, noise_var, right_sides, pair_list, pair_count):
    everyone = regions * members

    def from_region(value, step):
        pairs = [
            (source, source - step)
            for source in range(regions)
            if 0 <= source - step < regions
        ]
        return lax.ppermute(value, "region", pairs)

    def from_member(value, mask):
        return lax.ppermute(value, "sub", [(source, source ^ mask) for source in range(members)])

    def sum_over_all(value):
        low = 1
        while low < everyone:
            value = value + sum(
                lax.ppermute(
                    value,
                    ("region", "sub"),
                    [(source, source ^ (low * mask)) for source in range(everyone)],
                )
                for mask in (1, 2, 3)
            )
            low *= 4
        return value

    def shape(*dims, dtype=f32):
        return jax.ShapeDtypeStruct(dims, dtype)

    def held(*dims, dtype=bf16):
        return pltpu.VMEM(dims, dtype)

    tile_flops = 2 * BLOCK * BLOCK * 256
    field = (4, RHS, BLOCK)
    sent, left, right, own_sides, own_noise = call(
        prepare, "prepare",
        (shape(9, 32, BLOCK, dtype=bf16), shape(9, BLOCK, FEATURES, dtype=bf16),
         shape(4, FEATURES, BLOCK, dtype=bf16), shape(*field), shape(4, 1, BLOCK)),
        (points, noise_var, right_sides), tile_flops,
    )
    above = from_region(sent, 1)
    below = from_region(sent[4:9], -1)
    totals, tiles_here = call(
        within_layer, "within_layer", (shape(*field), held(19, BLOCK, BLOCK)),
        (sent, left, right), 19 * 4 * tile_flops,
    )
    totals, passed, tiles_up = call(
        above_own, "above_own", (shape(*field), shape(*field), held(16, BLOCK, BLOCK)),
        (sent, right, above, totals), 16 * 4 * tile_flops,
    )
    arrived = from_region(passed, -1)
    totals, tiles_side = pl.pallas_call(
        across, name="across",
        out_shape=(shape(*field), held(9, BLOCK, BLOCK)),
        in_specs=[VMEM] * 4, out_specs=(VMEM, VMEM),
        scratch_shapes=[pltpu.VMEM((5, BLOCK, FEATURES), bf16)] * 2,
        compiler_params=pltpu.CompilerParams(vmem_limit_bytes=16 << 20),
        cost_estimate=pl.CostEstimate(flops=18 * 4 * tile_flops, bytes_accessed=1 << 20, transcendentals=0),
    )(right, above, below, totals)
    image, rounded = call(
        finish_image, "finish_image", (shape(*field), shape(*field, dtype=bf16)),
        (totals, arrived, own_noise, own_sides), tile_flops // 8,
    )
    upper = from_region(rounded, 1)
    products, partial = call(
        inside, "inside", (shape(32, 32), shape(*field)),
        (own_sides, image, rounded, own_noise, tiles_here), 10 * 2 * tile_flops,
    )
    layers = jnp.stack([rounded, upper])
    from_row = from_member(layers[:, 2:4], 1)
    from_column = from_member(layers[:, 1::2], 2)
    from_corner = from_member(layers[:, 3:4], 3)
    partial = call(
        upward, "upward", shape(*field), (upper, tiles_up, partial), 16 * 2 * tile_flops,
    )
    system = call(
        sideways, "sideways", shape(32, 128),
        (from_row, from_column, from_corner, tiles_here, tiles_side, partial, image, products),
        18 * 2 * tile_flops,
    )
    system = sum_over_all(system)
    return call(
        conclude, "conclude", shape(*field), (system, own_sides, image), tile_flops,
    )


def solution(mesh):
    return jax.shard_map(
        functools.partial(local, mesh.shape["region"], mesh.shape["sub"]),
        mesh=mesh,
        in_specs=(
            P(None, "region", None),
            P("region", None),
            P("region", None, None),
            P("region", "sub", None, None),
            P("region", "sub"),
        ),
        out_specs=P(("region", "sub"), None, None),
        check_vma=False,
    )
```

time: 1100 us -> 100 us (0.09)
  blocking collectives: 506 us -> 0 us
  waiting for transfers between devices: 369 us -> 18.7 us
  matrix products: 131 us -> 0 us
  Pallas kernels: 0 us -> 40.5 us
  other arithmetic: 35.7 us -> 0.06 us
  local copies, waits for them, and re-layouts: 31.4 us -> 2.71 us
  starting transfers between devices: 15.5 us -> 36.7 us
  between operations: 14.3 us -> 0.11 us
    psum x3 -> x0, blocking collectives: 506 us -> none  [global_sum(): summed = lax.psum(matrix, 'region')]
    psum x2 -> x0, waiting for transfers between devices: 362 us -> none  [local(): summed = lax.psum(terms[:blocks] + earlier, 'sub')]
    dot_general x24 -> x0, matrix products: 130 us -> none  [the longest x8 61.1 us: one_group(): jnp.einsum('grb,gab->gra', extended[rows_right], tiles, preferred_element...]
    pallas_call x0 -> x9, Pallas kernels: none -> 40.5 us  [the longest x8 30.8 us: call(): pl.pallas_call(kernel, name=name, out_shape=out_shape, in_specs=[VMEM] *...]
    gather x48 -> x0, local copies, waits for them, and re-layouts: 28.7 us -> none  [the longest x16 9.41 us: one_group(): tiles = kernel_tile(all_points[rows_left], all_points[rows_right])]
    ppermute x5 -> x19, starting transfers between devices: 15.5 us -> 36.7 us  [the longest x12 24.3 us: sum_over_all(): lax.ppermute(value, ('region', 'sub'), [(source, source ^ low * mask) for...]
    scatter-add x16 -> x0, other arithmetic: 14.3 us -> none  [the longest x8 7.16 us: one_group(): return totals.at[rows_right].add(to_right * weight_right)]
    ppermute x5 -> x19, waiting for transfers between devices: 6.29 us -> 18.7 us  [the longest x12 13.5 us: sum_over_all(): lax.ppermute(value, ('region', 'sub'), [(source, source ^ low * mask) for...]
  transfers between devices with their start and end apart: 7 -> 19, of which waited for: 6 -> 11; matrix products, arithmetic and copies ran while one was open for 0% -> 0% of each run, Pallas kernels for 0% -> 35%
where the time goes in v1:
time: 100 us; the launch traced here: 98.7 us
  Pallas kernels  40.5 us (40%)
  starting transfers between devices  36.7 us (37%)
  waiting for transfers between devices  18.7 us (19%)
  local copies, waits for them, and re-layouts  2.71 us (3%)
    pallas_call x8, Pallas kernels, call(): pl.pallas_call(kernel, name=name, out_shape=out_shape, in_specs=[VMEM] *...  30.8 us
    ppermute x12, starting transfers between devices, sum_over_all(): lax.ppermute(value, ('region', 'sub'), [(source, source ^ low * mask) for...  24.3 us
    ppermute x12, waiting for transfers between devices, sum_over_all(): lax.ppermute(value, ('region', 'sub'), [(source, source ^ low * mask) for...  13.5 us
    pallas_call x1, Pallas kernels, local(): pl.pallas_call(across, name='across', out_shape=(shape(*field), held(9, B...  9.7 us
    ppermute x4, starting transfers between devices, from_region(): return lax.ppermute(value, 'region', pairs)  8.83 us
    ppermute x3, waiting for transfers between devices, from_member(): lax.ppermute(value, 'sub', [(source, source ^ mask) for source in range(m...  4.44 us
    ppermute x3, starting transfers between devices, from_member(): lax.ppermute(value, 'sub', [(source, source ^ mask) for source in range(m...  3.57 us
    unnamed x6, local copies, waits for them, and re-layouts  2.69 us
  transfers between devices with their start and end apart: 19, of which 11 were waited for; matrix products, arithmetic and copies ran while one was open for 0% of the time, Pallas kernels for 35%

profile of v1, /device:TPU:8, one launch (start us, length us, event | category | flops | bytes accessed | tf_op | source)
XLA Modules:
  0.0 98.7 jit_solution(36142597934376996)
XLA Ops:
  0.0 1.0 %copy-done = f32[16,16,512]{2,1,0:T(8,128)S(1)} copy-done((f32[16,16,512]{2,1,0:T(8,128)S(1)}, f32[16,16,512]{2,1,0:T(8,128)}, u32[]{:S(2)}) %copy-start) | copy-done | bytes 524312
  1.0 0.9 copy-done.1
  1.9 0.8 copy-done.2
  2.7 0.4 prepare.1
  3.1 1.3 %collective-permute-start = (bf16[9,32,512]{2,1,0:T(8,128)(2,1)S(1)}, bf16[9,32,512]{2,1,0:T(8,128)(2,1)S(1)}, u32[]{:S(2)}, u32[]{:S(2)}) collective-permute-start(bf16[9,32,512]{2,1,0:T(8,128)(2,1)S(1)} %get-tuple-element.22.sent), channel_id=1, source_target_pairs={{4,0},{8,4},{12,8},{16,12},{20,16},{24,20},{28,24},{32,28},{36,32}... | collective-permute-start | bytes 884744 | tf_op jit(solution)/shard_map/ppermute | solution.py:294
  4.5 3.0 %collective-permute-start.1 = (bf16[5,32,512]{2,1,0:T(8,128)(2,1)S(1)}, bf16[5,32,512]{2,1,0:T(8,128)(2,1)S(1)}, u32[]{:S(2)}, u32[]{:S(2)}) collective-permute-start(bf16[5,32,512]{2,1,0:T(8,128)(2,1)S(1)} %slice.12), channel_id=1, source_target_pairs={{0,4},{4,8},{8,12},{12,16},{16,20},{20,24},{24,28},{28,32},{32,36}... | collective-permute-start | bytes 491528 | tf_op jit(solution)/shard_map/ppermute | solution.py:294
  7.5 11.2 %within_layer.1 = (f32[4,16,512]{2,1,0:T(8,128)S(1)}, bf16[19,512,512]{2,1,0:T(8,128)(2,1)S(1)}) custom-call(bf16[9,32,512]{2,1,0:T(8,128)(2,1)S(1)} %get-tuple-element.22.sent, bf16[9,512,64]{2,1,0:T(8,128)(2,1)S(1)} %get-tuple-element.23.left, bf16[4,64,512]{2,1,0:T(8,128)(2,1)S(1)} %get-tuple-element.21.right), custom_call_target="tpu_custom_call" | custom-call | flops 10200547328 | bytes 1048576 | tf_op jit(solution)/shard_map/within_layer/pallas_call | solution.py:40
  18.8 0.0 collective-permute-done.above
  18.8 11.3 %above_own.1 = (f32[4,16,512]{2,1,0:T(8,128)S(1)}, f32[4,16,512]{2,1,0:T(8,128)S(1)}, bf16[16,512,512]{2,1,0:T(8,128)(2,1)S(1)}) custom-call(bf16[9,32,512]{2,1,0:T(8,128)(2,1)S(1)} %get-tuple-element.22.sent, bf16[4,64,512]{2,1,0:T(8,128)(2,1)S(1)} %get-tuple-element.21.right, bf16[9,32,512]{2,1,0:T(8,128)(2,1)S(1)} %collective-permute-done.above, ...), custom_call_target="tpu_custom_call" | custom-call | flops 8589934592 | bytes 1048576 | tf_op jit(solution)/shard_map/above_own/pallas_call | solution.py:40
  30.1 3.0 %collective-permute-start.2 = (f32[4,16,512]{2,1,0:T(8,128)S(1)}, f32[4,16,512]{2,1,0:T(8,128)S(1)}, u32[]{:S(2)}, u32[]{:S(2)}) collective-permute-start(f32[4,16,512]{2,1,0:T(8,128)S(1)} %get-tuple-element.27), channel_id=1, source_target_pairs={{0,4},{4,8},{8,12},{12,16},{16,20},{20,24},{24,28},{28,32},{32,36}... | collective-permute-start | bytes 393224 | tf_op jit(solution)/shard_map/ppermute | solution.py:294
  33.1 0.0 collective-permute-done.1.below
  33.1 9.7 %across.1 = (f32[4,16,512]{2,1,0:T(8,128)S(1)}, bf16[9,512,512]{2,1,0:T(8,128)(2,1)S(1)}) custom-call(bf16[4,64,512]{2,1,0:T(8,128)(2,1)S(1)} %get-tuple-element.21.right, bf16[9,32,512]{2,1,0:T(8,128)(2,1)S(1)} %collective-permute-done.above, bf16[5,32,512]{2,1,0:T(8,128)(2,1)S(1)} %collective-permute-done.1.below, f32[4,16,512]{2,1,0:T(8,128)S(1)} %get-tuple-element.25.before), custom_call_target="tpu_custom_call" | custom-call | flops 9663676416 | bytes 1048576 | tf_op jit(solution)/shard_map/across/pallas_call | solution.py:338
  42.8 0.0 collective-permute-done.2.arrived
  42.8 1.5 %collective-permute-start.3 = (bf16[4,16,512]{2,1,0:T(8,128)(2,1)S(1)}, bf16[4,16,512]{2,1,0:T(8,128)(2,1)S(1)}, u32[]{:S(2)}, u32[]{:S(2)}) collective-permute-start(bf16[4,16,512]{2,1,0:T(8,128)(2,1)S(1)} %get-tuple-element.30.rounded), channel_id=1, source_target_pairs={{4,0},{8,4},{12,8},{16,12},{20,16},{24,20},{28,24},{32,28},{36,32}... | collective-permute-start | bytes 196616 | tf_op jit(solution)/shard_map/ppermute | solution.py:294
  44.3 1.0 %inside.1 = (f32[32,32]{1,0:T(8,128)S(1)}, f32[4,16,512]{2,1,0:T(8,128)S(1)}) custom-call(f32[4,16,512]{2,1,0:T(8,128)S(1)} %get-tuple-element.29.own_sides, f32[4,16,512]{2,1,0:T(8,128)S(1)} %get-tuple-element.34.image, bf16[4,16,512]{2,1,0:T(8,128)(2,1)S(1)} %get-tuple-element.30.rounded, f32[4,1,512]{2,1,0:T(1,128)S(1)} %get-tuple-element.28.own_noise, ...), custom_call_target="tpu_custom_call" | custom-call | flops 2684354560 | bytes 1048576 | tf_op jit(solution)/shard_map/inside/pallas_call | solution.py:40
  45.3 0.7 collective-permute-done.3.above
  46.0 1.7 %collective-permute-start.6 = (bf16[2,1,16,512]{3,2,1,0:T(8,128)(2,1)S(1)}, bf16[2,1,16,512]{3,2,1,0:T(8,128)(2,1)S(1)}, u32[]{:S(2)}, u32[]{:S(2)}) collective-permute-start(bf16[2,1,16,512]{3,2,1,0:T(8,128)(2,1)S(1)} %fusion.1), channel_id=1, source_target_pairs={{0,3},{1,2},{2,1},{3,0},{4,7},{5,6},{6,5},{7,4},{8,11},{9,10},{10,... | collective-permute-start | bytes 98312 | tf_op jit(solution)/shard_map/ppermute | solution.py:297
  47.7 1.9 %collective-permute-start.4 = (bf16[2,2,16,512]{3,2,1,0:T(8,128)(2,1)S(1)}, bf16[2,2,16,512]{3,2,1,0:T(8,128)(2,1)S(1)}, u32[]{:S(2)}, u32[]{:S(2)}) collective-permute-start(bf16[2,2,16,512]{3,2,1,0:T(8,128)(2,1)S(1)} %fusion), channel_id=1, source_target_pairs={{0,1},{1,0},{2,3},{3,2},{4,5},{5,4},{6,7},{7,6},{8,9},{9,8},{10,11... | collective-permute-start | bytes 196616 | tf_op jit(solution)/shard_map/ppermute | solution.py:297
  49.6 0.0 collective-permute-start.5
  49.6 1.3 %upward.1.before = f32[4,16,512]{2,1,0:T(8,128)S(1)} custom-call(bf16[4,16,512]{2,1,0:T(8,128)(2,1)S(1)} %collective-permute-done.3.above, bf16[16,512,512]{2,1,0:T(8,128)(2,1)S(1)} %get-tuple-element.33.tiles, f32[4,16,512]{2,1,0:T(8,128)S(1)} %get-tuple-element.35.before), custom_call_target="tpu_custom_call" | custom-call | flops 4294967296 | bytes 1048576 | tf_op jit(solution)/shard_map/upward/pallas_call | solution.py:40
  50.9 0.0 collective-permute-done.6.from_corner
  50.9 1.0 %collective-permute-done.4.from_row = bf16[2,2,16,512]{3,2,1,0:T(8,128)(2,1)S(1)} collective-permute-done((bf16[2,2,16,512]{3,2,1,0:T(8,128)(2,1)S(1)}, bf16[2,2,16,512]{3,2,1,0:T(8,128)(2,1)S(1)}, u32[]{:S(2)}, u32[]{:S(2)}) %collective-permute-start.4) | collective-permute-done | bytes 65568 | tf_op jit(solution)/shard_map/ppermute | solution.py:297
  52.0 3.4 %collective-permute-done.5.from_column = bf16[2,2,16,512]{3,2,1,0:T(8,128)(2,1)S(1)} collective-permute-done((bf16[2,2,16,512]{3,2,1,0:T(8,128)(2,1)S(1)}, bf16[2,2,16,512]{3,2,1,0:T(8,128)(2,1)S(1)}, u32[]{:S(2)}, u32[]{:S(2)}) %collective-permute-start.5) | collective-permute-done | bytes 65568 | tf_op jit(solution)/shard_map/ppermute | solution.py:297
  55.4 1.7 %sideways.1 = f32[32,128]{1,0:T(8,128)S(1)} custom-call(bf16[2,2,16,512]{3,2,1,0:T(8,128)(2,1)S(1)} %collective-permute-done.4.from_row, bf16[2,2,16,512]{3,2,1,0:T(8,128)(2,1)S(1)} %collective-permute-done.5.from_column, bf16[2,1,16,512]{3,2,1,0:T(8,128)(2,1)S(1)} %collective-permute-done.6.from_corner, ...), custom_call_target="tpu_custom_call" | custom-call | flops 4831838208 | bytes 1048576 | tf_op jit(solution)/shard_map/sideways/pallas_call | solution.py:40
  57.1 0.8 collective-permute-start.9
  57.9 2.0 %collective-permute-start.8 = (f32[32,128]{1,0:T(8,128)S(1)}, f32[32,128]{1,0:T(8,128)S(1)}, u32[]{:S(2)}, u32[]{:S(2)}) collective-permute-start(f32[32,128]{1,0:T(8,128)S(1)} %sideways.1), channel_id=1, source_target_pairs={{0,2},{1,3},{2,0},{3,1},{4,6},{5,7},{6,4},{7,5},{8,10},{9,11},{10,... | collective-permute-start | bytes 49160 | tf_op jit(solution)/shard_map/ppermute | solution.py:303
  59.9 1.3 %collective-permute-start.7 = (f32[32,128]{1,0:T(8,128)S(1)}, f32[32,128]{1,0:T(8,128)S(1)}, u32[]{:S(2)}, u32[]{:S(2)}) collective-permute-start(f32[32,128]{1,0:T(8,128)S(1)} %sideways.1), channel_id=1, source_target_pairs={{0,1},{1,0},{2,3},{3,2},{4,5},{5,4},{6,7},{7,6},{8,9},{9,8},{10,11... | collective-permute-start | bytes 49160 | tf_op jit(solution)/shard_map/ppermute | solution.py:303
  61.2 0.0 collective-permute-done.9
  61.2 1.9 %collective-permute-done.8 = f32[32,128]{1,0:T(8,128)S(1)} collective-permute-done((f32[32,128]{1,0:T(8,128)S(1)}, f32[32,128]{1,0:T(8,128)S(1)}, u32[]{:S(2)}, u32[]{:S(2)}) %collective-permute-start.8) | collective-permute-done | bytes 16416 | tf_op jit(solution)/shard_map/ppermute | solution.py:303
  63.1 0.5 collective-permute-done.7
  63.7 1.1 %collective-permute-start.12 = (f32[32,128]{1,0:T(8,128)S(1)}, f32[32,128]{1,0:T(8,128)S(1)}, u32[]{:S(2)}, u32[]{:S(2)}) collective-permute-start(f32[32,128]{1,0:T(8,128)S(1)} %add_add_fusion.3), channel_id=1, source_target_pairs={{0,12},{1,13},{2,14},{3,15},{4,8},{5,9},{6,10},{7,11},{8,4},{9,5},... | collective-permute-start | bytes 49160 | tf_op jit(solution)/shard_map/ppermute | solution.py:303
  64.8 1.8 %collective-permute-start.11 = (f32[32,128]{1,0:T(8,128)S(1)}, f32[32,128]{1,0:T(8,128)S(1)}, u32[]{:S(2)}, u32[]{:S(2)}) collective-permute-start(f32[32,128]{1,0:T(8,128)S(1)} %add_add_fusion.3), channel_id=1, source_target_pairs={{0,8},{1,9},{2,10},{3,11},{4,12},{5,13},{6,14},{7,15},{8,0},{9,1},... | collective-permute-start | bytes 49160 | tf_op jit(solution)/shard_map/ppermute | solution.py:303
  66.6 0.0 collective-permute-start.10
  66.6 0.2 collective-permute-done.12
  66.8 1.7 %collective-permute-done.11 = f32[32,128]{1,0:T(8,128)S(1)} collective-permute-done((f32[32,128]{1,0:T(8,128)S(1)}, f32[32,128]{1,0:T(8,128)S(1)}, u32[]{:S(2)}, u32[]{:S(2)}) %collective-permute-start.11) | collective-permute-done | bytes 16416 | tf_op jit(solution)/shard_map/ppermute | solution.py:303
  68.5 0.0 collective-permute-done.10
  68.5 7.1 %collective-permute-start.15 = (f32[32,128]{1,0:T(8,128)S(1)}, f32[32,128]{1,0:T(8,128)S(1)}, u32[]{:S(2)}, u32[]{:S(2)}) collective-permute-start(f32[32,128]{1,0:T(8,128)S(1)} %add_add_fusion.2), channel_id=1, source_target_pairs={{0,48},{1,49},{2,50},{3,51},{4,52},{5,53},{6,54},{7,55},{8,56},{9,... | collective-permute-start | bytes 49160 | tf_op jit(solution)/shard_map/ppermute | solution.py:303
  75.7 0.1 collective-permute-start.14
  75.8 0.8 collective-permute-start.13
  76.6 0.8 collective-permute-done.15
  77.4 2.0 %collective-permute-done.14 = f32[32,128]{1,0:T(8,128)S(1)} collective-permute-done((f32[32,128]{1,0:T(8,128)S(1)}, f32[32,128]{1,0:T(8,128)S(1)}, u32[]{:S(2)}, u32[]{:S(2)}) %collective-permute-start.14) | collective-permute-done | bytes 16416 | tf_op jit(solution)/shard_map/ppermute | solution.py:303
  79.4 1.6 %collective-permute-done.13 = f32[32,128]{1,0:T(8,128)S(1)} collective-permute-done((f32[32,128]{1,0:T(8,128)S(1)}, f32[32,128]{1,0:T(8,128)S(1)}, u32[]{:S(2)}, u32[]{:S(2)}) %collective-permute-start.13) | collective-permute-done | bytes 16416 | tf_op jit(solution)/shard_map/ppermute | solution.py:303
  81.0 6.3 %collective-permute-start.18 = (f32[32,128]{1,0:T(8,128)S(1)}, f32[32,128]{1,0:T(8,128)S(1)}, u32[]{:S(2)}, u32[]{:S(2)}) collective-permute-start(f32[32,128]{1,0:T(8,128)S(1)} %add_add_fusion.1), channel_id=1, source_target_pairs={{0,192},{1,193},{2,194},{3,195},{4,196},{5,197},{6,198},{7,199},{8... | collective-permute-start | bytes 49160 | tf_op jit(solution)/shard_map/ppermute | solution.py:303
  87.3 2.8 %collective-permute-start.17 = (f32[32,128]{1,0:T(8,128)S(1)}, f32[32,128]{1,0:T(8,128)S(1)}, u32[]{:S(2)}, u32[]{:S(2)}) collective-permute-start(f32[32,128]{1,0:T(8,128)S(1)} %add_add_fusion.1), channel_id=1, source_target_pairs={{0,128},{1,129},{2,130},{3,131},{4,132},{5,133},{6,134},{7,135},{8... | collective-permute-start | bytes 49160 | tf_op jit(solution)/shard_map/ppermute | solution.py:303
  90.2 0.0 collective-permute-start.16
  90.2 4.8 %collective-permute-done.17 = f32[32,128]{1,0:T(8,128)S(1)} collective-permute-done((f32[32,128]{1,0:T(8,128)S(1)}, f32[32,128]{1,0:T(8,128)S(1)}, u32[]{:S(2)}, u32[]{:S(2)}) %collective-permute-start.17) | collective-permute-done | bytes 16416 | tf_op jit(solution)/shard_map/ppermute | solution.py:303
  95.0 0.0 collective-permute-done.16
  95.0 3.7 %conclude.1 = f32[4,16,512]{2,1,0:T(8,128)} custom-call(f32[32,128]{1,0:T(8,128)S(1)} %add_add_fusion.system, f32[4,16,512]{2,1,0:T(8,128)S(1)} %get-tuple-element.29.own_sides, f32[4,16,512]{2,1,0:T(8,128)S(1)} %get-tuple-element.34.image), custom_call_target="tpu_custom_call" | custom-call | flops 134217728 | bytes 1048576 | tf_op jit(solution)/shard_map/conclude/pallas_call | solution.py:40
  (14 shorter events, 0.1 us)
Async XLA Ops:
  0.0 1.0 %copy-start = (f32[16,16,512]{2,1,0:T(8,128)S(1)}, f32[16,16,512]{2,1,0:T(8,128)}, u32[]{:S(2)}) copy-start(f32[16,16,512]{2,1,0:T(8,128)} %right_sides.1) | copy-start | bytes 1572868
  1.0 0.9 copy-start.1
  1.9 0.8 copy-start.2
  3.1 15.6 %collective-permute-start = (bf16[9,32,512]{2,1,0:T(8,128)(2,1)S(1)}, bf16[9,32,512]{2,1,0:T(8,128)(2,1)S(1)}, u32[]{:S(2)}, u32[]{:S(2)}) collective-permute-start(bf16[9,32,512]{2,1,0:T(8,128)(2,1)S(1)} %get-tuple-element.22.sent), channel_id=1, source_target_pairs={{4,0},{8,4},{12,8},{16,12},{20,16},{24,20},{28,24},{32,28},{36,32}... | collective-permute-start | bytes 884744 | tf_op jit(solution)/shard_map/ppermute | solution.py:294
  4.5 28.6 %collective-permute-start.1 = (bf16[5,32,512]{2,1,0:T(8,128)(2,1)S(1)}, bf16[5,32,512]{2,1,0:T(8,128)(2,1)S(1)}, u32[]{:S(2)}, u32[]{:S(2)}) collective-permute-start(bf16[5,32,512]{2,1,0:T(8,128)(2,1)S(1)} %slice.12), channel_id=1, source_target_pairs={{0,4},{4,8},{8,12},{12,16},{16,20},{20,24},{24,28},{28,32},{32,36}... | collective-permute-start | bytes 491528 | tf_op jit(solution)/shard_map/ppermute | solution.py:294
  30.1 12.7 %collective-permute-start.2 = (f32[4,16,512]{2,1,0:T(8,128)S(1)}, f32[4,16,512]{2,1,0:T(8,128)S(1)}, u32[]{:S(2)}, u32[]{:S(2)}) collective-permute-start(f32[4,16,512]{2,1,0:T(8,128)S(1)} %get-tuple-element.27), channel_id=1, source_target_pairs={{0,4},{4,8},{8,12},{12,16},{16,20},{20,24},{24,28},{28,32},{32,36}... | collective-permute-start | bytes 393224 | tf_op jit(solution)/shard_map/ppermute | solution.py:294
  42.8 3.1 %collective-permute-start.3 = (bf16[4,16,512]{2,1,0:T(8,128)(2,1)S(1)}, bf16[4,16,512]{2,1,0:T(8,128)(2,1)S(1)}, u32[]{:S(2)}, u32[]{:S(2)}) collective-permute-start(bf16[4,16,512]{2,1,0:T(8,128)(2,1)S(1)} %get-tuple-element.30.rounded), channel_id=1, source_target_pairs={{4,0},{8,4},{12,8},{16,12},{20,16},{24,20},{28,24},{32,28},{36,32}... | collective-permute-start | bytes 196616 | tf_op jit(solution)/shard_map/ppermute | solution.py:294
  46.0 4.9 %collective-permute-start.6 = (bf16[2,1,16,512]{3,2,1,0:T(8,128)(2,1)S(1)}, bf16[2,1,16,512]{3,2,1,0:T(8,128)(2,1)S(1)}, u32[]{:S(2)}, u32[]{:S(2)}) collective-permute-start(bf16[2,1,16,512]{3,2,1,0:T(8,128)(2,1)S(1)} %fusion.1), channel_id=1, source_target_pairs={{0,3},{1,2},{2,1},{3,0},{4,7},{5,6},{6,5},{7,4},{8,11},{9,10},{10,... | collective-permute-start | bytes 98312 | tf_op jit(solution)/shard_map/ppermute | solution.py:297
  47.7 4.3 %collective-permute-start.4 = (bf16[2,2,16,512]{3,2,1,0:T(8,128)(2,1)S(1)}, bf16[2,2,16,512]{3,2,1,0:T(8,128)(2,1)S(1)}, u32[]{:S(2)}, u32[]{:S(2)}) collective-permute-start(bf16[2,2,16,512]{3,2,1,0:T(8,128)(2,1)S(1)} %fusion), channel_id=1, source_target_pairs={{0,1},{1,0},{2,3},{3,2},{4,5},{5,4},{6,7},{7,6},{8,9},{9,8},{10,11... | collective-permute-start | bytes 196616 | tf_op jit(solution)/shard_map/ppermute | solution.py:297
  49.6 5.8 %collective-permute-start.5 = (bf16[2,2,16,512]{3,2,1,0:T(8,128)(2,1)S(1)}, bf16[2,2,16,512]{3,2,1,0:T(8,128)(2,1)S(1)}, u32[]{:S(2)}, u32[]{:S(2)}) collective-permute-start(bf16[2,2,16,512]{3,2,1,0:T(8,128)(2,1)S(1)} %slice.14), channel_id=1, source_target_pairs={{0,2},{1,3},{2,0},{3,1},{4,6},{5,7},{6,4},{7,5},{8,10},{9,11},{10,... | collective-permute-start | bytes 196616 | tf_op jit(solution)/shard_map/ppermute | solution.py:297
  57.1 4.1 %collective-permute-start.9 = (f32[32,128]{1,0:T(8,128)S(1)}, f32[32,128]{1,0:T(8,128)S(1)}, u32[]{:S(2)}, u32[]{:S(2)}) collective-permute-start(f32[32,128]{1,0:T(8,128)S(1)} %sideways.1), channel_id=1, source_target_pairs={{0,3},{1,2},{2,1},{3,0},{4,7},{5,6},{6,5},{7,4},{8,11},{9,10},{10,... | collective-permute-start | bytes 49160 | tf_op jit(solution)/shard_map/ppermute | solution.py:303
  57.9 5.2 %collective-permute-start.8 = (f32[32,128]{1,0:T(8,128)S(1)}, f32[32,128]{1,0:T(8,128)S(1)}, u32[]{:S(2)}, u32[]{:S(2)}) collective-permute-start(f32[32,128]{1,0:T(8,128)S(1)} %sideways.1), channel_id=1, source_target_pairs={{0,2},{1,3},{2,0},{3,1},{4,6},{5,7},{6,4},{7,5},{8,10},{9,11},{10,... | collective-permute-start | bytes 49160 | tf_op jit(solution)/shard_map/ppermute | solution.py:303
  59.9 3.7 %collective-permute-start.7 = (f32[32,128]{1,0:T(8,128)S(1)}, f32[32,128]{1,0:T(8,128)S(1)}, u32[]{:S(2)}, u32[]{:S(2)}) collective-permute-start(f32[32,128]{1,0:T(8,128)S(1)} %sideways.1), channel_id=1, source_target_pairs={{0,1},{1,0},{2,3},{3,2},{4,5},{5,4},{6,7},{7,6},{8,9},{9,8},{10,11... | collective-permute-start | bytes 49160 | tf_op jit(solution)/shard_map/ppermute | solution.py:303
  63.7 3.2 %collective-permute-start.12 = (f32[32,128]{1,0:T(8,128)S(1)}, f32[32,128]{1,0:T(8,128)S(1)}, u32[]{:S(2)}, u32[]{:S(2)}) collective-permute-start(f32[32,128]{1,0:T(8,128)S(1)} %add_add_fusion.3), channel_id=1, source_target_pairs={{0,12},{1,13},{2,14},{3,15},{4,8},{5,9},{6,10},{7,11},{8,4},{9,5},... | collective-permute-start | bytes 49160 | tf_op jit(solution)/shard_map/ppermute | solution.py:303
  64.8 3.7 %collective-permute-start.11 = (f32[32,128]{1,0:T(8,128)S(1)}, f32[32,128]{1,0:T(8,128)S(1)}, u32[]{:S(2)}, u32[]{:S(2)}) collective-permute-start(f32[32,128]{1,0:T(8,128)S(1)} %add_add_fusion.3), channel_id=1, source_target_pairs={{0,8},{1,9},{2,10},{3,11},{4,12},{5,13},{6,14},{7,15},{8,0},{9,1},... | collective-permute-start | bytes 49160 | tf_op jit(solution)/shard_map/ppermute | solution.py:303
  66.6 1.9 %collective-permute-start.10 = (f32[32,128]{1,0:T(8,128)S(1)}, f32[32,128]{1,0:T(8,128)S(1)}, u32[]{:S(2)}, u32[]{:S(2)}) collective-permute-start(f32[32,128]{1,0:T(8,128)S(1)} %add_add_fusion.3), channel_id=1, source_target_pairs={{0,4},{1,5},{2,6},{3,7},{4,0},{5,1},{6,2},{7,3},{8,12},{9,13},{10,... | collective-permute-start | bytes 49160 | tf_op jit(solution)/shard_map/ppermute | solution.py:303
  68.5 8.9 %collective-permute-start.15 = (f32[32,128]{1,0:T(8,128)S(1)}, f32[32,128]{1,0:T(8,128)S(1)}, u32[]{:S(2)}, u32[]{:S(2)}) collective-permute-start(f32[32,128]{1,0:T(8,128)S(1)} %add_add_fusion.2), channel_id=1, source_target_pairs={{0,48},{1,49},{2,50},{3,51},{4,52},{5,53},{6,54},{7,55},{8,56},{9,... | collective-permute-start | bytes 49160 | tf_op jit(solution)/shard_map/ppermute | solution.py:303
  75.7 3.7 %collective-permute-start.14 = (f32[32,128]{1,0:T(8,128)S(1)}, f32[32,128]{1,0:T(8,128)S(1)}, u32[]{:S(2)}, u32[]{:S(2)}) collective-permute-start(f32[32,128]{1,0:T(8,128)S(1)} %add_add_fusion.2), channel_id=1, source_target_pairs={{0,32},{1,33},{2,34},{3,35},{4,36},{5,37},{6,38},{7,39},{8,40},{9,... | collective-permute-start | bytes 49160 | tf_op jit(solution)/shard_map/ppermute | solution.py:303
  75.8 5.2 %collective-permute-start.13 = (f32[32,128]{1,0:T(8,128)S(1)}, f32[32,128]{1,0:T(8,128)S(1)}, u32[]{:S(2)}, u32[]{:S(2)}) collective-permute-start(f32[32,128]{1,0:T(8,128)S(1)} %add_add_fusion.2), channel_id=1, source_target_pairs={{0,16},{1,17},{2,18},{3,19},{4,20},{5,21},{6,22},{7,23},{8,24},{9,... | collective-permute-start | bytes 49160 | tf_op jit(solution)/shard_map/ppermute | solution.py:303
  81.0 9.2 %collective-permute-start.18 = (f32[32,128]{1,0:T(8,128)S(1)}, f32[32,128]{1,0:T(8,128)S(1)}, u32[]{:S(2)}, u32[]{:S(2)}) collective-permute-start(f32[32,128]{1,0:T(8,128)S(1)} %add_add_fusion.1), channel_id=1, source_target_pairs={{0,192},{1,193},{2,194},{3,195},{4,196},{5,197},{6,198},{7,199},{8... | collective-permute-start | bytes 49160 | tf_op jit(solution)/shard_map/ppermute | solution.py:303
  87.3 7.6 %collective-permute-start.17 = (f32[32,128]{1,0:T(8,128)S(1)}, f32[32,128]{1,0:T(8,128)S(1)}, u32[]{:S(2)}, u32[]{:S(2)}) collective-permute-start(f32[32,128]{1,0:T(8,128)S(1)} %add_add_fusion.1), channel_id=1, source_target_pairs={{0,128},{1,129},{2,130},{3,131},{4,132},{5,133},{6,134},{7,135},{8... | collective-permute-start | bytes 49160 | tf_op jit(solution)/shard_map/ppermute | solution.py:303
  90.2 4.8 %collective-permute-start.16 = (f32[32,128]{1,0:T(8,128)S(1)}, f32[32,128]{1,0:T(8,128)S(1)}, u32[]{:S(2)}, u32[]{:S(2)}) collective-permute-start(f32[32,128]{1,0:T(8,128)S(1)} %add_add_fusion.1), channel_id=1, source_target_pairs={{0,64},{1,65},{2,66},{3,67},{4,68},{5,69},{6,70},{7,71},{8,72},{9,... | collective-permute-start | bytes 49160 | tf_op jit(solution)/shard_map/ppermute | solution.py:303

commit v2 on v1

v2 whole, which is shorter than its diff:
```python
import functools
import jax
import jax.numpy as jnp
from jax import lax
from jax.experimental import pallas as pl
from jax.experimental.pallas import tpu as pltpu
from jax.sharding import PartitionSpec as P

OWN = ((0, 0), (0, 1), (1, 0), (1, 1))
BORDER = ((0, 2), (1, 2), (2, 0), (2, 1), (2, 2))
WINDOW = OWN + BORDER
PAIRED = tuple((i, j) for j in range(4) for i in range(j))
SELF = tuple((i, i) for i in range(4))
CROSS = tuple(
    (i, j)
    for j in range(4, 9)
    for i in range(4)
    if max(abs(OWN[i][0] - WINDOW[j][0]), abs(OWN[i][1] - WINDOW[j][1])) <= 1
)
BLOCK = 512
RHS = 16
FEATURES = 64
f32, bf16 = jnp.float32, jnp.bfloat16
VMEM = pl.BlockSpec(memory_space=pltpu.VMEM)


def call(kernel, name, out_shape, args, flops, scratch=(), args_space=pltpu.VMEM):
    return pl.pallas_call(
        kernel,
        name=name,
        out_shape=out_shape,
        in_specs=[pl.BlockSpec(memory_space=args_space)] * len(args),
        out_specs=jax.tree.map(lambda _: VMEM, out_shape),
        scratch_shapes=scratch,
        compiler_params=pltpu.CompilerParams(vmem_limit_bytes=16 << 20),
        cost_estimate=pl.CostEstimate(flops=flops, bytes_accessed=1 << 20, transcendentals=0),
    )(*args)


def split(value):
    high = value.astype(bf16).astype(f32)
    rest = value - high
    middle = rest.astype(bf16).astype(f32)
    return high, middle, rest - middle


def feature_rows(place):
    rows = lax.broadcasted_iota(jnp.int32, place.shape, 0)
    parts = split(place)
    norms = split(16.0 * jnp.sum(place * place, axis=0, keepdims=True))
    left, right = [], []
    for group, (a, b) in enumerate(((0, 0), (0, 1), (1, 0), (1, 1), (0, 2), (2, 0), (1, 2), (2, 1))):
        one_left, one_right = -32.0 * parts[a], parts[b]
        if group < 3:
            norm = jnp.broadcast_to(norms[group], place.shape)
            one_left = jnp.where(rows == 3, norm, jnp.where(rows == 4, 1.0, one_left))
            one_right = jnp.where(rows == 4, norm, jnp.where(rows == 3, 1.0, one_right))
        left.append(one_left)
        right.append(one_right)
    return jnp.concatenate(left, axis=0), jnp.concatenate(right, axis=0)


def prepare(
    points_far, noise_far, sides_far, sent, left, right, own_sides, own_noise,
    points, noise_var, right_sides, arrivals,
):
    copies = [
        pltpu.make_async_copy(source, target, arrivals.at[place])
        for place, (source, target) in enumerate(
            ((points_far, points), (noise_far, noise_var), (sides_far, right_sides))
        )
    ]
    for copy in copies:
        copy.start()
    for copy in copies:
        copy.wait()
    region = lax.axis_index("region")
    member = lax.axis_index("sub")
    row_half, column_half = member & 1, member >> 1
    rows = lax.broadcasted_iota(jnp.int32, (8, BLOCK), 0)
    centers = (
        region.astype(f32) + 0.5,
        row_half.astype(f32) + 1.5,
        column_half.astype(f32) + 1.5,
    )
    for index, (row, column) in enumerate(WINDOW):
        row = jnp.where(row_half == 1, 3 - row, row)
        column = jnp.where(column_half == 1, 3 - column, column)
        block = (row & 1) + 2 * (column & 1) + 4 * (row >> 1) + 8 * (column >> 1)
        place = jnp.zeros((8, BLOCK), f32)
        for axis in range(3):
            line = points[axis, pl.ds(block, 1), :] - centers[axis]
            place = jnp.where(rows == axis, jnp.broadcast_to(line, place.shape), place)
        side = right_sides[block]
        sent[index, 0:16, :] = side.astype(bf16)
        high, middle, low = split(place)
        sent[index, 16:32, :] = jnp.concatenate(
            [high + pltpu.roll(low, 3, 0), middle], axis=0
        ).astype(bf16)
        left_rows, right_rows = feature_rows(place)
        left[index] = jnp.transpose(left_rows).astype(bf16)
        if index < 4:
            right[index] = right_rows.astype(bf16)
            own_sides[index] = side
            own_noise[index] = noise_var[pl.ds(block, 1), :]


def neighbour_features(packed, shift):
    rows = lax.broadcasted_iota(jnp.int32, (8, BLOCK), 0)
    packed = packed.astype(f32)
    top, middle = packed[0:8], packed[8:16]
    place = jnp.where(rows < 3, top + middle + pltpu.roll(top, 5, 0), 0.0)
    place = jnp.where(rows == 0, place + shift, place)
    return feature_rows(place)


def sweep(lefts, rights, buffers, use):
    count = len(lefts)

    def distances(step):
        buffers[step % 2][...] = jnp.dot(
            lefts[step](), rights[step](), preferred_element_type=f32
        )

    distances(0)
    for step in range(count):
        if step + 1 < count:
            distances(step + 1)
        parts = []
        for start in range(0, BLOCK, 64):
            squared = jnp.maximum(buffers[step % 2][start:start + 64, :], 1e-30)
            falloff = jnp.maximum(4.0 - squared * lax.rsqrt(squared), 0.0)
            second = falloff * falloff
            parts.append(((second * second) * (5.0 - falloff)).astype(bf16))
        use(step, jnp.concatenate(parts, axis=0))


def times(vectors, tile):
    return jnp.dot(vectors, tile, preferred_element_type=f32)


def times_transposed(vectors, tile):
    return lax.dot_general(vectors, tile, (((1,), (1,)), ((), ())), preferred_element_type=f32)


def within_layer(sent, left, right, totals, tiles, *buffers):
    totals[...] = jnp.zeros_like(totals)
    pairs = SELF + PAIRED + CROSS

    def use(step, tile):
        i, j = pairs[step]
        tiles[step] = tile
        totals[i] += times(sent[j, 0:16, :], tile)
        if i != j and j < 4:
            totals[j] += times_transposed(sent[i, 0:16, :], tile)

    sweep(
        [lambda j=j: left[j] for i, j in pairs],
        [lambda i=i: right[i] for i, j in pairs],
        buffers, use,
    )


def above_own(sent, left, right, above, before, totals, passed, tiles, left_above, right_above, *buffers):
    totals[...] = before[...]
    passed[...] = jnp.zeros_like(passed)
    for j in range(4):
        left_rows, right_rows = neighbour_features(above[j, 16:32, :], 1.0)
        left_above[j] = jnp.transpose(left_rows).astype(bf16)
        right_above[j] = right_rows.astype(bf16)

    def use(step, tile):
        tiles[step] = tile
        if step < 16:
            i, j = step % 4, step // 4
            totals[i] += times(above[j, 0:16, :], tile)
            passed[j] += times_transposed(sent[i, 0:16, :], tile)
        else:
            j, border = CROSS[step - 16]
            passed[j] += times(sent[border, 0:16, :], tile)

    sweep(
        [lambda j=step // 4: left_above[j] for step in range(16)]
        + [lambda border=border: left[border] for j, border in CROSS],
        [lambda i=step % 4: right[i] for step in range(16)]
        + [lambda j=j: right_above[j] for j, border in CROSS],
        buffers, use,
    )


def above_border(right, above, before, totals, left_above, *buffers):
    totals[...] = before[...]
    for j in range(5):
        left_above[j] = jnp.transpose(
            neighbour_features(above[4 + j, 16:32, :], 1.0)[0]
        ).astype(bf16)

    def use(step, tile):
        i, j = CROSS[step]
        totals[i] += times(above[j, 0:16, :], tile)

    sweep(
        [lambda j=j: left_above[j - 4] for i, j in CROSS],
        [lambda i=i: right[i] for i, j in CROSS],
        buffers, use,
    )


def finish_image(totals, arrived, own_noise, own_sides, image, rounded):
    value = (totals[...] + arrived[...]) * (1.0 / 256.0) + own_noise[...] * own_sides[...]
    image[...] = value
    rounded[...] = value.astype(bf16)


def gram(first, second):
    return lax.dot_general(
        first, second, (((1,), (1,)), ((), ())),
        precision=lax.Precision.HIGHEST, preferred_element_type=f32,
    )


def side_by_side(blocks):
    return jnp.concatenate(blocks, axis=1)


def inside(own_sides, image, rounded, own_noise, tiles, products, partial):
    both = jnp.concatenate(
        [side_by_side([image[i] for i in range(4)]), side_by_side([own_sides[i] for i in range(4)])],
        axis=0,
    )
    products[...] = gram(both, both)
    single = [times(rounded[i], tiles[i]) for i in range(4)]
    double = [jnp.zeros((RHS, BLOCK), f32)] * 4
    for step, (i, j) in enumerate(PAIRED):
        double[i] += times(rounded[j], tiles[4 + step])
    for i in range(4):
        partial[i] = own_noise[i] * image[i] * 256.0 + single[i] + 2.0 * double[i]


def outside(from_row, from_column, from_corner, upper, tiles_here, tiles_up, before, image, products, system):
    sources = {4: (from_column, 0), 5: (from_column, 1), 6: (from_row, 0), 7: (from_row, 1), 8: (from_corner, 0)}
    border = {j: ref[place] for j, (ref, place) in sources.items()}
    partial = [before[i] for i in range(4)]
    double = [jnp.zeros((RHS, BLOCK), f32)] * 4
    raised = [jnp.zeros((RHS, BLOCK), f32)] * 4
    for step in range(16):
        double[step % 4] += times(upper[step // 4], tiles_up[step])
    for step, (i, j) in enumerate(CROSS):
        partial[i] += times(border[j], tiles_here[10 + step])
        raised[i] += times(border[j], tiles_up[16 + step])
    third = gram(
        side_by_side([image[i] for i in range(4)] + [upper[i].astype(f32) for i in range(4)]),
        side_by_side([partial[i] + 2.0 * double[i] for i in range(4)] + [2.0 * raised[i] for i in range(4)]),
    ) * (1.0 / 256.0)
    known = products[...]
    second, mixed = known[0:16, 0:16], known[0:16, 16:32]
    crossed, start = known[16:32, 0:16], known[16:32, 16:32]
    top = jnp.concatenate([crossed, second, start, jnp.zeros((RHS, 80), f32)], axis=1)
    bottom = jnp.concatenate([second, third, mixed, jnp.zeros((RHS, 80), f32)], axis=1)
    system[...] = jnp.concatenate([top, bottom], axis=0)


def conclude(system, own_sides, image, result):
    value = system[...]
    lanes = lax.broadcasted_iota(jnp.int32, (32, 128), 1)
    rows = lax.broadcasted_iota(jnp.int32, (32, 128), 0)
    flipped = jnp.transpose(jnp.concatenate([value, jnp.zeros((96, 128), f32)], axis=0))[0:32]
    value = jnp.where(lanes < 32, 0.5 * (value + flipped), value)
    for k in range(0, 32, 2):
        first_column = jnp.broadcast_to(value[:, k:k + 1], value.shape)
        second_column = jnp.broadcast_to(value[:, k + 1:k + 2], value.shape)
        a, b = first_column[k:k + 1], second_column[k:k + 1]
        c, d = first_column[k + 1:k + 2], second_column[k + 1:k + 2]
        first_row, second_row = value[k:k + 1], value[k + 1:k + 2]
        inverse = 1.0 / (a * d - b * c)
        first_new = (d * first_row - b * second_row) * inverse
        second_new = (a * second_row - c * first_row) * inverse
        value = value - first_column * first_new - second_column * second_new
        value = jnp.where(rows == k, first_new, jnp.where(rows == k + 1, second_new, value))
    weights = jnp.transpose(jnp.concatenate([value, jnp.zeros((96, 128), f32)], axis=0))[32:48, 0:32]
    member = lax.axis_index("sub")
    for i, (row, column) in enumerate(OWN):
        both = jnp.concatenate([own_sides[i], image[i]], axis=0)
        place = (row ^ (member & 1)) + 2 * (column ^ (member >> 1))
        result[place] = jnp.dot(
            weights, both, precision=lax.Precision.HIGHEST, preferred_element_type=f32
        )


def local(regions, members, points, noise_var, right_sides, pair_list, pair_count):
    everyone = regions * members

    def from_region(value, step):
        pairs = [
            (source, source - step)
            for source in range(regions)
            if 0 <= source - step < regions
        ]
        return lax.ppermute(value, "region", pairs)

    def from_member(value, mask):
        return lax.ppermute(value, "sub", [(source, source ^ mask) for source in range(members)])

    def sum_over_all(value):
        rounds = [[lambda p, m=m: p ^ m for m in masks] for masks in ((1, 2, 3), (4, 8, 12), (24,))]
        for order in ((1, 0, 3, 2, 5, 4, 7, 6), (7, 2, 1, 4, 3, 6, 5, 0), (3, 6, 5, 0, 7, 2, 1, 4)):
            rounds.append([lambda p, order=order: p % 32 + 32 * order[p // 32]])
        for partners in rounds:
            value = value + sum(
                lax.ppermute(value, ("region", "sub"), [(p, partner(p)) for p in range(everyone)])
                for partner in partners
            )
        return value

    def shape(*dims, dtype=f32):
        return jax.ShapeDtypeStruct(dims, dtype)

    def held(*dims, dtype=bf16):
        return pltpu.VMEM(dims, dtype)

    tile_flops = 2 * BLOCK * BLOCK * 256
    field = (4, RHS, BLOCK)
    buffers = [pltpu.VMEM((BLOCK, BLOCK), f32)] * 2
    sent, left, right, own_sides, own_noise = call(
        prepare, "prepare",
        (shape(9, 32, BLOCK, dtype=bf16), shape(9, BLOCK, FEATURES, dtype=bf16),
         shape(4, FEATURES, BLOCK, dtype=bf16), shape(*field), shape(4, 1, BLOCK)),
        [pltpu.with_memory_space_constraint(value, pltpu.HBM) for value in (points, noise_var, right_sides)],
        tile_flops,
        [pltpu.VMEM(value.shape, f32) for value in (points, noise_var, right_sides)]
        + [pltpu.SemaphoreType.DMA((3,))],
        pltpu.HBM,
    )
    above = from_region(sent, 1)
    totals, tiles_here = call(
        within_layer, "within_layer", (shape(*field), held(19, BLOCK, BLOCK)),
        (sent, left, right), 19 * 4 * tile_flops, buffers,
    )
    totals, passed, tiles_up = call(
        above_own, "above_own", (shape(*field), shape(*field), held(25, BLOCK, BLOCK)),
        (sent, left, right, above, totals), 25 * 4 * tile_flops,
        [pltpu.VMEM((4, BLOCK, FEATURES), bf16), pltpu.VMEM((4, FEATURES, BLOCK), bf16)] + buffers,
    )
    arrived = from_region(passed, -1)
    totals = call(
        above_border, "above_border", shape(*field), (right, above, totals), 9 * 4 * tile_flops,
        [pltpu.VMEM((5, BLOCK, FEATURES), bf16)] + buffers,
    )
    image, rounded = call(
        finish_image, "finish_image", (shape(*field), shape(*field, dtype=bf16)),
        (totals, arrived, own_noise, own_sides), tile_flops // 8,
    )
    upper = from_region(rounded, 1)
    from_row = from_member(rounded[2:4], 1)
    from_column = from_member(rounded[1::2], 2)
    from_corner = from_member(rounded[3:4], 3)
    products, partial = call(
        inside, "inside", (shape(32, 32), shape(*field)),
        (own_sides, image, rounded, own_noise, tiles_here), 10 * 2 * tile_flops,
    )
    system = call(
        outside, "outside", shape(32, 128),
        (from_row, from_column, from_corner, upper, tiles_here, tiles_up, partial, image, products),
        34 * 2 * tile_flops,
    )
    system = sum_over_all(system)
    return call(
        conclude, "conclude", shape(*field), (system, own_sides, image), tile_flops,
    )


def solution(mesh):
    return jax.shard_map(
        functools.partial(local, mesh.shape["region"], mesh.shape["sub"]),
        mesh=mesh,
        in_specs=(
            P(None, "region", None),
            P("region", None),
            P("region", None, None),
            P("region", "sub", None, None),
            P("region", "sub"),
        ),
        out_specs=P(("region", "sub"), None, None),
        check_vma=False,
    )
```

time: 100 us -> 84 us (0.84); the launches traced: 98.7 us -> 83.8 us
  Pallas kernels: 40.5 us -> 31.6 us
  local copies, waits for them, and re-layouts: 2.71 us -> 0.01 us
  waiting for transfers between devices: 18.7 us -> 16.1 us
    pallas_call x9 -> x8, Pallas kernels: 40.5 us -> 31.6 us  [call(): pl.pallas_call(kernel, name=name, out_shape=out_shape, in_specs=[pl.Block...]
    ppermute x4 -> x3, starting transfers between devices: 8.83 us -> 5.61 us  [from_region(): return lax.ppermute(value, 'region', pairs)]
    unnamed x6 -> x0, local copies, waits for them, and re-layouts: 2.69 us -> none
    ppermute x12 -> x10, starting transfers between devices: 24.3 us -> 26 us  [sum_over_all(): lax.ppermute(value, ('region', 'sub'), [(p, partner(p)) for p in range(ev...]
    ppermute x3, waiting for transfers between devices: 4.44 us -> 2.9 us  [from_member(): lax.ppermute(value, 'sub', [(source, source ^ mask) for source in range(m...]
    ppermute x12 -> x10, waiting for transfers between devices: 13.5 us -> 13.2 us  [sum_over_all(): lax.ppermute(value, ('region', 'sub'), [(p, partner(p)) for p in range(ev...]
  transfers between devices with their start and end apart: 19 -> 16, of which waited for: 11 -> 9; matrix products, arithmetic and copies ran while one was open for 0% -> 0% of each run, Pallas kernels for 35% -> 16%
where the time goes in v2:
time: 84 us; the launch traced here: 83.8 us
  starting transfers between devices  36 us (43%)
  Pallas kernels  31.6 us (38%)
  waiting for transfers between devices  16.1 us (19%)
    pallas_call x8, Pallas kernels, call(): pl.pallas_call(kernel, name=name, out_shape=out_shape, in_specs=[pl.Block...  31.6 us
    ppermute x10, starting transfers between devices, sum_over_all(): lax.ppermute(value, ('region', 'sub'), [(p, partner(p)) for p in range(ev...  26 us
    ppermute x10, waiting for transfers between devices, sum_over_all(): lax.ppermute(value, ('region', 'sub'), [(p, partner(p)) for p in range(ev...  13.2 us
    ppermute x3, starting transfers between devices, from_region(): return lax.ppermute(value, 'region', pairs)  5.61 us
    ppermute x3, starting transfers between devices, from_member(): lax.ppermute(value, 'sub', [(source, source ^ mask) for source in range(m...  4.34 us
    ppermute x3, waiting for transfers between devices, from_member(): lax.ppermute(value, 'sub', [(source, source ^ mask) for source in range(m...  2.9 us
  transfers between devices with their start and end apart: 16, of which 9 were waited for; matrix products, arithmetic and copies ran while one was open for 0% of the time, Pallas kernels for 16%

profile of v2, /device:TPU:8, one launch (start us, length us, event | category | flops | bytes accessed | tf_op | source)
XLA Modules:
  0.0 83.8 jit_solution(4628409236729314723)
XLA Ops:
  0.0 1.6 %prepare.1 = (bf16[9,32,512]{2,1,0:T(8,128)(2,1)S(1)}, bf16[9,512,64]{2,1,0:T(8,128)(2,1)S(1)}, bf16[4,64,512]{2,1,0:T(8,128)(2,1)S(1)}, f32[4,16,512]{2,1,0:T(8,128)S(1)}, f32[4,1,512]{2,1,0:T(1,128)S(1)}) custom-call(f32[3,16,512]{2,1,0:T(8,128)} %points_far.1, f32[16,512]{1,0:T(8,128)} %noise_far.1, f32[16,16,512]{2,1,0:T(8,128)} %sides_far.1), custom_call_target="tpu_custom_call" | custom-call | flops 134217728 | bytes 1048576 | tf_op jit(solution)/shard_map/prepare/pallas_call | solution.py:28
  1.6 1.3 %collective-permute-start = (bf16[9,32,512]{2,1,0:T(8,128)(2,1)S(1)}, bf16[9,32,512]{2,1,0:T(8,128)(2,1)S(1)}, u32[]{:S(2)}, u32[]{:S(2)}) collective-permute-start(bf16[9,32,512]{2,1,0:T(8,128)(2,1)S(1)} %get-tuple-element.20.sent), channel_id=1, source_target_pairs={{4,0},{8,4},{12,8},{16,12},{20,16},{24,20},{28,24},{32,28},{36,32}... | collective-permute-start | bytes 884744 | tf_op jit(solution)/shard_map/ppermute | solution.py:299
  2.9 8.1 %within_layer.1 = (f32[4,16,512]{2,1,0:T(8,128)S(1)}, bf16[19,512,512]{2,1,0:T(8,128)(2,1)S(1)}) custom-call(bf16[9,32,512]{2,1,0:T(8,128)(2,1)S(1)} %get-tuple-element.20.sent, bf16[9,512,64]{2,1,0:T(8,128)(2,1)S(1)} %get-tuple-element.21.left, bf16[4,64,512]{2,1,0:T(8,128)(2,1)S(1)} %get-tuple-element.19.right), custom_call_target="tpu_custom_call" | custom-call | flops 10200547328 | bytes 1048576 | tf_op jit(solution)/shard_map/within_layer/pallas_call | solution.py:28
  11.0 0.0 collective-permute-done.above
  11.0 11.1 %above_own.1 = (f32[4,16,512]{2,1,0:T(8,128)S(1)}, f32[4,16,512]{2,1,0:T(8,128)S(1)}, bf16[25,512,512]{2,1,0:T(8,128)(2,1)S(1)}) custom-call(bf16[9,32,512]{2,1,0:T(8,128)(2,1)S(1)} %get-tuple-element.20.sent, bf16[9,512,64]{2,1,0:T(8,128)(2,1)S(1)} %get-tuple-element.21.left, bf16[4,64,512]{2,1,0:T(8,128)(2,1)S(1)} %get-tuple-element.19.right, ...), custom_call_target="tpu_custom_call" | custom-call | flops 13421772800 | bytes 1048576 | tf_op jit(solution)/shard_map/above_own/pallas_call | solution.py:28
  22.1 3.0 %collective-permute-start.1 = (f32[4,16,512]{2,1,0:T(8,128)S(1)}, f32[4,16,512]{2,1,0:T(8,128)S(1)}, u32[]{:S(2)}, u32[]{:S(2)}) collective-permute-start(f32[4,16,512]{2,1,0:T(8,128)S(1)} %get-tuple-element.24), channel_id=1, source_target_pairs={{0,4},{4,8},{8,12},{12,16},{16,20},{20,24},{24,28},{28,32},{32,36}... | collective-permute-start | bytes 393224 | tf_op jit(solution)/shard_map/ppermute | solution.py:299
  25.1 4.0 %above_border.1.totals = f32[4,16,512]{2,1,0:T(8,128)S(1)} custom-call(bf16[4,64,512]{2,1,0:T(8,128)(2,1)S(1)} %get-tuple-element.19.right, bf16[9,32,512]{2,1,0:T(8,128)(2,1)S(1)} %collective-permute-done.above, f32[4,16,512]{2,1,0:T(8,128)S(1)} %get-tuple-element.23.before), custom_call_target="tpu_custom_call" | custom-call | flops 4831838208 | bytes 1048576 | tf_op jit(solution)/shard_map/above_border/pallas_call | solution.py:28
  29.1 0.0 collective-permute-done.1.arrived
  29.2 1.3 %collective-permute-start.5 = (bf16[4,16,512]{2,1,0:T(8,128)(2,1)S(1)}, bf16[4,16,512]{2,1,0:T(8,128)(2,1)S(1)}, u32[]{:S(2)}, u32[]{:S(2)}) collective-permute-start(bf16[4,16,512]{2,1,0:T(8,128)(2,1)S(1)} %get-tuple-element.27.rounded), channel_id=1, source_target_pairs={{4,0},{8,4},{12,8},{16,12},{20,16},{24,20},{28,24},{32,28},{36,32}... | collective-permute-start | bytes 196616 | tf_op jit(solution)/shard_map/ppermute | solution.py:299
  30.5 1.7 %collective-permute-start.4 = (bf16[1,16,512]{2,1,0:T(8,128)(2,1)S(1)}, bf16[1,16,512]{2,1,0:T(8,128)(2,1)S(1)}, u32[]{:S(2)}, u32[]{:S(2)}) collective-permute-start(bf16[1,16,512]{2,1,0:T(8,128)(2,1)S(1)} %slice.11), channel_id=1, source_target_pairs={{0,3},{1,2},{2,1},{3,0},{4,7},{5,6},{6,5},{7,4},{8,11},{9,10},{10,... | collective-permute-start | bytes 49160 | tf_op jit(solution)/shard_map/ppermute | solution.py:302
  32.2 2.7 %collective-permute-start.3 = (bf16[2,16,512]{2,1,0:T(8,128)(2,1)S(1)}, bf16[2,16,512]{2,1,0:T(8,128)(2,1)S(1)}, u32[]{:S(2)}, u32[]{:S(2)}) collective-permute-start(bf16[2,16,512]{2,1,0:T(8,128)(2,1)S(1)} %get-tuple-element.33), channel_id=1, source_target_pairs={{0,2},{1,3},{2,0},{3,1},{4,6},{5,7},{6,4},{7,5},{8,10},{9,11},{10,... | collective-permute-start | bytes 98312 | tf_op jit(solution)/shard_map/ppermute | solution.py:302
  34.8 0.0 collective-permute-start.2
  34.8 1.0 %inside.1 = (f32[32,32]{1,0:T(8,128)S(1)}, f32[4,16,512]{2,1,0:T(8,128)S(1)}) custom-call(f32[4,16,512]{2,1,0:T(8,128)S(1)} %get-tuple-element.26.own_sides, f32[4,16,512]{2,1,0:T(8,128)S(1)} %get-tuple-element.30.image, bf16[4,16,512]{2,1,0:T(8,128)(2,1)S(1)} %get-tuple-element.27.rounded, f32[4,1,512]{2,1,0:T(1,128)S(1)} %get-tuple-element.25.own_noise, ...), custom_call_target="tpu_custom_call" | custom-call | flops 2684354560 | bytes 1048576 | tf_op jit(solution)/shard_map/inside/pallas_call | solution.py:28
  35.8 0.0 collective-permute-done.4.from_corner
  35.9 1.7 %collective-permute-done.3.from_column = bf16[2,16,512]{2,1,0:T(8,128)(2,1)S(1)} collective-permute-done((bf16[2,16,512]{2,1,0:T(8,128)(2,1)S(1)}, bf16[2,16,512]{2,1,0:T(8,128)(2,1)S(1)}, u32[]{:S(2)}, u32[]{:S(2)}) %collective-permute-start.3) | collective-permute-done | bytes 32800 | tf_op jit(solution)/shard_map/ppermute | solution.py:302
  37.6 1.2 %collective-permute-done.2.from_row = bf16[2,16,512]{2,1,0:T(8,128)(2,1)S(1)} collective-permute-done((bf16[2,16,512]{2,1,0:T(8,128)(2,1)S(1)}, bf16[2,16,512]{2,1,0:T(8,128)(2,1)S(1)}, u32[]{:S(2)}, u32[]{:S(2)}) %collective-permute-start.2) | collective-permute-done | bytes 32800 | tf_op jit(solution)/shard_map/ppermute | solution.py:302
  38.8 0.0 collective-permute-done.5.upper
  38.8 3.2 %outside.1 = f32[32,128]{1,0:T(8,128)S(1)} custom-call(bf16[2,16,512]{2,1,0:T(8,128)(2,1)S(1)} %collective-permute-done.2.from_row, bf16[2,16,512]{2,1,0:T(8,128)(2,1)S(1)} %collective-permute-done.3.from_column, bf16[1,16,512]{2,1,0:T(8,128)(2,1)S(1)} %collective-permute-done.4.from_corner, bf16[4,16,512]{2,1,0:T(8,128)(2,1)S(1)} %collective-permute-done.5.upper, ...), custom_call_target="tpu_custom_call" | custom-call | flops 9126805504 | bytes 1048576 | tf_op jit(solution)/shard_map/outside/pallas_call | solution.py:28
  42.0 0.9 %collective-permute-start.8 = (f32[32,128]{1,0:T(8,128)S(1)}, f32[32,128]{1,0:T(8,128)S(1)}, u32[]{:S(2)}, u32[]{:S(2)}) collective-permute-start(f32[32,128]{1,0:T(8,128)S(1)} %outside.1), channel_id=1, source_target_pairs={{0,3},{1,2},{2,1},{3,0},{4,7},{5,6},{6,5},{7,4},{8,11},{9,10},{10,... | collective-permute-start | bytes 49160 | tf_op jit(solution)/shard_map/ppermute | solution.py:310
  42.8 2.2 %collective-permute-start.7 = (f32[32,128]{1,0:T(8,128)S(1)}, f32[32,128]{1,0:T(8,128)S(1)}, u32[]{:S(2)}, u32[]{:S(2)}) collective-permute-start(f32[32,128]{1,0:T(8,128)S(1)} %outside.1), channel_id=1, source_target_pairs={{0,2},{1,3},{2,0},{3,1},{4,6},{5,7},{6,4},{7,5},{8,10},{9,11},{10,... | collective-permute-start | bytes 49160 | tf_op jit(solution)/shard_map/ppermute | solution.py:310
  45.0 1.1 %collective-permute-start.6 = (f32[32,128]{1,0:T(8,128)S(1)}, f32[32,128]{1,0:T(8,128)S(1)}, u32[]{:S(2)}, u32[]{:S(2)}) collective-permute-start(f32[32,128]{1,0:T(8,128)S(1)} %outside.1), channel_id=1, source_target_pairs={{0,1},{1,0},{2,3},{3,2},{4,5},{5,4},{6,7},{7,6},{8,9},{9,8},{10,11... | collective-permute-start | bytes 49160 | tf_op jit(solution)/shard_map/ppermute | solution.py:310
  46.1 0.0 collective-permute-done.8
  46.1 2.1 %collective-permute-done.7 = f32[32,128]{1,0:T(8,128)S(1)} collective-permute-done((f32[32,128]{1,0:T(8,128)S(1)}, f32[32,128]{1,0:T(8,128)S(1)}, u32[]{:S(2)}, u32[]{:S(2)}) %collective-permute-start.7) | collective-permute-done | bytes 16416 | tf_op jit(solution)/shard_map/ppermute | solution.py:310
  48.2 0.6 collective-permute-done.6
  48.8 0.0 collective-permute-start.11
  48.8 3.2 %collective-permute-start.10 = (f32[32,128]{1,0:T(8,128)S(1)}, f32[32,128]{1,0:T(8,128)S(1)}, u32[]{:S(2)}, u32[]{:S(2)}) collective-permute-start(f32[32,128]{1,0:T(8,128)S(1)} %add_add_fusion.1), channel_id=1, source_target_pairs={{0,8},{1,9},{2,10},{3,11},{4,12},{5,13},{6,14},{7,15},{8,0},{9,1},... | collective-permute-start | bytes 49160 | tf_op jit(solution)/shard_map/ppermute | solution.py:310
  52.0 0.0 collective-permute-start.9
  52.0 0.0 collective-permute-done.11
  52.0 1.8 %collective-permute-done.10 = f32[32,128]{1,0:T(8,128)S(1)} collective-permute-done((f32[32,128]{1,0:T(8,128)S(1)}, f32[32,128]{1,0:T(8,128)S(1)}, u32[]{:S(2)}, u32[]{:S(2)}) %collective-permute-start.10) | collective-permute-done | bytes 16416 | tf_op jit(solution)/shard_map/ppermute | solution.py:310
  53.8 0.0 collective-permute-done.9
  53.8 3.6 %collective-permute-start.12 = (f32[32,128]{1,0:T(8,128)S(1)}, f32[32,128]{1,0:T(8,128)S(1)}, u32[]{:S(2)}, u32[]{:S(2)}) collective-permute-start(f32[32,128]{1,0:T(8,128)S(1)} %add_add_fusion), channel_id=1, source_target_pairs={{0,24},{1,25},{2,26},{3,27},{4,28},{5,29},{6,30},{7,31},{8,16},{9,... | collective-permute-start | bytes 49160 | tf_op jit(solution)/shard_map/ppermute | solution.py:310
  57.4 1.7 %collective-permute-done.12 = f32[32,128]{1,0:T(8,128)S(1)} collective-permute-done((f32[32,128]{1,0:T(8,128)S(1)}, f32[32,128]{1,0:T(8,128)S(1)}, u32[]{:S(2)}, u32[]{:S(2)}) %collective-permute-start.12) | collective-permute-done | bytes 16416 | tf_op jit(solution)/shard_map/ppermute | solution.py:310
  59.1 6.0 %collective-permute-start.13 = (f32[32,128]{1,0:T(8,128)S(1)}, f32[32,128]{1,0:T(8,128)S(1)}, u32[]{:S(2)}, u32[]{:S(2)}) collective-permute-start(f32[32,128]{1,0:T(8,128)S(1)} %add.36), channel_id=1, source_target_pairs={{0,32},{1,33},{2,34},{3,35},{4,36},{5,37},{6,38},{7,39},{8,40},{9,... | collective-permute-start | bytes 49160 | tf_op jit(solution)/shard_map/ppermute | solution.py:310
  65.1 1.7 %collective-permute-done.13 = f32[32,128]{1,0:T(8,128)S(1)} collective-permute-done((f32[32,128]{1,0:T(8,128)S(1)}, f32[32,128]{1,0:T(8,128)S(1)}, u32[]{:S(2)}, u32[]{:S(2)}) %collective-permute-start.13) | collective-permute-done | bytes 16416 | tf_op jit(solution)/shard_map/ppermute | solution.py:310
  66.8 6.9 %collective-permute-start.14 = (f32[32,128]{1,0:T(8,128)S(1)}, f32[32,128]{1,0:T(8,128)S(1)}, u32[]{:S(2)}, u32[]{:S(2)}) collective-permute-start(f32[32,128]{1,0:T(8,128)S(1)} %add.37), channel_id=1, source_target_pairs={{0,224},{1,225},{2,226},{3,227},{4,228},{5,229},{6,230},{7,231},{8... | collective-permute-start | bytes 49160 | tf_op jit(solution)/shard_map/ppermute | solution.py:310
  73.7 1.7 %collective-permute-done.14 = f32[32,128]{1,0:T(8,128)S(1)} collective-permute-done((f32[32,128]{1,0:T(8,128)S(1)}, f32[32,128]{1,0:T(8,128)S(1)}, u32[]{:S(2)}, u32[]{:S(2)}) %collective-permute-start.14) | collective-permute-done | bytes 16416 | tf_op jit(solution)/shard_map/ppermute | solution.py:310
  75.4 2.2 %collective-permute-start.15 = (f32[32,128]{1,0:T(8,128)S(1)}, f32[32,128]{1,0:T(8,128)S(1)}, u32[]{:S(2)}, u32[]{:S(2)}) collective-permute-start(f32[32,128]{1,0:T(8,128)S(1)} %add.38), channel_id=1, source_target_pairs={{0,96},{1,97},{2,98},{3,99},{4,100},{5,101},{6,102},{7,103},{8,104... | collective-permute-start | bytes 49160 | tf_op jit(solution)/shard_map/ppermute | solution.py:310
  77.6 3.6 %collective-permute-done.15 = f32[32,128]{1,0:T(8,128)S(1)} collective-permute-done((f32[32,128]{1,0:T(8,128)S(1)}, f32[32,128]{1,0:T(8,128)S(1)}, u32[]{:S(2)}, u32[]{:S(2)}) %collective-permute-start.15) | collective-permute-done | bytes 16416 | tf_op jit(solution)/shard_map/ppermute | solution.py:310
  81.2 2.6 %conclude.1 = f32[4,16,512]{2,1,0:T(8,128)} custom-call(f32[32,128]{1,0:T(8,128)S(1)} %add.39.system, f32[4,16,512]{2,1,0:T(8,128)S(1)} %get-tuple-element.26.own_sides, f32[4,16,512]{2,1,0:T(8,128)S(1)} %get-tuple-element.30.image), custom_call_target="tpu_custom_call" | custom-call | flops 134217728 | bytes 1048576 | tf_op jit(solution)/shard_map/conclude/pallas_call | solution.py:28
  (9 shorter events, 0.1 us)
Async XLA Ops:
  1.6 9.4 %collective-permute-start = (bf16[9,32,512]{2,1,0:T(8,128)(2,1)S(1)}, bf16[9,32,512]{2,1,0:T(8,128)(2,1)S(1)}, u32[]{:S(2)}, u32[]{:S(2)}) collective-permute-start(bf16[9,32,512]{2,1,0:T(8,128)(2,1)S(1)} %get-tuple-element.20.sent), channel_id=1, source_target_pairs={{4,0},{8,4},{12,8},{16,12},{20,16},{24,20},{28,24},{32,28},{36,32}... | collective-permute-start | bytes 884744 | tf_op jit(solution)/shard_map/ppermute | solution.py:299
  22.1 7.1 %collective-permute-start.1 = (f32[4,16,512]{2,1,0:T(8,128)S(1)}, f32[4,16,512]{2,1,0:T(8,128)S(1)}, u32[]{:S(2)}, u32[]{:S(2)}) collective-permute-start(f32[4,16,512]{2,1,0:T(8,128)S(1)} %get-tuple-element.24), channel_id=1, source_target_pairs={{0,4},{4,8},{8,12},{12,16},{16,20},{20,24},{24,28},{28,32},{32,36}... | collective-permute-start | bytes 393224 | tf_op jit(solution)/shard_map/ppermute | solution.py:299
  29.2 9.6 %collective-permute-start.5 = (bf16[4,16,512]{2,1,0:T(8,128)(2,1)S(1)}, bf16[4,16,512]{2,1,0:T(8,128)(2,1)S(1)}, u32[]{:S(2)}, u32[]{:S(2)}) collective-permute-start(bf16[4,16,512]{2,1,0:T(8,128)(2,1)S(1)} %get-tuple-element.27.rounded), channel_id=1, source_target_pairs={{4,0},{8,4},{12,8},{16,12},{20,16},{24,20},{28,24},{32,28},{36,32}... | collective-permute-start | bytes 196616 | tf_op jit(solution)/shard_map/ppermute | solution.py:299
  30.5 5.3 %collective-permute-start.4 = (bf16[1,16,512]{2,1,0:T(8,128)(2,1)S(1)}, bf16[1,16,512]{2,1,0:T(8,128)(2,1)S(1)}, u32[]{:S(2)}, u32[]{:S(2)}) collective-permute-start(bf16[1,16,512]{2,1,0:T(8,128)(2,1)S(1)} %slice.11), channel_id=1, source_target_pairs={{0,3},{1,2},{2,1},{3,0},{4,7},{5,6},{6,5},{7,4},{8,11},{9,10},{10,... | collective-permute-start | bytes 49160 | tf_op jit(solution)/shard_map/ppermute | solution.py:302
  32.2 5.4 %collective-permute-start.3 = (bf16[2,16,512]{2,1,0:T(8,128)(2,1)S(1)}, bf16[2,16,512]{2,1,0:T(8,128)(2,1)S(1)}, u32[]{:S(2)}, u32[]{:S(2)}) collective-permute-start(bf16[2,16,512]{2,1,0:T(8,128)(2,1)S(1)} %get-tuple-element.33), channel_id=1, source_target_pairs={{0,2},{1,3},{2,0},{3,1},{4,6},{5,7},{6,4},{7,5},{8,10},{9,11},{10,... | collective-permute-start | bytes 98312 | tf_op jit(solution)/shard_map/ppermute | solution.py:302
  34.8 3.9 %collective-permute-start.2 = (bf16[2,16,512]{2,1,0:T(8,128)(2,1)S(1)}, bf16[2,16,512]{2,1,0:T(8,128)(2,1)S(1)}, u32[]{:S(2)}, u32[]{:S(2)}) collective-permute-start(bf16[2,16,512]{2,1,0:T(8,128)(2,1)S(1)} %get-tuple-element.34), channel_id=1, source_target_pairs={{0,1},{1,0},{2,3},{3,2},{4,5},{5,4},{6,7},{7,6},{8,9},{9,8},{10,11... | collective-permute-start | bytes 98312 | tf_op jit(solution)/shard_map/ppermute | solution.py:302
  42.0 4.1 %collective-permute-start.8 = (f32[32,128]{1,0:T(8,128)S(1)}, f32[32,128]{1,0:T(8,128)S(1)}, u32[]{:S(2)}, u32[]{:S(2)}) collective-permute-start(f32[32,128]{1,0:T(8,128)S(1)} %outside.1), channel_id=1, source_target_pairs={{0,3},{1,2},{2,1},{3,0},{4,7},{5,6},{6,5},{7,4},{8,11},{9,10},{10,... | collective-permute-start | bytes 49160 | tf_op jit(solution)/shard_map/ppermute | solution.py:310
  42.8 5.4 %collective-permute-start.7 = (f32[32,128]{1,0:T(8,128)S(1)}, f32[32,128]{1,0:T(8,128)S(1)}, u32[]{:S(2)}, u32[]{:S(2)}) collective-permute-start(f32[32,128]{1,0:T(8,128)S(1)} %outside.1), channel_id=1, source_target_pairs={{0,2},{1,3},{2,0},{3,1},{4,6},{5,7},{6,4},{7,5},{8,10},{9,11},{10,... | collective-permute-start | bytes 49160 | tf_op jit(solution)/shard_map/ppermute | solution.py:310
  45.0 3.7 %collective-permute-start.6 = (f32[32,128]{1,0:T(8,128)S(1)}, f32[32,128]{1,0:T(8,128)S(1)}, u32[]{:S(2)}, u32[]{:S(2)}) collective-permute-start(f32[32,128]{1,0:T(8,128)S(1)} %outside.1), channel_id=1, source_target_pairs={{0,1},{1,0},{2,3},{3,2},{4,5},{5,4},{6,7},{7,6},{8,9},{9,8},{10,11... | collective-permute-start | bytes 49160 | tf_op jit(solution)/shard_map/ppermute | solution.py:310
  48.8 3.3 %collective-permute-start.11 = (f32[32,128]{1,0:T(8,128)S(1)}, f32[32,128]{1,0:T(8,128)S(1)}, u32[]{:S(2)}, u32[]{:S(2)}) collective-permute-start(f32[32,128]{1,0:T(8,128)S(1)} %add_add_fusion.1), channel_id=1, source_target_pairs={{0,12},{1,13},{2,14},{3,15},{4,8},{5,9},{6,10},{7,11},{8,4},{9,5},... | collective-permute-start | bytes 49160 | tf_op jit(solution)/shard_map/ppermute | solution.py:310
  48.8 5.0 %collective-permute-start.10 = (f32[32,128]{1,0:T(8,128)S(1)}, f32[32,128]{1,0:T(8,128)S(1)}, u32[]{:S(2)}, u32[]{:S(2)}) collective-permute-start(f32[32,128]{1,0:T(8,128)S(1)} %add_add_fusion.1), channel_id=1, source_target_pairs={{0,8},{1,9},{2,10},{3,11},{4,12},{5,13},{6,14},{7,15},{8,0},{9,1},... | collective-permute-start | bytes 49160 | tf_op jit(solution)/shard_map/ppermute | solution.py:310
  52.0 1.8 %collective-permute-start.9 = (f32[32,128]{1,0:T(8,128)S(1)}, f32[32,128]{1,0:T(8,128)S(1)}, u32[]{:S(2)}, u32[]{:S(2)}) collective-permute-start(f32[32,128]{1,0:T(8,128)S(1)} %add_add_fusion.1), channel_id=1, source_target_pairs={{0,4},{1,5},{2,6},{3,7},{4,0},{5,1},{6,2},{7,3},{8,12},{9,13},{10,... | collective-permute-start | bytes 49160 | tf_op jit(solution)/shard_map/ppermute | solution.py:310
  53.8 5.3 %collective-permute-start.12 = (f32[32,128]{1,0:T(8,128)S(1)}, f32[32,128]{1,0:T(8,128)S(1)}, u32[]{:S(2)}, u32[]{:S(2)}) collective-permute-start(f32[32,128]{1,0:T(8,128)S(1)} %add_add_fusion), channel_id=1, source_target_pairs={{0,24},{1,25},{2,26},{3,27},{4,28},{5,29},{6,30},{7,31},{8,16},{9,... | collective-permute-start | bytes 49160 | tf_op jit(solution)/shard_map/ppermute | solution.py:310
  59.1 7.7 %collective-permute-start.13 = (f32[32,128]{1,0:T(8,128)S(1)}, f32[32,128]{1,0:T(8,128)S(1)}, u32[]{:S(2)}, u32[]{:S(2)}) collective-permute-start(f32[32,128]{1,0:T(8,128)S(1)} %add.36), channel_id=1, source_target_pairs={{0,32},{1,33},{2,34},{3,35},{4,36},{5,37},{6,38},{7,39},{8,40},{9,... | collective-permute-start | bytes 49160 | tf_op jit(solution)/shard_map/ppermute | solution.py:310
  66.8 8.6 %collective-permute-start.14 = (f32[32,128]{1,0:T(8,128)S(1)}, f32[32,128]{1,0:T(8,128)S(1)}, u32[]{:S(2)}, u32[]{:S(2)}) collective-permute-start(f32[32,128]{1,0:T(8,128)S(1)} %add.37), channel_id=1, source_target_pairs={{0,224},{1,225},{2,226},{3,227},{4,228},{5,229},{6,230},{7,231},{8... | collective-permute-start | bytes 49160 | tf_op jit(solution)/shard_map/ppermute | solution.py:310
  75.4 5.8 %collective-permute-start.15 = (f32[32,128]{1,0:T(8,128)S(1)}, f32[32,128]{1,0:T(8,128)S(1)}, u32[]{:S(2)}, u32[]{:S(2)}) collective-permute-start(f32[32,128]{1,0:T(8,128)S(1)} %add.38), channel_id=1, source_target_pairs={{0,96},{1,97},{2,98},{3,99},{4,100},{5,101},{6,102},{7,103},{8,104... | collective-permute-start | bytes 49160 | tf_op jit(solution)/shard_map/ppermute | solution.py:310

commit v3 on v2

--- a/solution.py
+++ b/solution.py
@@ -237,7 +237,7 @@
         partial[i] = own_noise[i] * image[i] * 256.0 + single[i] + 2.0 * double[i]
 
 
-def outside(from_row, from_column, from_corner, upper, tiles_here, tiles_up, before, image, products, system):
+def outside(from_row, from_column, from_corner, upper, tiles_here, tiles_up, before, image, products, copies):
     sources = {4: (from_column, 0), 5: (from_column, 1), 6: (from_row, 0), 7: (from_row, 1), 8: (from_corner, 0)}
     border = {j: ref[place] for j, (ref, place) in sources.items()}
     partial = [before[i] for i in range(4)]
@@ -253,19 +253,30 @@
         side_by_side([partial[i] + 2.0 * double[i] for i in range(4)] + [2.0 * raised[i] for i in range(4)]),
     ) * (1.0 / 256.0)
     known = products[...]
-    second, mixed = known[0:16, 0:16], known[0:16, 16:32]
-    crossed, start = known[16:32, 0:16], known[16:32, 16:32]
-    top = jnp.concatenate([crossed, second, start, jnp.zeros((RHS, 80), f32)], axis=1)
-    bottom = jnp.concatenate([second, third, mixed, jnp.zeros((RHS, 80), f32)], axis=1)
-    system[...] = jnp.concatenate([top, bottom], axis=0)
-
-
-def conclude(system, own_sides, image, result):
-    value = system[...]
-    lanes = lax.broadcasted_iota(jnp.int32, (32, 128), 1)
+    ordered = jnp.concatenate(
+        [known[16:32, 16:32], known[16:32, 0:16], known[0:16, 0:16], third], axis=1
+    )
+    packed = jnp.concatenate([ordered[0:8], ordered[8:16]], axis=1)
+    copies[...] = jnp.broadcast_to(packed[None], copies.shape)
+
+
+def add_up(arrived, copies):
+    copies[...] = jnp.broadcast_to(jnp.sum(arrived[...], axis=0, keepdims=True), copies.shape)
+
+
+def conclude(arrived, own_sides, image, result):
+    packed = jnp.sum(arrived[...], axis=0)
+    ordered = jnp.concatenate([packed[:, 0:64], packed[:, 64:128]], axis=0)
+    start, first, second, third = (ordered[:, 16 * part:16 * part + 16] for part in range(4))
+    square = jnp.concatenate(
+        [jnp.concatenate([first, second], axis=1), jnp.concatenate([second, third], axis=1)], axis=0
+    )
+    square = jnp.concatenate([square, jnp.zeros((32, 96), f32)], axis=1)
+    flipped = jnp.transpose(jnp.concatenate([square, jnp.zeros((96, 128), f32)], axis=0))[0:32]
+    square = 0.5 * (square + flipped)
+    known = jnp.concatenate([start, square[0:16, 0:16]], axis=0)
+    value = jnp.concatenate([square[:, 0:32], known, jnp.zeros((32, 80), f32)], axis=1)
     rows = lax.broadcasted_iota(jnp.int32, (32, 128), 0)
-    flipped = jnp.transpose(jnp.concatenate([value, jnp.zeros((96, 128), f32)], axis=0))[0:32]
-    value = jnp.where(lanes < 32, 0.5 * (value + flipped), value)
     for k in range(0, 32, 2):
         first_column = jnp.broadcast_to(value[:, k:k + 1], value.shape)
         second_column = jnp.broadcast_to(value[:, k + 1:k + 2], value.shape)
@@ -301,16 +312,16 @@
     def from_member(value, mask):
         return lax.ppermute(value, "sub", [(source, source ^ mask) for source in range(members)])
 
-    def sum_over_all(value):
-        rounds = [[lambda p, m=m: p ^ m for m in masks] for masks in ((1, 2, 3), (4, 8, 12), (24,))]
-        for order in ((1, 0, 3, 2, 5, 4, 7, 6), (7, 2, 1, 4, 3, 6, 5, 0), (3, 6, 5, 0, 7, 2, 1, 4)):
-            rounds.append([lambda p, order=order: p % 32 + 32 * order[p // 32]])
-        for partners in rounds:
-            value = value + sum(
-                lax.ppermute(value, ("region", "sub"), [(p, partner(p)) for p in range(everyone)])
-                for partner in partners
-            )
-        return value
+    def swap(copies, stride):
+        size = copies.shape[0]
+        groups = [
+            [first + stride * place for place in range(size)]
+            for first in range(everyone)
+            if first // stride % size == 0
+        ]
+        return lax.all_to_all(
+            copies, ("region", "sub"), 0, 0, axis_index_groups=groups, tiled=True
+        )
 
     def shape(*dims, dtype=f32):
         return jax.ShapeDtypeStruct(dims, dtype)
@@ -358,14 +369,17 @@
         inside, "inside", (shape(32, 32), shape(*field)),
         (own_sides, image, rounded, own_noise, tiles_here), 10 * 2 * tile_flops,
     )
-    system = call(
-        outside, "outside", shape(32, 128),
+    plane = 8 * members
+    copies = call(
+        outside, "outside", shape(plane, 8, 128),
         (from_row, from_column, from_corner, upper, tiles_here, tiles_up, partial, image, products),
         34 * 2 * tile_flops,
     )
-    system = sum_over_all(system)
+    arrived = swap(copies, 1)
+    copies = call(add_up, "add_up", shape(everyone // plane, 8, 128), (arrived,), 1024)
+    arrived = swap(copies, plane)
     return call(
-        conclude, "conclude", shape(*field), (system, own_sides, image), tile_flops,
+        conclude, "conclude", shape(*field), (arrived, own_sides, image), tile_flops,
     )
 
 

time: 84 us -> 79.5 us (0.946); the launches traced: 83.8 us -> 78.4 us
  blocking collectives: 0 us -> 33.6 us
  starting transfers between devices: 36 us -> 9.96 us
  waiting for transfers between devices: 16.1 us -> 2.91 us
    all_to_all x0 -> x2, blocking collectives: none -> 33.6 us  [swap(): lax.all_to_all(copies, ('region', 'sub'), 0, 0, axis_index_groups=groups,...]
    ppermute x10 -> x0, starting transfers between devices: 26 us -> none  [sum_over_all(): lax.ppermute(value, ('region', 'sub'), [(p, partner(p)) for p in range(ev...]
    ppermute x10 -> x0, waiting for transfers between devices: 13.2 us -> none  [sum_over_all(): lax.ppermute(value, ('region', 'sub'), [(p, partner(p)) for p in range(ev...]
    pallas_call x8 -> x9, Pallas kernels: 31.6 us -> 31.8 us  [call(): pl.pallas_call(kernel, name=name, out_shape=out_shape, in_specs=[pl.Block...]
  transfers between devices with their start and end apart: 16 -> 6, of which waited for: 9 -> 2; matrix products, arithmetic and copies ran while one was open for 0% -> 0% of each run, Pallas kernels for 16% -> 17%
where the time goes in v3:
time: 79.5 us; the launch traced here: 78.4 us
  blocking collectives  33.6 us (42%)
  Pallas kernels  31.8 us (40%)
  starting transfers between devices  9.96 us (13%)
  waiting for transfers between devices  2.91 us (4%)
    all_to_all x2, blocking collectives, swap(): lax.all_to_all(copies, ('region', 'sub'), 0, 0, axis_index_groups=groups,...  33.6 us
    pallas_call x9, Pallas kernels, call(): pl.pallas_call(kernel, name=name, out_shape=out_shape, in_specs=[pl.Block...  31.8 us
    ppermute x3, starting transfers between devices, from_region(): return lax.ppermute(value, 'region', pairs)  5.61 us
    ppermute x3, starting transfers between devices, from_member(): lax.ppermute(value, 'sub', [(source, source ^ mask) for source in range(m...  4.34 us
    ppermute x3, waiting for transfers between devices, from_member(): lax.ppermute(value, 'sub', [(source, source ^ mask) for source in range(m...  2.9 us
  transfers between devices with their start and end apart: 6, of which 2 were waited for; matrix products, arithmetic and copies ran while one was open for 0% of the time, Pallas kernels for 17%

profile of v3, /device:TPU:8, one launch (start us, length us, event | category | flops | bytes accessed | tf_op | source)
XLA Modules:
  0.0 78.4 jit_solution(5978870772386374615)
XLA Ops:
  0.0 1.6 %prepare.1 = (bf16[9,32,512]{2,1,0:T(8,128)(2,1)S(1)}, bf16[9,512,64]{2,1,0:T(8,128)(2,1)S(1)}, bf16[4,64,512]{2,1,0:T(8,128)(2,1)S(1)}, f32[4,16,512]{2,1,0:T(8,128)S(1)}, f32[4,1,512]{2,1,0:T(1,128)S(1)}) custom-call(f32[3,16,512]{2,1,0:T(8,128)} %points_far.1, f32[16,512]{1,0:T(8,128)} %noise_far.1, f32[16,16,512]{2,1,0:T(8,128)} %sides_far.1), custom_call_target="tpu_custom_call" | custom-call | flops 134217728 | bytes 1048576 | tf_op jit(solution)/shard_map/prepare/pallas_call | solution.py:28
  1.6 1.3 %collective-permute-start = (bf16[9,32,512]{2,1,0:T(8,128)(2,1)S(1)}, bf16[9,32,512]{2,1,0:T(8,128)(2,1)S(1)}, u32[]{:S(2)}, u32[]{:S(2)}) collective-permute-start(bf16[9,32,512]{2,1,0:T(8,128)(2,1)S(1)} %get-tuple-element.20.sent), channel_id=1, source_target_pairs={{4,0},{8,4},{12,8},{16,12},{20,16},{24,20},{28,24},{32,28},{36,32}... | collective-permute-start | bytes 884744 | tf_op jit(solution)/shard_map/ppermute | solution.py:310
  2.9 8.1 %within_layer.1 = (f32[4,16,512]{2,1,0:T(8,128)S(1)}, bf16[19,512,512]{2,1,0:T(8,128)(2,1)S(1)}) custom-call(bf16[9,32,512]{2,1,0:T(8,128)(2,1)S(1)} %get-tuple-element.20.sent, bf16[9,512,64]{2,1,0:T(8,128)(2,1)S(1)} %get-tuple-element.21.left, bf16[4,64,512]{2,1,0:T(8,128)(2,1)S(1)} %get-tuple-element.19.right), custom_call_target="tpu_custom_call" | custom-call | flops 10200547328 | bytes 1048576 | tf_op jit(solution)/shard_map/within_layer/pallas_call | solution.py:28
  11.0 0.0 collective-permute-done.above
  11.0 11.1 %above_own.1 = (f32[4,16,512]{2,1,0:T(8,128)S(1)}, f32[4,16,512]{2,1,0:T(8,128)S(1)}, bf16[25,512,512]{2,1,0:T(8,128)(2,1)S(1)}) custom-call(bf16[9,32,512]{2,1,0:T(8,128)(2,1)S(1)} %get-tuple-element.20.sent, bf16[9,512,64]{2,1,0:T(8,128)(2,1)S(1)} %get-tuple-element.21.left, bf16[4,64,512]{2,1,0:T(8,128)(2,1)S(1)} %get-tuple-element.19.right, ...), custom_call_target="tpu_custom_call" | custom-call | flops 13421772800 | bytes 1048576 | tf_op jit(solution)/shard_map/above_own/pallas_call | solution.py:28
  22.1 3.0 %collective-permute-start.1 = (f32[4,16,512]{2,1,0:T(8,128)S(1)}, f32[4,16,512]{2,1,0:T(8,128)S(1)}, u32[]{:S(2)}, u32[]{:S(2)}) collective-permute-start(f32[4,16,512]{2,1,0:T(8,128)S(1)} %get-tuple-element.24), channel_id=1, source_target_pairs={{0,4},{4,8},{8,12},{12,16},{16,20},{20,24},{24,28},{28,32},{32,36}... | collective-permute-start | bytes 393224 | tf_op jit(solution)/shard_map/ppermute | solution.py:310
  25.1 4.0 %above_border.1.totals = f32[4,16,512]{2,1,0:T(8,128)S(1)} custom-call(bf16[4,64,512]{2,1,0:T(8,128)(2,1)S(1)} %get-tuple-element.19.right, bf16[9,32,512]{2,1,0:T(8,128)(2,1)S(1)} %collective-permute-done.above, f32[4,16,512]{2,1,0:T(8,128)S(1)} %get-tuple-element.23.before), custom_call_target="tpu_custom_call" | custom-call | flops 4831838208 | bytes 1048576 | tf_op jit(solution)/shard_map/above_border/pallas_call | solution.py:28
  29.1 0.0 collective-permute-done.1.arrived
  29.2 1.3 %collective-permute-start.5 = (bf16[4,16,512]{2,1,0:T(8,128)(2,1)S(1)}, bf16[4,16,512]{2,1,0:T(8,128)(2,1)S(1)}, u32[]{:S(2)}, u32[]{:S(2)}) collective-permute-start(bf16[4,16,512]{2,1,0:T(8,128)(2,1)S(1)} %get-tuple-element.27.rounded), channel_id=1, source_target_pairs={{4,0},{8,4},{12,8},{16,12},{20,16},{24,20},{28,24},{32,28},{36,32}... | collective-permute-start | bytes 196616 | tf_op jit(solution)/shard_map/ppermute | solution.py:310
  30.5 1.7 %collective-permute-start.4 = (bf16[1,16,512]{2,1,0:T(8,128)(2,1)S(1)}, bf16[1,16,512]{2,1,0:T(8,128)(2,1)S(1)}, u32[]{:S(2)}, u32[]{:S(2)}) collective-permute-start(bf16[1,16,512]{2,1,0:T(8,128)(2,1)S(1)} %slice.11), channel_id=1, source_target_pairs={{0,3},{1,2},{2,1},{3,0},{4,7},{5,6},{6,5},{7,4},{8,11},{9,10},{10,... | collective-permute-start | bytes 49160 | tf_op jit(solution)/shard_map/ppermute | solution.py:313
  32.2 2.7 %collective-permute-start.3 = (bf16[2,16,512]{2,1,0:T(8,128)(2,1)S(1)}, bf16[2,16,512]{2,1,0:T(8,128)(2,1)S(1)}, u32[]{:S(2)}, u32[]{:S(2)}) collective-permute-start(bf16[2,16,512]{2,1,0:T(8,128)(2,1)S(1)} %get-tuple-element.33), channel_id=1, source_target_pairs={{0,2},{1,3},{2,0},{3,1},{4,6},{5,7},{6,4},{7,5},{8,10},{9,11},{10,... | collective-permute-start | bytes 98312 | tf_op jit(solution)/shard_map/ppermute | solution.py:313
  34.8 0.0 collective-permute-start.2
  34.8 1.0 %inside.1 = (f32[32,32]{1,0:T(8,128)S(1)}, f32[4,16,512]{2,1,0:T(8,128)S(1)}) custom-call(f32[4,16,512]{2,1,0:T(8,128)S(1)} %get-tuple-element.26.own_sides, f32[4,16,512]{2,1,0:T(8,128)S(1)} %get-tuple-element.30.image, bf16[4,16,512]{2,1,0:T(8,128)(2,1)S(1)} %get-tuple-element.27.rounded, f32[4,1,512]{2,1,0:T(1,128)S(1)} %get-tuple-element.25.own_noise, ...), custom_call_target="tpu_custom_call" | custom-call | flops 2684354560 | bytes 1048576 | tf_op jit(solution)/shard_map/inside/pallas_call | solution.py:28
  35.8 0.0 collective-permute-done.4.from_corner
  35.9 1.7 %collective-permute-done.3.from_column = bf16[2,16,512]{2,1,0:T(8,128)(2,1)S(1)} collective-permute-done((bf16[2,16,512]{2,1,0:T(8,128)(2,1)S(1)}, bf16[2,16,512]{2,1,0:T(8,128)(2,1)S(1)}, u32[]{:S(2)}, u32[]{:S(2)}) %collective-permute-start.3) | collective-permute-done | bytes 32800 | tf_op jit(solution)/shard_map/ppermute | solution.py:313
  37.6 1.2 %collective-permute-done.2.from_row = bf16[2,16,512]{2,1,0:T(8,128)(2,1)S(1)} collective-permute-done((bf16[2,16,512]{2,1,0:T(8,128)(2,1)S(1)}, bf16[2,16,512]{2,1,0:T(8,128)(2,1)S(1)}, u32[]{:S(2)}, u32[]{:S(2)}) %collective-permute-start.2) | collective-permute-done | bytes 32800 | tf_op jit(solution)/shard_map/ppermute | solution.py:313
  38.8 0.0 collective-permute-done.5.upper
  38.8 3.2 %outside.1 = f32[32,8,128]{2,1,0:T(8,128)S(1)} custom-call(bf16[2,16,512]{2,1,0:T(8,128)(2,1)S(1)} %collective-permute-done.2.from_row, bf16[2,16,512]{2,1,0:T(8,128)(2,1)S(1)} %collective-permute-done.3.from_column, bf16[1,16,512]{2,1,0:T(8,128)(2,1)S(1)} %collective-permute-done.4.from_corner, bf16[4,16,512]{2,1,0:T(8,128)(2,1)S(1)} %collective-permute-done.5.upper, ...), custom_call_target="tpu_custom_call" | custom-call | flops 9126805504 | bytes 1048576 | tf_op jit(solution)/shard_map/outside/pallas_call | solution.py:28
  42.1 14.9 %all_to_all.10.arrived = f32[32,8,128]{2,1,0:T(8,128)S(1)} all-to-all(f32[32,8,128]{2,1,0:T(8,128)S(1)} %outside.1), channel_id=1, replica_groups={{0,1,2,3,4,5,6,7,8,9,10,11,12,13,14,15,16,17,18,19,20,21,22,23,24,25,26..., dimensions={0} | all-to-all | bytes 262144 | tf_op jit(solution)/shard_map/all_to_all | solution.py:322
  57.0 18.7 %all_to_all.11.arrived = f32[8,8,128]{2,1,0:T(8,128)S(1)} all-to-all(f32[8,8,128]{2,1,0:T(8,128)S(1)} %add_up.1), channel_id=1, replica_groups={{0,32,64,96,128,160,192,224},{1,33,65,97,129,161,193,225},{2,34,66,98,1..., dimensions={0} | all-to-all | bytes 65536 | tf_op jit(solution)/shard_map/all_to_all | solution.py:322
  75.7 2.7 %conclude.1 = f32[4,16,512]{2,1,0:T(8,128)} custom-call(f32[8,8,128]{2,1,0:T(8,128)S(1)} %all_to_all.11.arrived, f32[4,16,512]{2,1,0:T(8,128)S(1)} %get-tuple-element.26.own_sides, f32[4,16,512]{2,1,0:T(8,128)S(1)} %get-tuple-element.30.image), custom_call_target="tpu_custom_call" | custom-call | flops 134217728 | bytes 1048576 | tf_op jit(solution)/shard_map/conclude/pallas_call | solution.py:28
  (4 shorter events, 0.1 us)
Async XLA Ops:
  1.6 9.4 %collective-permute-start = (bf16[9,32,512]{2,1,0:T(8,128)(2,1)S(1)}, bf16[9,32,512]{2,1,0:T(8,128)(2,1)S(1)}, u32[]{:S(2)}, u32[]{:S(2)}) collective-permute-start(bf16[9,32,512]{2,1,0:T(8,128)(2,1)S(1)} %get-tuple-element.20.sent), channel_id=1, source_target_pairs={{4,0},{8,4},{12,8},{16,12},{20,16},{24,20},{28,24},{32,28},{36,32}... | collective-permute-start | bytes 884744 | tf_op jit(solution)/shard_map/ppermute | solution.py:310
  22.1 7.1 %collective-permute-start.1 = (f32[4,16,512]{2,1,0:T(8,128)S(1)}, f32[4,16,512]{2,1,0:T(8,128)S(1)}, u32[]{:S(2)}, u32[]{:S(2)}) collective-permute-start(f32[4,16,512]{2,1,0:T(8,128)S(1)} %get-tuple-element.24), channel_id=1, source_target_pairs={{0,4},{4,8},{8,12},{12,16},{16,20},{20,24},{24,28},{28,32},{32,36}... | collective-permute-start | bytes 393224 | tf_op jit(solution)/shard_map/ppermute | solution.py:310
  29.2 9.6 %collective-permute-start.5 = (bf16[4,16,512]{2,1,0:T(8,128)(2,1)S(1)}, bf16[4,16,512]{2,1,0:T(8,128)(2,1)S(1)}, u32[]{:S(2)}, u32[]{:S(2)}) collective-permute-start(bf16[4,16,512]{2,1,0:T(8,128)(2,1)S(1)} %get-tuple-element.27.rounded), channel_id=1, source_target_pairs={{4,0},{8,4},{12,8},{16,12},{20,16},{24,20},{28,24},{32,28},{36,32}... | collective-permute-start | bytes 196616 | tf_op jit(solution)/shard_map/ppermute | solution.py:310
  30.5 5.3 %collective-permute-start.4 = (bf16[1,16,512]{2,1,0:T(8,128)(2,1)S(1)}, bf16[1,16,512]{2,1,0:T(8,128)(2,1)S(1)}, u32[]{:S(2)}, u32[]{:S(2)}) collective-permute-start(bf16[1,16,512]{2,1,0:T(8,128)(2,1)S(1)} %slice.11), channel_id=1, source_target_pairs={{0,3},{1,2},{2,1},{3,0},{4,7},{5,6},{6,5},{7,4},{8,11},{9,10},{10,... | collective-permute-start | bytes 49160 | tf_op jit(solution)/shard_map/ppermute | solution.py:313
  32.2 5.4 %collective-permute-start.3 = (bf16[2,16,512]{2,1,0:T(8,128)(2,1)S(1)}, bf16[2,16,512]{2,1,0:T(8,128)(2,1)S(1)}, u32[]{:S(2)}, u32[]{:S(2)}) collective-permute-start(bf16[2,16,512]{2,1,0:T(8,128)(2,1)S(1)} %get-tuple-element.33), channel_id=1, source_target_pairs={{0,2},{1,3},{2,0},{3,1},{4,6},{5,7},{6,4},{7,5},{8,10},{9,11},{10,... | collective-permute-start | bytes 98312 | tf_op jit(solution)/shard_map/ppermute | solution.py:313
  34.8 3.9 %collective-permute-start.2 = (bf16[2,16,512]{2,1,0:T(8,128)(2,1)S(1)}, bf16[2,16,512]{2,1,0:T(8,128)(2,1)S(1)}, u32[]{:S(2)}, u32[]{:S(2)}) collective-permute-start(bf16[2,16,512]{2,1,0:T(8,128)(2,1)S(1)} %get-tuple-element.34), channel_id=1, source_target_pairs={{0,1},{1,0},{2,3},{3,2},{4,5},{5,4},{6,7},{7,6},{8,9},{9,8},{10,11... | collective-permute-start | bytes 98312 | tf_op jit(solution)/shard_map/ppermute | solution.py:313

commit v4 on v3

--- a/solution.py
+++ b/solution.py
@@ -17,6 +17,8 @@
     for i in range(4)
     if max(abs(OWN[i][0] - WINDOW[j][0]), abs(OWN[i][1] - WINDOW[j][1])) <= 1
 )
+EARLY = SELF + PAIRED + CROSS[:2]
+LATE = CROSS[2:]
 BLOCK = 512
 RHS = 16
 FEATURES = 64
@@ -72,8 +74,7 @@
     ]
     for copy in copies:
         copy.start()
-    for copy in copies:
-        copy.wait()
+    copies[0].wait()
     region = lax.axis_index("region")
     member = lax.axis_index("sub")
     row_half, column_half = member & 1, member >> 1
@@ -83,6 +84,7 @@
         row_half.astype(f32) + 1.5,
         column_half.astype(f32) + 1.5,
     )
+    blocks = []
     for index, (row, column) in enumerate(WINDOW):
         row = jnp.where(row_half == 1, 3 - row, row)
         column = jnp.where(column_half == 1, 3 - column, column)
@@ -91,8 +93,7 @@
         for axis in range(3):
             line = points[axis, pl.ds(block, 1), :] - centers[axis]
             place = jnp.where(rows == axis, jnp.broadcast_to(line, place.shape), place)
-        side = right_sides[block]
-        sent[index, 0:16, :] = side.astype(bf16)
+        blocks.append(block)
         high, middle, low = split(place)
         sent[index, 16:32, :] = jnp.concatenate(
             [high + pltpu.roll(low, 3, 0), middle], axis=0
@@ -101,6 +102,12 @@
         left[index] = jnp.transpose(left_rows).astype(bf16)
         if index < 4:
             right[index] = right_rows.astype(bf16)
+    copies[1].wait()
+    copies[2].wait()
+    for index, block in enumerate(blocks):
+        side = right_sides[block]
+        sent[index, 0:16, :] = side.astype(bf16)
+        if index < 4:
             own_sides[index] = side
             own_noise[index] = noise_var[pl.ds(block, 1), :]
 
@@ -145,7 +152,7 @@
 
 def within_layer(sent, left, right, totals, tiles, *buffers):
     totals[...] = jnp.zeros_like(totals)
-    pairs = SELF + PAIRED + CROSS
+    pairs = EARLY
 
     def use(step, tile):
         i, j = pairs[step]
@@ -188,7 +195,7 @@
     )
 
 
-def above_border(right, above, before, totals, left_above, *buffers):
+def borders(sent, left, right, above, before, totals, tiles, left_above, *buffers):
     totals[...] = before[...]
     for j in range(5):
         left_above[j] = jnp.transpose(
@@ -196,12 +203,17 @@
         ).astype(bf16)
 
     def use(step, tile):
-        i, j = CROSS[step]
-        totals[i] += times(above[j, 0:16, :], tile)
+        if step < len(LATE):
+            i, j = LATE[step]
+            tiles[step] = tile
+            totals[i] += times(sent[j, 0:16, :], tile)
+        else:
+            i, j = CROSS[step - len(LATE)]
+            totals[i] += times(above[j, 0:16, :], tile)
 
     sweep(
-        [lambda j=j: left_above[j - 4] for i, j in CROSS],
-        [lambda i=i: right[i] for i, j in CROSS],
+        [lambda j=j: left[j] for i, j in LATE] + [lambda j=j: left_above[j - 4] for i, j in CROSS],
+        [lambda i=i: right[i] for i, j in LATE + CROSS],
         buffers, use,
     )
 
@@ -237,20 +249,27 @@
         partial[i] = own_noise[i] * image[i] * 256.0 + single[i] + 2.0 * double[i]
 
 
-def outside(from_row, from_column, from_corner, upper, tiles_here, tiles_up, before, image, products, copies):
+def upward(upper, tiles, before, partial):
+    double = [jnp.zeros((RHS, BLOCK), f32)] * 4
+    for step in range(16):
+        double[step % 4] += times(upper[step // 4], tiles[step])
+    for i in range(4):
+        partial[i] = before[i] + 2.0 * double[i]
+
+
+def outside(from_row, from_column, from_corner, upper, tiles_early, tiles_late, tiles_up, before, image, products, copies):
     sources = {4: (from_column, 0), 5: (from_column, 1), 6: (from_row, 0), 7: (from_row, 1), 8: (from_corner, 0)}
     border = {j: ref[place] for j, (ref, place) in sources.items()}
-    partial = [before[i] for i in range(4)]
-    double = [jnp.zeros((RHS, BLOCK), f32)] * 4
+    single = [jnp.zeros((RHS, BLOCK), f32)] * 4
     raised = [jnp.zeros((RHS, BLOCK), f32)] * 4
-    for step in range(16):
-        double[step % 4] += times(upper[step // 4], tiles_up[step])
+    first = len(CROSS) - len(LATE)
     for step, (i, j) in enumerate(CROSS):
-        partial[i] += times(border[j], tiles_here[10 + step])
+        tile = tiles_early[10 + step] if step < first else tiles_late[step - first]
+        single[i] += times(border[j], tile)
         raised[i] += times(border[j], tiles_up[16 + step])
     third = gram(
         side_by_side([image[i] for i in range(4)] + [upper[i].astype(f32) for i in range(4)]),
-        side_by_side([partial[i] + 2.0 * double[i] for i in range(4)] + [2.0 * raised[i] for i in range(4)]),
+        side_by_side([before[i] + single[i] for i in range(4)] + [2.0 * raised[i] for i in range(4)]),
     ) * (1.0 / 256.0)
     known = products[...]
     ordered = jnp.concatenate(
@@ -343,9 +362,9 @@
         pltpu.HBM,
     )
     above = from_region(sent, 1)
-    totals, tiles_here = call(
-        within_layer, "within_layer", (shape(*field), held(19, BLOCK, BLOCK)),
-        (sent, left, right), 19 * 4 * tile_flops, buffers,
+    totals, tiles_early = call(
+        within_layer, "within_layer", (shape(*field), held(len(EARLY), BLOCK, BLOCK)),
+        (sent, left, right), len(EARLY) * 4 * tile_flops, buffers,
     )
     totals, passed, tiles_up = call(
         above_own, "above_own", (shape(*field), shape(*field), held(25, BLOCK, BLOCK)),
@@ -353,8 +372,9 @@
         [pltpu.VMEM((4, BLOCK, FEATURES), bf16), pltpu.VMEM((4, FEATURES, BLOCK), bf16)] + buffers,
     )
     arrived = from_region(passed, -1)
-    totals = call(
-        above_border, "above_border", shape(*field), (right, above, totals), 9 * 4 * tile_flops,
+    totals, tiles_late = call(
+        borders, "borders", (shape(*field), held(len(LATE), BLOCK, BLOCK)),
+        (sent, left, right, above, totals), 16 * 4 * tile_flops,
         [pltpu.VMEM((5, BLOCK, FEATURES), bf16)] + buffers,
     )
     image, rounded = call(
@@ -367,13 +387,17 @@
     from_corner = from_member(rounded[3:4], 3)
     products, partial = call(
         inside, "inside", (shape(32, 32), shape(*field)),
-        (own_sides, image, rounded, own_noise, tiles_here), 10 * 2 * tile_flops,
+        (own_sides, image, rounded, own_noise, tiles_early), 10 * 2 * tile_flops,
+    )
+    partial = call(
+        upward, "upward", shape(*field), (upper, tiles_up, partial), 16 * 2 * tile_flops,
     )
     plane = 8 * members
     copies = call(
         outside, "outside", shape(plane, 8, 128),
-        (from_row, from_column, from_corner, upper, tiles_here, tiles_up, partial, image, products),
-        34 * 2 * tile_flops,
+        (from_row, from_column, from_corner, upper, tiles_early, tiles_late, tiles_up, partial,
+         image, products),
+        18 * 2 * tile_flops,
     )
     arrived = swap(copies, 1)
     copies = call(add_up, "add_up", shape(everyone // plane, 8, 128), (arrived,), 1024)

time: 79.5 us -> 78.1 us (0.982)
  waiting for transfers between devices: 2.91 us -> 1.72 us
    ppermute x3, waiting for transfers between devices: 2.9 us -> 1.71 us  [from_member(): lax.ppermute(value, 'sub', [(source, source ^ mask) for source in range(m...]
    pallas_call x9 -> x10, Pallas kernels: 31.8 us -> 31.7 us  [call(): pl.pallas_call(kernel, name=name, out_shape=out_shape, in_specs=[pl.Block...]
  transfers between devices with their start and end apart: 6 -> 6, of which waited for: 2 -> 2; matrix products, arithmetic and copies ran while one was open for 0% -> 0% of each run, Pallas kernels for 17% -> 19%
where the time goes in v4:
time: 78.1 us; the launch traced here: 77.1 us
  blocking collectives  33.6 us (43%)
  Pallas kernels  31.7 us (41%)
  starting transfers between devices  9.95 us (13%)
  waiting for transfers between devices  1.72 us (2%)
    all_to_all x2, blocking collectives, swap(): lax.all_to_all(copies, ('region', 'sub'), 0, 0, axis_index_groups=groups,...  33.6 us
    pallas_call x10, Pallas kernels, call(): pl.pallas_call(kernel, name=name, out_shape=out_shape, in_specs=[pl.Block...  31.7 us
    ppermute x3, starting transfers between devices, from_region(): return lax.ppermute(value, 'region', pairs)  5.77 us
    ppermute x3, starting transfers between devices, from_member(): lax.ppermute(value, 'sub', [(source, source ^ mask) for source in range(m...  4.18 us
    ppermute x3, waiting for transfers between devices, from_member(): lax.ppermute(value, 'sub', [(source, source ^ mask) for source in range(m...  1.71 us
  transfers between devices with their start and end apart: 6, of which 2 were waited for; matrix products, arithmetic and copies ran while one was open for 0% of the time, Pallas kernels for 19%

profile of v4, /device:TPU:8, one launch (start us, length us, event | category | flops | bytes accessed | tf_op | source)
XLA Modules:
  0.0 77.1 jit_solution(13067008310408405283)
XLA Ops:
  0.0 1.4 %prepare.1 = (bf16[9,32,512]{2,1,0:T(8,128)(2,1)S(1)}, bf16[9,512,64]{2,1,0:T(8,128)(2,1)S(1)}, bf16[4,64,512]{2,1,0:T(8,128)(2,1)S(1)}, f32[4,16,512]{2,1,0:T(8,128)S(1)}, f32[4,1,512]{2,1,0:T(1,128)S(1)}) custom-call(f32[3,16,512]{2,1,0:T(8,128)} %points_far.1, f32[16,512]{1,0:T(8,128)} %noise_far.1, f32[16,16,512]{2,1,0:T(8,128)} %sides_far.1), custom_call_target="tpu_custom_call" | custom-call | flops 134217728 | bytes 1048576 | tf_op jit(solution)/shard_map/prepare/pallas_call | solution.py:30
  1.4 1.3 %collective-permute-start = (bf16[9,32,512]{2,1,0:T(8,128)(2,1)S(1)}, bf16[9,32,512]{2,1,0:T(8,128)(2,1)S(1)}, u32[]{:S(2)}, u32[]{:S(2)}) collective-permute-start(bf16[9,32,512]{2,1,0:T(8,128)(2,1)S(1)} %get-tuple-element.21.sent), channel_id=1, source_target_pairs={{4,0},{8,4},{12,8},{16,12},{20,16},{24,20},{28,24},{32,28},{36,32}... | collective-permute-start | bytes 884744 | tf_op jit(solution)/shard_map/ppermute | solution.py:329
  2.7 5.3 %within_layer.1 = (f32[4,16,512]{2,1,0:T(8,128)S(1)}, bf16[12,512,512]{2,1,0:T(8,128)(2,1)S(1)}) custom-call(bf16[9,32,512]{2,1,0:T(8,128)(2,1)S(1)} %get-tuple-element.21.sent, bf16[9,512,64]{2,1,0:T(8,128)(2,1)S(1)} %get-tuple-element.22.left, bf16[4,64,512]{2,1,0:T(8,128)(2,1)S(1)} %get-tuple-element.23.right), custom_call_target="tpu_custom_call" | custom-call | flops 6442450944 | bytes 1048576 | tf_op jit(solution)/shard_map/within_layer/pallas_call | solution.py:30
  8.0 0.0 collective-permute-done.above
  8.0 11.1 %above_own.1 = (f32[4,16,512]{2,1,0:T(8,128)S(1)}, f32[4,16,512]{2,1,0:T(8,128)S(1)}, bf16[25,512,512]{2,1,0:T(8,128)(2,1)S(1)}) custom-call(bf16[9,32,512]{2,1,0:T(8,128)(2,1)S(1)} %get-tuple-element.21.sent, bf16[9,512,64]{2,1,0:T(8,128)(2,1)S(1)} %get-tuple-element.22.left, bf16[4,64,512]{2,1,0:T(8,128)(2,1)S(1)} %get-tuple-element.23.right, ...), custom_call_target="tpu_custom_call" | custom-call | flops 13421772800 | bytes 1048576 | tf_op jit(solution)/shard_map/above_own/pallas_call | solution.py:30
  19.1 3.2 %collective-permute-start.1 = (f32[4,16,512]{2,1,0:T(8,128)S(1)}, f32[4,16,512]{2,1,0:T(8,128)S(1)}, u32[]{:S(2)}, u32[]{:S(2)}) collective-permute-start(f32[4,16,512]{2,1,0:T(8,128)S(1)} %get-tuple-element.27), channel_id=1, source_target_pairs={{0,4},{4,8},{8,12},{12,16},{16,20},{20,24},{24,28},{28,32},{32,36}... | collective-permute-start | bytes 393224 | tf_op jit(solution)/shard_map/ppermute | solution.py:329
  22.3 6.8 %borders.1 = (f32[4,16,512]{2,1,0:T(8,128)S(1)}, bf16[7,512,512]{2,1,0:T(8,128)(2,1)S(1)}) custom-call(bf16[9,32,512]{2,1,0:T(8,128)(2,1)S(1)} %get-tuple-element.21.sent, bf16[9,512,64]{2,1,0:T(8,128)(2,1)S(1)} %get-tuple-element.22.left, bf16[4,64,512]{2,1,0:T(8,128)(2,1)S(1)} %get-tuple-element.23.right, ...), custom_call_target="tpu_custom_call" | custom-call | flops 8589934592 | bytes 1048576 | tf_op jit(solution)/shard_map/borders/pallas_call | solution.py:30
  29.1 0.0 collective-permute-done.1.arrived
  29.1 1.3 %collective-permute-start.5 = (bf16[4,16,512]{2,1,0:T(8,128)(2,1)S(1)}, bf16[4,16,512]{2,1,0:T(8,128)(2,1)S(1)}, u32[]{:S(2)}, u32[]{:S(2)}) collective-permute-start(bf16[4,16,512]{2,1,0:T(8,128)(2,1)S(1)} %get-tuple-element.30.rounded), channel_id=1, source_target_pairs={{4,0},{8,4},{12,8},{16,12},{20,16},{24,20},{28,24},{32,28},{36,32}... | collective-permute-start | bytes 196616 | tf_op jit(solution)/shard_map/ppermute | solution.py:329
  30.4 1.7 %collective-permute-start.4 = (bf16[1,16,512]{2,1,0:T(8,128)(2,1)S(1)}, bf16[1,16,512]{2,1,0:T(8,128)(2,1)S(1)}, u32[]{:S(2)}, u32[]{:S(2)}) collective-permute-start(bf16[1,16,512]{2,1,0:T(8,128)(2,1)S(1)} %slice.11), channel_id=1, source_target_pairs={{0,3},{1,2},{2,1},{3,0},{4,7},{5,6},{6,5},{7,4},{8,11},{9,10},{10,... | collective-permute-start | bytes 49160 | tf_op jit(solution)/shard_map/ppermute | solution.py:332
  32.1 2.5 %collective-permute-start.3 = (bf16[2,16,512]{2,1,0:T(8,128)(2,1)S(1)}, bf16[2,16,512]{2,1,0:T(8,128)(2,1)S(1)}, u32[]{:S(2)}, u32[]{:S(2)}) collective-permute-start(bf16[2,16,512]{2,1,0:T(8,128)(2,1)S(1)} %get-tuple-element.37), channel_id=1, source_target_pairs={{0,2},{1,3},{2,0},{3,1},{4,6},{5,7},{6,4},{7,5},{8,10},{9,11},{10,... | collective-permute-start | bytes 98312 | tf_op jit(solution)/shard_map/ppermute | solution.py:332
  34.6 0.0 collective-permute-start.2
  34.6 1.0 %inside.1 = (f32[32,32]{1,0:T(8,128)S(1)}, f32[4,16,512]{2,1,0:T(8,128)S(1)}) custom-call(f32[4,16,512]{2,1,0:T(8,128)S(1)} %get-tuple-element.29.own_sides, f32[4,16,512]{2,1,0:T(8,128)S(1)} %get-tuple-element.34.image, bf16[4,16,512]{2,1,0:T(8,128)(2,1)S(1)} %get-tuple-element.30.rounded, f32[4,1,512]{2,1,0:T(1,128)S(1)} %get-tuple-element.28.own_noise, ...), custom_call_target="tpu_custom_call" | custom-call | flops 2684354560 | bytes 1048576 | tf_op jit(solution)/shard_map/inside/pallas_call | solution.py:30
  35.6 0.0 collective-permute-done.5.upper
  35.6 1.2 %upward.1.before = f32[4,16,512]{2,1,0:T(8,128)S(1)} custom-call(bf16[4,16,512]{2,1,0:T(8,128)(2,1)S(1)} %collective-permute-done.5.upper, bf16[25,512,512]{2,1,0:T(8,128)(2,1)S(1)} %get-tuple-element.33.tiles.tiles_up, f32[4,16,512]{2,1,0:T(8,128)S(1)} %get-tuple-element.35.before), custom_call_target="tpu_custom_call" | custom-call | flops 4294967296 | bytes 1048576 | tf_op jit(solution)/shard_map/upward/pallas_call | solution.py:30
  36.8 0.0 collective-permute-done.4.from_corner
  36.8 0.7 collective-permute-done.3.from_column
  37.5 1.0 %collective-permute-done.2.from_row = bf16[2,16,512]{2,1,0:T(8,128)(2,1)S(1)} collective-permute-done((bf16[2,16,512]{2,1,0:T(8,128)(2,1)S(1)}, bf16[2,16,512]{2,1,0:T(8,128)(2,1)S(1)}, u32[]{:S(2)}, u32[]{:S(2)}) %collective-permute-start.2) | collective-permute-done | bytes 32800 | tf_op jit(solution)/shard_map/ppermute | solution.py:332
  38.5 2.2 %outside.1 = f32[32,8,128]{2,1,0:T(8,128)S(1)} custom-call(bf16[2,16,512]{2,1,0:T(8,128)(2,1)S(1)} %collective-permute-done.2.from_row, bf16[2,16,512]{2,1,0:T(8,128)(2,1)S(1)} %collective-permute-done.3.from_column, bf16[1,16,512]{2,1,0:T(8,128)(2,1)S(1)} %collective-permute-done.4.from_corner, bf16[4,16,512]{2,1,0:T(8,128)(2,1)S(1)} %collective-permute-done.5.upper, ...), custom_call_target="tpu_custom_call" | custom-call | flops 4831838208 | bytes 1048576 | tf_op jit(solution)/shard_map/outside/pallas_call | solution.py:30
  40.7 15.6 %all_to_all.10.arrived = f32[32,8,128]{2,1,0:T(8,128)S(1)} all-to-all(f32[32,8,128]{2,1,0:T(8,128)S(1)} %outside.1), channel_id=1, replica_groups={{0,1,2,3,4,5,6,7,8,9,10,11,12,13,14,15,16,17,18,19,20,21,22,23,24,25,26..., dimensions={0} | all-to-all | bytes 262144 | tf_op jit(solution)/shard_map/all_to_all | solution.py:341
  56.4 18.0 %all_to_all.11.arrived = f32[8,8,128]{2,1,0:T(8,128)S(1)} all-to-all(f32[8,8,128]{2,1,0:T(8,128)S(1)} %add_up.1), channel_id=1, replica_groups={{0,32,64,96,128,160,192,224},{1,33,65,97,129,161,193,225},{2,34,66,98,1..., dimensions={0} | all-to-all | bytes 65536 | tf_op jit(solution)/shard_map/all_to_all | solution.py:341
  74.3 2.7 %conclude.1 = f32[4,16,512]{2,1,0:T(8,128)} custom-call(f32[8,8,128]{2,1,0:T(8,128)S(1)} %all_to_all.11.arrived, f32[4,16,512]{2,1,0:T(8,128)S(1)} %get-tuple-element.29.own_sides, f32[4,16,512]{2,1,0:T(8,128)S(1)} %get-tuple-element.34.image), custom_call_target="tpu_custom_call" | custom-call | flops 134217728 | bytes 1048576 | tf_op jit(solution)/shard_map/conclude/pallas_call | solution.py:30
  (4 shorter events, 0.1 us)
Async XLA Ops:
  1.4 6.6 %collective-permute-start = (bf16[9,32,512]{2,1,0:T(8,128)(2,1)S(1)}, bf16[9,32,512]{2,1,0:T(8,128)(2,1)S(1)}, u32[]{:S(2)}, u32[]{:S(2)}) collective-permute-start(bf16[9,32,512]{2,1,0:T(8,128)(2,1)S(1)} %get-tuple-element.21.sent), channel_id=1, source_target_pairs={{4,0},{8,4},{12,8},{16,12},{20,16},{24,20},{28,24},{32,28},{36,32}... | collective-permute-start | bytes 884744 | tf_op jit(solution)/shard_map/ppermute | solution.py:329
  19.1 10.0 %collective-permute-start.1 = (f32[4,16,512]{2,1,0:T(8,128)S(1)}, f32[4,16,512]{2,1,0:T(8,128)S(1)}, u32[]{:S(2)}, u32[]{:S(2)}) collective-permute-start(f32[4,16,512]{2,1,0:T(8,128)S(1)} %get-tuple-element.27), channel_id=1, source_target_pairs={{0,4},{4,8},{8,12},{12,16},{16,20},{20,24},{24,28},{28,32},{32,36}... | collective-permute-start | bytes 393224 | tf_op jit(solution)/shard_map/ppermute | solution.py:329
  29.1 6.5 %collective-permute-start.5 = (bf16[4,16,512]{2,1,0:T(8,128)(2,1)S(1)}, bf16[4,16,512]{2,1,0:T(8,128)(2,1)S(1)}, u32[]{:S(2)}, u32[]{:S(2)}) collective-permute-start(bf16[4,16,512]{2,1,0:T(8,128)(2,1)S(1)} %get-tuple-element.30.rounded), channel_id=1, source_target_pairs={{4,0},{8,4},{12,8},{16,12},{20,16},{24,20},{28,24},{32,28},{36,32}... | collective-permute-start | bytes 196616 | tf_op jit(solution)/shard_map/ppermute | solution.py:329
  30.4 6.4 %collective-permute-start.4 = (bf16[1,16,512]{2,1,0:T(8,128)(2,1)S(1)}, bf16[1,16,512]{2,1,0:T(8,128)(2,1)S(1)}, u32[]{:S(2)}, u32[]{:S(2)}) collective-permute-start(bf16[1,16,512]{2,1,0:T(8,128)(2,1)S(1)} %slice.11), channel_id=1, source_target_pairs={{0,3},{1,2},{2,1},{3,0},{4,7},{5,6},{6,5},{7,4},{8,11},{9,10},{10,... | collective-permute-start | bytes 49160 | tf_op jit(solution)/shard_map/ppermute | solution.py:332
  32.1 5.4 %collective-permute-start.3 = (bf16[2,16,512]{2,1,0:T(8,128)(2,1)S(1)}, bf16[2,16,512]{2,1,0:T(8,128)(2,1)S(1)}, u32[]{:S(2)}, u32[]{:S(2)}) collective-permute-start(bf16[2,16,512]{2,1,0:T(8,128)(2,1)S(1)} %get-tuple-element.37), channel_id=1, source_target_pairs={{0,2},{1,3},{2,0},{3,1},{4,6},{5,7},{6,4},{7,5},{8,10},{9,11},{10,... | collective-permute-start | bytes 98312 | tf_op jit(solution)/shard_map/ppermute | solution.py:332
  34.6 3.9 %collective-permute-start.2 = (bf16[2,16,512]{2,1,0:T(8,128)(2,1)S(1)}, bf16[2,16,512]{2,1,0:T(8,128)(2,1)S(1)}, u32[]{:S(2)}, u32[]{:S(2)}) collective-permute-start(bf16[2,16,512]{2,1,0:T(8,128)(2,1)S(1)} %get-tuple-element.38), channel_id=1, source_target_pairs={{0,1},{1,0},{2,3},{3,2},{4,5},{5,4},{6,7},{7,6},{8,9},{9,8},{10,11... | collective-permute-start | bytes 98312 | tf_op jit(solution)/shard_map/ppermute | solution.py:332

commit v5 on v4

--- a/solution.py
+++ b/solution.py
@@ -17,8 +17,8 @@
     for i in range(4)
     if max(abs(OWN[i][0] - WINDOW[j][0]), abs(OWN[i][1] - WINDOW[j][1])) <= 1
 )
-EARLY = SELF + PAIRED + CROSS[:2]
-LATE = CROSS[2:]
+EARLY = SELF + PAIRED + CROSS[:6]
+LATE = CROSS[6:]
 BLOCK = 512
 RHS = 16
 FEATURES = 64
@@ -168,7 +168,10 @@
     )
 
 
-def above_own(sent, left, right, above, before, totals, passed, tiles, left_above, right_above, *buffers):
+def above_own(
+    sent, left, right, above, before, totals, leaving, tiles,
+    left_above, right_above, passed, *buffers,
+):
     totals[...] = before[...]
     passed[...] = jnp.zeros_like(passed)
     for j in range(4):
@@ -193,6 +196,7 @@
         + [lambda j=j: right_above[j] for j, border in CROSS],
         buffers, use,
     )
+    leaving[...] = passed[...].astype(bf16)
 
 
 def borders(sent, left, right, above, before, totals, tiles, left_above, *buffers):
@@ -219,7 +223,7 @@
 
 
 def finish_image(totals, arrived, own_noise, own_sides, image, rounded):
-    value = (totals[...] + arrived[...]) * (1.0 / 256.0) + own_noise[...] * own_sides[...]
+    value = (totals[...] + arrived[...].astype(f32)) * (1.0 / 256.0) + own_noise[...] * own_sides[...]
     image[...] = value
     rounded[...] = value.astype(bf16)
 
@@ -367,9 +371,11 @@
         (sent, left, right), len(EARLY) * 4 * tile_flops, buffers,
     )
     totals, passed, tiles_up = call(
-        above_own, "above_own", (shape(*field), shape(*field), held(25, BLOCK, BLOCK)),
+        above_own, "above_own",
+        (shape(*field), shape(*field, dtype=bf16), held(25, BLOCK, BLOCK)),
         (sent, left, right, above, totals), 25 * 4 * tile_flops,
-        [pltpu.VMEM((4, BLOCK, FEATURES), bf16), pltpu.VMEM((4, FEATURES, BLOCK), bf16)] + buffers,
+        [pltpu.VMEM((4, BLOCK, FEATURES), bf16), pltpu.VMEM((4, FEATURES, BLOCK), bf16),
+         pltpu.VMEM(field, f32)] + buffers,
     )
     arrived = from_region(passed, -1)
     totals, tiles_late = call(

time: 78.1 us -> 78.1 us (level)
  no operation moved by 1% of the time
where the time goes in v5:
time: 78.1 us; the launch traced here: 77.1 us
  blocking collectives  33.5 us (43%)
  Pallas kernels  31.7 us (41%)
  starting transfers between devices  9.95 us (13%)
  waiting for transfers between devices  1.72 us (2%)
    all_to_all x2, blocking collectives, swap(): lax.all_to_all(copies, ('region', 'sub'), 0, 0, axis_index_groups=groups,...  33.5 us
    pallas_call x10, Pallas kernels, call(): pl.pallas_call(kernel, name=name, out_shape=out_shape, in_specs=[pl.Block...  31.7 us
    ppermute x3, starting transfers between devices, from_region(): return lax.ppermute(value, 'region', pairs)  5.61 us
    ppermute x3, starting transfers between devices, from_member(): lax.ppermute(value, 'sub', [(source, source ^ mask) for source in range(m...  4.34 us
    ppermute x3, waiting for transfers between devices, from_member(): lax.ppermute(value, 'sub', [(source, source ^ mask) for source in range(m...  1.71 us
  transfers between devices with their start and end apart: 6, of which 2 were waited for; matrix products, arithmetic and copies ran while one was open for 0% of the time, Pallas kernels for 19%

profile of v5, /device:TPU:8, one launch (start us, length us, event | category | flops | bytes accessed | tf_op | source)
XLA Modules:
  0.0 77.1 jit_solution(15314876484389512450)
XLA Ops:
  0.0 1.4 %prepare.1 = (bf16[9,32,512]{2,1,0:T(8,128)(2,1)S(1)}, bf16[9,512,64]{2,1,0:T(8,128)(2,1)S(1)}, bf16[4,64,512]{2,1,0:T(8,128)(2,1)S(1)}, f32[4,16,512]{2,1,0:T(8,128)S(1)}, f32[4,1,512]{2,1,0:T(1,128)S(1)}) custom-call(f32[3,16,512]{2,1,0:T(8,128)} %points_far.1, f32[16,512]{1,0:T(8,128)} %noise_far.1, f32[16,16,512]{2,1,0:T(8,128)} %sides_far.1), custom_call_target="tpu_custom_call" | custom-call | flops 134217728 | bytes 1048576 | tf_op jit(solution)/shard_map/prepare/pallas_call | solution.py:30
  1.4 1.3 %collective-permute-start = (bf16[9,32,512]{2,1,0:T(8,128)(2,1)S(1)}, bf16[9,32,512]{2,1,0:T(8,128)(2,1)S(1)}, u32[]{:S(2)}, u32[]{:S(2)}) collective-permute-start(bf16[9,32,512]{2,1,0:T(8,128)(2,1)S(1)} %get-tuple-element.21.sent), channel_id=1, source_target_pairs={{4,0},{8,4},{12,8},{16,12},{20,16},{24,20},{28,24},{32,28},{36,32}... | collective-permute-start | bytes 884744 | tf_op jit(solution)/shard_map/ppermute | solution.py:333
  2.7 6.9 %within_layer.1 = (f32[4,16,512]{2,1,0:T(8,128)S(1)}, bf16[16,512,512]{2,1,0:T(8,128)(2,1)S(1)}) custom-call(bf16[9,32,512]{2,1,0:T(8,128)(2,1)S(1)} %get-tuple-element.21.sent, bf16[9,512,64]{2,1,0:T(8,128)(2,1)S(1)} %get-tuple-element.22.left, bf16[4,64,512]{2,1,0:T(8,128)(2,1)S(1)} %get-tuple-element.23.right), custom_call_target="tpu_custom_call" | custom-call | flops 8589934592 | bytes 1048576 | tf_op jit(solution)/shard_map/within_layer/pallas_call | solution.py:30
  9.6 0.0 collective-permute-done.above
  9.6 11.1 %above_own.1 = (f32[4,16,512]{2,1,0:T(8,128)S(1)}, bf16[4,16,512]{2,1,0:T(8,128)(2,1)S(1)}, bf16[25,512,512]{2,1,0:T(8,128)(2,1)S(1)}) custom-call(bf16[9,32,512]{2,1,0:T(8,128)(2,1)S(1)} %get-tuple-element.21.sent, bf16[9,512,64]{2,1,0:T(8,128)(2,1)S(1)} %get-tuple-element.22.left, bf16[4,64,512]{2,1,0:T(8,128)(2,1)S(1)} %get-tuple-element.23.right, ...), custom_call_target="tpu_custom_call" | custom-call | flops 13421772800 | bytes 1048576 | tf_op jit(solution)/shard_map/above_own/pallas_call | solution.py:30
  20.7 3.0 %collective-permute-start.1 = (bf16[4,16,512]{2,1,0:T(8,128)(2,1)S(1)}, bf16[4,16,512]{2,1,0:T(8,128)(2,1)S(1)}, u32[]{:S(2)}, u32[]{:S(2)}) collective-permute-start(bf16[4,16,512]{2,1,0:T(8,128)(2,1)S(1)} %get-tuple-element.27), channel_id=1, source_target_pairs={{0,4},{4,8},{8,12},{12,16},{16,20},{20,24},{24,28},{28,32},{32,36}... | collective-permute-start | bytes 196616 | tf_op jit(solution)/shard_map/ppermute | solution.py:333
  23.7 5.2 %borders.1 = (f32[4,16,512]{2,1,0:T(8,128)S(1)}, bf16[3,512,512]{2,1,0:T(8,128)(2,1)S(1)}) custom-call(bf16[9,32,512]{2,1,0:T(8,128)(2,1)S(1)} %get-tuple-element.21.sent, bf16[9,512,64]{2,1,0:T(8,128)(2,1)S(1)} %get-tuple-element.22.left, bf16[4,64,512]{2,1,0:T(8,128)(2,1)S(1)} %get-tuple-element.23.right, ...), custom_call_target="tpu_custom_call" | custom-call | flops 8589934592 | bytes 1048576 | tf_op jit(solution)/shard_map/borders/pallas_call | solution.py:30
  28.9 0.0 collective-permute-done.1.arrived
  29.0 1.3 %collective-permute-start.5 = (bf16[4,16,512]{2,1,0:T(8,128)(2,1)S(1)}, bf16[4,16,512]{2,1,0:T(8,128)(2,1)S(1)}, u32[]{:S(2)}, u32[]{:S(2)}) collective-permute-start(bf16[4,16,512]{2,1,0:T(8,128)(2,1)S(1)} %get-tuple-element.30.rounded), channel_id=1, source_target_pairs={{4,0},{8,4},{12,8},{16,12},{20,16},{24,20},{28,24},{32,28},{36,32}... | collective-permute-start | bytes 196616 | tf_op jit(solution)/shard_map/ppermute | solution.py:333
  30.3 1.7 %collective-permute-start.4 = (bf16[1,16,512]{2,1,0:T(8,128)(2,1)S(1)}, bf16[1,16,512]{2,1,0:T(8,128)(2,1)S(1)}, u32[]{:S(2)}, u32[]{:S(2)}) collective-permute-start(bf16[1,16,512]{2,1,0:T(8,128)(2,1)S(1)} %slice.11), channel_id=1, source_target_pairs={{0,3},{1,2},{2,1},{3,0},{4,7},{5,6},{6,5},{7,4},{8,11},{9,10},{10,... | collective-permute-start | bytes 49160 | tf_op jit(solution)/shard_map/ppermute | solution.py:336
  31.9 2.7 %collective-permute-start.3 = (bf16[2,16,512]{2,1,0:T(8,128)(2,1)S(1)}, bf16[2,16,512]{2,1,0:T(8,128)(2,1)S(1)}, u32[]{:S(2)}, u32[]{:S(2)}) collective-permute-start(bf16[2,16,512]{2,1,0:T(8,128)(2,1)S(1)} %get-tuple-element.37), channel_id=1, source_target_pairs={{0,2},{1,3},{2,0},{3,1},{4,6},{5,7},{6,4},{7,5},{8,10},{9,11},{10,... | collective-permute-start | bytes 98312 | tf_op jit(solution)/shard_map/ppermute | solution.py:336
  34.6 0.0 collective-permute-start.2
  34.6 1.0 %inside.1 = (f32[32,32]{1,0:T(8,128)S(1)}, f32[4,16,512]{2,1,0:T(8,128)S(1)}) custom-call(f32[4,16,512]{2,1,0:T(8,128)S(1)} %get-tuple-element.29.own_sides, f32[4,16,512]{2,1,0:T(8,128)S(1)} %get-tuple-element.34.image, bf16[4,16,512]{2,1,0:T(8,128)(2,1)S(1)} %get-tuple-element.30.rounded, f32[4,1,512]{2,1,0:T(1,128)S(1)} %get-tuple-element.28.own_noise, ...), custom_call_target="tpu_custom_call" | custom-call | flops 2684354560 | bytes 1048576 | tf_op jit(solution)/shard_map/inside/pallas_call | solution.py:30
  35.6 0.0 collective-permute-done.5.upper
  35.6 1.2 %upward.1.before = f32[4,16,512]{2,1,0:T(8,128)S(1)} custom-call(bf16[4,16,512]{2,1,0:T(8,128)(2,1)S(1)} %collective-permute-done.5.upper, bf16[25,512,512]{2,1,0:T(8,128)(2,1)S(1)} %get-tuple-element.33.tiles.tiles_up, f32[4,16,512]{2,1,0:T(8,128)S(1)} %get-tuple-element.35.before), custom_call_target="tpu_custom_call" | custom-call | flops 4294967296 | bytes 1048576 | tf_op jit(solution)/shard_map/upward/pallas_call | solution.py:30
  36.8 0.0 collective-permute-done.4.from_corner
  36.8 0.5 collective-permute-done.3.from_column
  37.4 1.2 %collective-permute-done.2.from_row = bf16[2,16,512]{2,1,0:T(8,128)(2,1)S(1)} collective-permute-done((bf16[2,16,512]{2,1,0:T(8,128)(2,1)S(1)}, bf16[2,16,512]{2,1,0:T(8,128)(2,1)S(1)}, u32[]{:S(2)}, u32[]{:S(2)}) %collective-permute-start.2) | collective-permute-done | bytes 32800 | tf_op jit(solution)/shard_map/ppermute | solution.py:336
  38.5 2.2 %outside.1 = f32[32,8,128]{2,1,0:T(8,128)S(1)} custom-call(bf16[2,16,512]{2,1,0:T(8,128)(2,1)S(1)} %collective-permute-done.2.from_row, bf16[2,16,512]{2,1,0:T(8,128)(2,1)S(1)} %collective-permute-done.3.from_column, bf16[1,16,512]{2,1,0:T(8,128)(2,1)S(1)} %collective-permute-done.4.from_corner, bf16[4,16,512]{2,1,0:T(8,128)(2,1)S(1)} %collective-permute-done.5.upper, ...), custom_call_target="tpu_custom_call" | custom-call | flops 4831838208 | bytes 1048576 | tf_op jit(solution)/shard_map/outside/pallas_call | solution.py:30
  40.8 15.6 %all_to_all.10.arrived = f32[32,8,128]{2,1,0:T(8,128)S(1)} all-to-all(f32[32,8,128]{2,1,0:T(8,128)S(1)} %outside.1), channel_id=1, replica_groups={{0,1,2,3,4,5,6,7,8,9,10,11,12,13,14,15,16,17,18,19,20,21,22,23,24,25,26..., dimensions={0} | all-to-all | bytes 262144 | tf_op jit(solution)/shard_map/all_to_all | solution.py:345
  56.4 17.9 %all_to_all.11.arrived = f32[8,8,128]{2,1,0:T(8,128)S(1)} all-to-all(f32[8,8,128]{2,1,0:T(8,128)S(1)} %add_up.1), channel_id=1, replica_groups={{0,32,64,96,128,160,192,224},{1,33,65,97,129,161,193,225},{2,34,66,98,1..., dimensions={0} | all-to-all | bytes 65536 | tf_op jit(solution)/shard_map/all_to_all | solution.py:345
  74.3 2.7 %conclude.1 = f32[4,16,512]{2,1,0:T(8,128)} custom-call(f32[8,8,128]{2,1,0:T(8,128)S(1)} %all_to_all.11.arrived, f32[4,16,512]{2,1,0:T(8,128)S(1)} %get-tuple-element.29.own_sides, f32[4,16,512]{2,1,0:T(8,128)S(1)} %get-tuple-element.34.image), custom_call_target="tpu_custom_call" | custom-call | flops 134217728 | bytes 1048576 | tf_op jit(solution)/shard_map/conclude/pallas_call | solution.py:30
  (4 shorter events, 0.1 us)
Async XLA Ops:
  1.4 8.2 %collective-permute-start = (bf16[9,32,512]{2,1,0:T(8,128)(2,1)S(1)}, bf16[9,32,512]{2,1,0:T(8,128)(2,1)S(1)}, u32[]{:S(2)}, u32[]{:S(2)}) collective-permute-start(bf16[9,32,512]{2,1,0:T(8,128)(2,1)S(1)} %get-tuple-element.21.sent), channel_id=1, source_target_pairs={{4,0},{8,4},{12,8},{16,12},{20,16},{24,20},{28,24},{32,28},{36,32}... | collective-permute-start | bytes 884744 | tf_op jit(solution)/shard_map/ppermute | solution.py:333
  20.7 8.2 %collective-permute-start.1 = (bf16[4,16,512]{2,1,0:T(8,128)(2,1)S(1)}, bf16[4,16,512]{2,1,0:T(8,128)(2,1)S(1)}, u32[]{:S(2)}, u32[]{:S(2)}) collective-permute-start(bf16[4,16,512]{2,1,0:T(8,128)(2,1)S(1)} %get-tuple-element.27), channel_id=1, source_target_pairs={{0,4},{4,8},{8,12},{12,16},{16,20},{20,24},{24,28},{28,32},{32,36}... | collective-permute-start | bytes 196616 | tf_op jit(solution)/shard_map/ppermute | solution.py:333
  29.0 6.6 %collective-permute-start.5 = (bf16[4,16,512]{2,1,0:T(8,128)(2,1)S(1)}, bf16[4,16,512]{2,1,0:T(8,128)(2,1)S(1)}, u32[]{:S(2)}, u32[]{:S(2)}) collective-permute-start(bf16[4,16,512]{2,1,0:T(8,128)(2,1)S(1)} %get-tuple-element.30.rounded), channel_id=1, source_target_pairs={{4,0},{8,4},{12,8},{16,12},{20,16},{24,20},{28,24},{32,28},{36,32}... | collective-permute-start | bytes 196616 | tf_op jit(solution)/shard_map/ppermute | solution.py:333
  30.3 6.5 %collective-permute-start.4 = (bf16[1,16,512]{2,1,0:T(8,128)(2,1)S(1)}, bf16[1,16,512]{2,1,0:T(8,128)(2,1)S(1)}, u32[]{:S(2)}, u32[]{:S(2)}) collective-permute-start(bf16[1,16,512]{2,1,0:T(8,128)(2,1)S(1)} %slice.11), channel_id=1, source_target_pairs={{0,3},{1,2},{2,1},{3,0},{4,7},{5,6},{6,5},{7,4},{8,11},{9,10},{10,... | collective-permute-start | bytes 49160 | tf_op jit(solution)/shard_map/ppermute | solution.py:336
  31.9 5.4 %collective-permute-start.3 = (bf16[2,16,512]{2,1,0:T(8,128)(2,1)S(1)}, bf16[2,16,512]{2,1,0:T(8,128)(2,1)S(1)}, u32[]{:S(2)}, u32[]{:S(2)}) collective-permute-start(bf16[2,16,512]{2,1,0:T(8,128)(2,1)S(1)} %get-tuple-element.37), channel_id=1, source_target_pairs={{0,2},{1,3},{2,0},{3,1},{4,6},{5,7},{6,4},{7,5},{8,10},{9,11},{10,... | collective-permute-start | bytes 98312 | tf_op jit(solution)/shard_map/ppermute | solution.py:336
  34.6 3.9 %collective-permute-start.2 = (bf16[2,16,512]{2,1,0:T(8,128)(2,1)S(1)}, bf16[2,16,512]{2,1,0:T(8,128)(2,1)S(1)}, u32[]{:S(2)}, u32[]{:S(2)}) collective-permute-start(bf16[2,16,512]{2,1,0:T(8,128)(2,1)S(1)} %get-tuple-element.38), channel_id=1, source_target_pairs={{0,1},{1,0},{2,3},{3,2},{4,5},{5,4},{6,7},{7,6},{8,9},{9,8},{10,11... | collective-permute-start | bytes 98312 | tf_op jit(solution)/shard_map/ppermute | solution.py:336

commit v6 on v5

--- a/solution.py
+++ b/solution.py
@@ -261,16 +261,32 @@
         partial[i] = before[i] + 2.0 * double[i]
 
 
-def outside(from_row, from_column, from_corner, upper, tiles_early, tiles_late, tiles_up, before, image, products, copies):
-    sources = {4: (from_column, 0), 5: (from_column, 1), 6: (from_row, 0), 7: (from_row, 1), 8: (from_corner, 0)}
-    border = {j: ref[place] for j, (ref, place) in sources.items()}
+def cross_tile(step, tiles_early, tiles_late):
+    first = len(CROSS) - len(LATE)
+    return tiles_early[10 + step] if step < first else tiles_late[step - first]
+
+
+def by_column(from_column, tiles_early, tiles_late, tiles_up, before, partial, raised):
+    border = {4: from_column[0], 5: from_column[1]}
     single = [jnp.zeros((RHS, BLOCK), f32)] * 4
-    raised = [jnp.zeros((RHS, BLOCK), f32)] * 4
-    first = len(CROSS) - len(LATE)
+    lifted = [jnp.zeros((RHS, BLOCK), f32)] * 4
     for step, (i, j) in enumerate(CROSS):
-        tile = tiles_early[10 + step] if step < first else tiles_late[step - first]
-        single[i] += times(border[j], tile)
-        raised[i] += times(border[j], tiles_up[16 + step])
+        if j in border:
+            single[i] += times(border[j], cross_tile(step, tiles_early, tiles_late))
+            lifted[i] += times(border[j], tiles_up[16 + step])
+    for i in range(4):
+        partial[i] = before[i] + single[i]
+        raised[i] = lifted[i]
+
+
+def outside(from_row, from_corner, upper, tiles_early, tiles_late, tiles_up, before, lifted, image, products, copies):
+    border = {6: from_row[0], 7: from_row[1], 8: from_corner[0]}
+    single = [jnp.zeros((RHS, BLOCK), f32)] * 4
+    raised = [lifted[i] for i in range(4)]
+    for step, (i, j) in enumerate(CROSS):
+        if j in border:
+            single[i] += times(border[j], cross_tile(step, tiles_early, tiles_late))
+            raised[i] += times(border[j], tiles_up[16 + step])
     third = gram(
         side_by_side([image[i] for i in range(4)] + [upper[i].astype(f32) for i in range(4)]),
         side_by_side([before[i] + single[i] for i in range(4)] + [2.0 * raised[i] for i in range(4)]),
@@ -287,6 +303,48 @@
     copies[...] = jnp.broadcast_to(jnp.sum(arrived[...], axis=0, keepdims=True), copies.shape)
 
 
+def inverse_of_two(block):
+    (a, b), (c, d) = block
+    scale = 1.0 / (a * d - b * c)
+    return ((d * scale, -b * scale), (-c * scale, a * scale))
+
+
+def product_of_two(first, second):
+    return tuple(
+        tuple(first[p][0] * second[0][q] + first[p][1] * second[1][q] for q in range(2))
+        for p in range(2)
+    )
+
+
+def eliminate_four(value, rows, k):
+    columns = [jnp.broadcast_to(value[:, k + q:k + q + 1], value.shape) for q in range(4)]
+    lines = [value[k + q:k + q + 1] for q in range(4)]
+    pivot = [[columns[q][k + p:k + p + 1] for q in range(4)] for p in range(4)]
+
+    def block(p, q):
+        return ((pivot[p][q], pivot[p][q + 1]), (pivot[p + 1][q], pivot[p + 1][q + 1]))
+
+    head = inverse_of_two(block(0, 0))
+    right = block(0, 2)
+    reduced = product_of_two(block(2, 0), head)
+    corner = block(2, 2)
+    taken = product_of_two(reduced, right)
+    tail = inverse_of_two(
+        tuple(tuple(corner[p][q] - taken[p][q] for q in range(2)) for p in range(2))
+    )
+    low = [lines[2 + p] - (reduced[p][0] * lines[0] + reduced[p][1] * lines[1]) for p in range(2)]
+    low = [tail[p][0] * low[0] + tail[p][1] * low[1] for p in range(2)]
+    high = [lines[p] - (right[p][0] * low[0] + right[p][1] * low[1]) for p in range(2)]
+    high = [head[p][0] * high[0] + head[p][1] * high[1] for p in range(2)]
+    new = high + low
+    value = (value - columns[0] * new[0] - columns[1] * new[1]) - (
+        columns[2] * new[2] + columns[3] * new[3]
+    )
+    for q in range(4):
+        value = jnp.where(rows == k + q, new[q], value)
+    return value
+
+
 def conclude(arrived, own_sides, image, result):
     packed = jnp.sum(arrived[...], axis=0)
     ordered = jnp.concatenate([packed[:, 0:64], packed[:, 64:128]], axis=0)
@@ -300,17 +358,8 @@
     known = jnp.concatenate([start, square[0:16, 0:16]], axis=0)
     value = jnp.concatenate([square[:, 0:32], known, jnp.zeros((32, 80), f32)], axis=1)
     rows = lax.broadcasted_iota(jnp.int32, (32, 128), 0)
-    for k in range(0, 32, 2):
-        first_column = jnp.broadcast_to(value[:, k:k + 1], value.shape)
-        second_column = jnp.broadcast_to(value[:, k + 1:k + 2], value.shape)
-        a, b = first_column[k:k + 1], second_column[k:k + 1]
-        c, d = first_column[k + 1:k + 2], second_column[k + 1:k + 2]
-        first_row, second_row = value[k:k + 1], value[k + 1:k + 2]
-        inverse = 1.0 / (a * d - b * c)
-        first_new = (d * first_row - b * second_row) * inverse
-        second_new = (a * second_row - c * first_row) * inverse
-        value = value - first_column * first_new - second_column * second_new
-        value = jnp.where(rows == k, first_new, jnp.where(rows == k + 1, second_new, value))
+    for k in range(0, 32, 4):
+        value = eliminate_four(value, rows, k)
     weights = jnp.transpose(jnp.concatenate([value, jnp.zeros((96, 128), f32)], axis=0))[32:48, 0:32]
     member = lax.axis_index("sub")
     for i, (row, column) in enumerate(OWN):
@@ -398,12 +447,16 @@
     partial = call(
         upward, "upward", shape(*field), (upper, tiles_up, partial), 16 * 2 * tile_flops,
     )
+    partial, raised = call(
+        by_column, "by_column", (shape(*field), shape(*field)),
+        (from_column, tiles_early, tiles_late, tiles_up, partial), 8 * 2 * tile_flops,
+    )
     plane = 8 * members
     copies = call(
         outside, "outside", shape(plane, 8, 128),
-        (from_row, from_column, from_corner, upper, tiles_early, tiles_late, tiles_up, partial,
-         image, products),
-        18 * 2 * tile_flops,
+        (from_row, from_corner, upper, tiles_early, tiles_late, tiles_up, partial, raised, image,
+         products),
+        10 * 2 * tile_flops,
     )
     arrived = swap(copies, 1)
     copies = call(add_up, "add_up", shape(everyone // plane, 8, 128), (arrived,), 1024)

time: 78.1 us -> 77.4 us (level)
    pallas_call x10 -> x11, Pallas kernels: 31.7 us -> 31.5 us  [call(): pl.pallas_call(kernel, name=name, out_shape=out_shape, in_specs=[pl.Block...]
  transfers between devices with their start and end apart: 6 -> 6, of which waited for: 2 -> 2; matrix products, arithmetic and copies ran while one was open for 0% -> 0% of each run, Pallas kernels for 19% -> 20%
where the time goes in v6:
time: 77.4 us; the launch traced here: 76.4 us
  blocking collectives  33.7 us (44%)
  Pallas kernels  31.5 us (41%)
  starting transfers between devices  9.95 us (13%)
  waiting for transfers between devices  1.08 us (1%)
    all_to_all x2, blocking collectives, swap(): lax.all_to_all(copies, ('region', 'sub'), 0, 0, axis_index_groups=groups,...  33.7 us
    pallas_call x11, Pallas kernels, call(): pl.pallas_call(kernel, name=name, out_shape=out_shape, in_specs=[pl.Block...  31.5 us
    ppermute x3, starting transfers between devices, from_region(): return lax.ppermute(value, 'region', pairs)  5.61 us
    ppermute x3, starting transfers between devices, from_member(): lax.ppermute(value, 'sub', [(source, source ^ mask) for source in range(m...  4.34 us
  transfers between devices with their start and end apart: 6, of which 2 were waited for; matrix products, arithmetic and copies ran while one was open for 0% of the time, Pallas kernels for 20%

profile of v6, /device:TPU:8, one launch (start us, length us, event | category | flops | bytes accessed | tf_op | source)
XLA Modules:
  0.0 76.4 jit_solution(13681118400329069757)
XLA Ops:
  0.0 1.4 %prepare.1 = (bf16[9,32,512]{2,1,0:T(8,128)(2,1)S(1)}, bf16[9,512,64]{2,1,0:T(8,128)(2,1)S(1)}, bf16[4,64,512]{2,1,0:T(8,128)(2,1)S(1)}, f32[4,16,512]{2,1,0:T(8,128)S(1)}, f32[4,1,512]{2,1,0:T(1,128)S(1)}) custom-call(f32[3,16,512]{2,1,0:T(8,128)} %points_far.1, f32[16,512]{1,0:T(8,128)} %noise_far.1, f32[16,16,512]{2,1,0:T(8,128)} %sides_far.1), custom_call_target="tpu_custom_call" | custom-call | flops 134217728 | bytes 1048576 | tf_op jit(solution)/shard_map/prepare/pallas_call | solution.py:30
  1.4 1.3 %collective-permute-start = (bf16[9,32,512]{2,1,0:T(8,128)(2,1)S(1)}, bf16[9,32,512]{2,1,0:T(8,128)(2,1)S(1)}, u32[]{:S(2)}, u32[]{:S(2)}) collective-permute-start(bf16[9,32,512]{2,1,0:T(8,128)(2,1)S(1)} %get-tuple-element.23.sent), channel_id=1, source_target_pairs={{4,0},{8,4},{12,8},{16,12},{20,16},{24,20},{28,24},{32,28},{36,32}... | collective-permute-start | bytes 884744 | tf_op jit(solution)/shard_map/ppermute | solution.py:382
  2.7 6.9 %within_layer.1 = (f32[4,16,512]{2,1,0:T(8,128)S(1)}, bf16[16,512,512]{2,1,0:T(8,128)(2,1)S(1)}) custom-call(bf16[9,32,512]{2,1,0:T(8,128)(2,1)S(1)} %get-tuple-element.23.sent, bf16[9,512,64]{2,1,0:T(8,128)(2,1)S(1)} %get-tuple-element.24.left, bf16[4,64,512]{2,1,0:T(8,128)(2,1)S(1)} %get-tuple-element.25.right), custom_call_target="tpu_custom_call" | custom-call | flops 8589934592 | bytes 1048576 | tf_op jit(solution)/shard_map/within_layer/pallas_call | solution.py:30
  9.6 0.0 collective-permute-done.above
  9.6 11.1 %above_own.1 = (f32[4,16,512]{2,1,0:T(8,128)S(1)}, bf16[4,16,512]{2,1,0:T(8,128)(2,1)S(1)}, bf16[25,512,512]{2,1,0:T(8,128)(2,1)S(1)}) custom-call(bf16[9,32,512]{2,1,0:T(8,128)(2,1)S(1)} %get-tuple-element.23.sent, bf16[9,512,64]{2,1,0:T(8,128)(2,1)S(1)} %get-tuple-element.24.left, bf16[4,64,512]{2,1,0:T(8,128)(2,1)S(1)} %get-tuple-element.25.right, ...), custom_call_target="tpu_custom_call" | custom-call | flops 13421772800 | bytes 1048576 | tf_op jit(solution)/shard_map/above_own/pallas_call | solution.py:30
  20.7 3.0 %collective-permute-start.1 = (bf16[4,16,512]{2,1,0:T(8,128)(2,1)S(1)}, bf16[4,16,512]{2,1,0:T(8,128)(2,1)S(1)}, u32[]{:S(2)}, u32[]{:S(2)}) collective-permute-start(bf16[4,16,512]{2,1,0:T(8,128)(2,1)S(1)} %get-tuple-element.29), channel_id=1, source_target_pairs={{0,4},{4,8},{8,12},{12,16},{16,20},{20,24},{24,28},{28,32},{32,36}... | collective-permute-start | bytes 196616 | tf_op jit(solution)/shard_map/ppermute | solution.py:382
  23.7 5.2 %borders.1 = (f32[4,16,512]{2,1,0:T(8,128)S(1)}, bf16[3,512,512]{2,1,0:T(8,128)(2,1)S(1)}) custom-call(bf16[9,32,512]{2,1,0:T(8,128)(2,1)S(1)} %get-tuple-element.23.sent, bf16[9,512,64]{2,1,0:T(8,128)(2,1)S(1)} %get-tuple-element.24.left, bf16[4,64,512]{2,1,0:T(8,128)(2,1)S(1)} %get-tuple-element.25.right, ...), custom_call_target="tpu_custom_call" | custom-call | flops 8589934592 | bytes 1048576 | tf_op jit(solution)/shard_map/borders/pallas_call | solution.py:30
  28.9 0.0 collective-permute-done.1.arrived
  29.0 1.3 %collective-permute-start.4 = (bf16[4,16,512]{2,1,0:T(8,128)(2,1)S(1)}, bf16[4,16,512]{2,1,0:T(8,128)(2,1)S(1)}, u32[]{:S(2)}, u32[]{:S(2)}) collective-permute-start(bf16[4,16,512]{2,1,0:T(8,128)(2,1)S(1)} %get-tuple-element.32.rounded), channel_id=1, source_target_pairs={{4,0},{8,4},{12,8},{16,12},{20,16},{24,20},{28,24},{32,28},{36,32}... | collective-permute-start | bytes 196616 | tf_op jit(solution)/shard_map/ppermute | solution.py:382
  30.3 1.7 %collective-permute-start.3 = (bf16[1,16,512]{2,1,0:T(8,128)(2,1)S(1)}, bf16[1,16,512]{2,1,0:T(8,128)(2,1)S(1)}, u32[]{:S(2)}, u32[]{:S(2)}) collective-permute-start(bf16[1,16,512]{2,1,0:T(8,128)(2,1)S(1)} %slice.10), channel_id=1, source_target_pairs={{0,3},{1,2},{2,1},{3,0},{4,7},{5,6},{6,5},{7,4},{8,11},{9,10},{10,... | collective-permute-start | bytes 49160 | tf_op jit(solution)/shard_map/ppermute | solution.py:385
  31.9 2.7 %collective-permute-start.5 = (bf16[2,16,512]{2,1,0:T(8,128)(2,1)S(1)}, bf16[2,16,512]{2,1,0:T(8,128)(2,1)S(1)}, u32[]{:S(2)}, u32[]{:S(2)}) collective-permute-start(bf16[2,16,512]{2,1,0:T(8,128)(2,1)S(1)} %get-tuple-element.41), channel_id=1, source_target_pairs={{0,2},{1,3},{2,0},{3,1},{4,6},{5,7},{6,4},{7,5},{8,10},{9,11},{10,... | collective-permute-start | bytes 98312 | tf_op jit(solution)/shard_map/ppermute | solution.py:385
  34.6 0.0 collective-permute-start.2
  34.6 1.0 %inside.1 = (f32[32,32]{1,0:T(8,128)S(1)}, f32[4,16,512]{2,1,0:T(8,128)S(1)}) custom-call(f32[4,16,512]{2,1,0:T(8,128)S(1)} %get-tuple-element.31.own_sides, f32[4,16,512]{2,1,0:T(8,128)S(1)} %get-tuple-element.36.image, bf16[4,16,512]{2,1,0:T(8,128)(2,1)S(1)} %get-tuple-element.32.rounded, f32[4,1,512]{2,1,0:T(1,128)S(1)} %get-tuple-element.30.own_noise, ...), custom_call_target="tpu_custom_call" | custom-call | flops 2684354560 | bytes 1048576 | tf_op jit(solution)/shard_map/inside/pallas_call | solution.py:30
  35.6 0.0 collective-permute-done.4.upper
  35.6 1.2 %upward.1.before = f32[4,16,512]{2,1,0:T(8,128)S(1)} custom-call(bf16[4,16,512]{2,1,0:T(8,128)(2,1)S(1)} %collective-permute-done.4.upper, bf16[25,512,512]{2,1,0:T(8,128)(2,1)S(1)} %get-tuple-element.35.tiles.tiles_up, f32[4,16,512]{2,1,0:T(8,128)S(1)} %get-tuple-element.37.before), custom_call_target="tpu_custom_call" | custom-call | flops 4294967296 | bytes 1048576 | tf_op jit(solution)/shard_map/upward/pallas_call | solution.py:30
  36.8 0.5 collective-permute-done.5.from_column
  37.4 0.6 by_column.1
  38.0 0.0 collective-permute-done.3.from_corner
  38.0 0.5 collective-permute-done.2.from_row
  38.5 1.6 %outside.1 = f32[32,8,128]{2,1,0:T(8,128)S(1)} custom-call(bf16[2,16,512]{2,1,0:T(8,128)(2,1)S(1)} %collective-permute-done.2.from_row, bf16[1,16,512]{2,1,0:T(8,128)(2,1)S(1)} %collective-permute-done.3.from_corner, bf16[4,16,512]{2,1,0:T(8,128)(2,1)S(1)} %collective-permute-done.4.upper, bf16[16,512,512]{2,1,0:T(8,128)(2,1)S(1)} %get-tuple-element.33.tiles.tiles_early, ...), custom_call_target="tpu_custom_call" | custom-call | flops 2684354560 | bytes 1048576 | tf_op jit(solution)/shard_map/outside/pallas_call | solution.py:30
  40.2 16.2 %all_to_all.10.arrived = f32[32,8,128]{2,1,0:T(8,128)S(1)} all-to-all(f32[32,8,128]{2,1,0:T(8,128)S(1)} %outside.1), channel_id=1, replica_groups={{0,1,2,3,4,5,6,7,8,9,10,11,12,13,14,15,16,17,18,19,20,21,22,23,24,25,26..., dimensions={0} | all-to-all | bytes 262144 | tf_op jit(solution)/shard_map/all_to_all | solution.py:394
  56.5 17.4 %all_to_all.11.arrived = f32[8,8,128]{2,1,0:T(8,128)S(1)} all-to-all(f32[8,8,128]{2,1,0:T(8,128)S(1)} %add_up.1), channel_id=1, replica_groups={{0,32,64,96,128,160,192,224},{1,33,65,97,129,161,193,225},{2,34,66,98,1..., dimensions={0} | all-to-all | bytes 65536 | tf_op jit(solution)/shard_map/all_to_all | solution.py:394
  73.9 2.4 %conclude.1 = f32[4,16,512]{2,1,0:T(8,128)} custom-call(f32[8,8,128]{2,1,0:T(8,128)S(1)} %all_to_all.11.arrived, f32[4,16,512]{2,1,0:T(8,128)S(1)} %get-tuple-element.31.own_sides, f32[4,16,512]{2,1,0:T(8,128)S(1)} %get-tuple-element.36.image), custom_call_target="tpu_custom_call" | custom-call | flops 134217728 | bytes 1048576 | tf_op jit(solution)/shard_map/conclude/pallas_call | solution.py:30
  (4 shorter events, 0.1 us)
Async XLA Ops:
  1.4 8.2 %collective-permute-start = (bf16[9,32,512]{2,1,0:T(8,128)(2,1)S(1)}, bf16[9,32,512]{2,1,0:T(8,128)(2,1)S(1)}, u32[]{:S(2)}, u32[]{:S(2)}) collective-permute-start(bf16[9,32,512]{2,1,0:T(8,128)(2,1)S(1)} %get-tuple-element.23.sent), channel_id=1, source_target_pairs={{4,0},{8,4},{12,8},{16,12},{20,16},{24,20},{28,24},{32,28},{36,32}... | collective-permute-start | bytes 884744 | tf_op jit(solution)/shard_map/ppermute | solution.py:382
  20.7 8.2 %collective-permute-start.1 = (bf16[4,16,512]{2,1,0:T(8,128)(2,1)S(1)}, bf16[4,16,512]{2,1,0:T(8,128)(2,1)S(1)}, u32[]{:S(2)}, u32[]{:S(2)}) collective-permute-start(bf16[4,16,512]{2,1,0:T(8,128)(2,1)S(1)} %get-tuple-element.29), channel_id=1, source_target_pairs={{0,4},{4,8},{8,12},{12,16},{16,20},{20,24},{24,28},{28,32},{32,36}... | collective-permute-start | bytes 196616 | tf_op jit(solution)/shard_map/ppermute | solution.py:382
  29.0 6.6 %collective-permute-start.4 = (bf16[4,16,512]{2,1,0:T(8,128)(2,1)S(1)}, bf16[4,16,512]{2,1,0:T(8,128)(2,1)S(1)}, u32[]{:S(2)}, u32[]{:S(2)}) collective-permute-start(bf16[4,16,512]{2,1,0:T(8,128)(2,1)S(1)} %get-tuple-element.32.rounded), channel_id=1, source_target_pairs={{4,0},{8,4},{12,8},{16,12},{20,16},{24,20},{28,24},{32,28},{36,32}... | collective-permute-start | bytes 196616 | tf_op jit(solution)/shard_map/ppermute | solution.py:382
  30.3 7.7 %collective-permute-start.3 = (bf16[1,16,512]{2,1,0:T(8,128)(2,1)S(1)}, bf16[1,16,512]{2,1,0:T(8,128)(2,1)S(1)}, u32[]{:S(2)}, u32[]{:S(2)}) collective-permute-start(bf16[1,16,512]{2,1,0:T(8,128)(2,1)S(1)} %slice.10), channel_id=1, source_target_pairs={{0,3},{1,2},{2,1},{3,0},{4,7},{5,6},{6,5},{7,4},{8,11},{9,10},{10,... | collective-permute-start | bytes 49160 | tf_op jit(solution)/shard_map/ppermute | solution.py:385
  31.9 5.4 %collective-permute-start.5 = (bf16[2,16,512]{2,1,0:T(8,128)(2,1)S(1)}, bf16[2,16,512]{2,1,0:T(8,128)(2,1)S(1)}, u32[]{:S(2)}, u32[]{:S(2)}) collective-permute-start(bf16[2,16,512]{2,1,0:T(8,128)(2,1)S(1)} %get-tuple-element.41), channel_id=1, source_target_pairs={{0,2},{1,3},{2,0},{3,1},{4,6},{5,7},{6,4},{7,5},{8,10},{9,11},{10,... | collective-permute-start | bytes 98312 | tf_op jit(solution)/shard_map/ppermute | solution.py:385
  34.6 3.9 %collective-permute-start.2 = (bf16[2,16,512]{2,1,0:T(8,128)(2,1)S(1)}, bf16[2,16,512]{2,1,0:T(8,128)(2,1)S(1)}, u32[]{:S(2)}, u32[]{:S(2)}) collective-permute-start(bf16[2,16,512]{2,1,0:T(8,128)(2,1)S(1)} %get-tuple-element.42), channel_id=1, source_target_pairs={{0,1},{1,0},{2,3},{3,2},{4,5},{5,4},{6,7},{7,6},{8,9},{9,8},{10,11... | collective-permute-start | bytes 98312 | tf_op jit(solution)/shard_map/ppermute | solution.py:385

commit v7 on v6

--- a/solution.py
+++ b/solution.py
@@ -10,14 +10,15 @@
 BORDER = ((0, 2), (1, 2), (2, 0), (2, 1), (2, 2))
 WINDOW = OWN + BORDER
 PAIRED = tuple((i, j) for j in range(4) for i in range(j))
-SELF = tuple((i, i) for i in range(4))
 CROSS = tuple(
     (i, j)
     for j in range(4, 9)
     for i in range(4)
     if max(abs(OWN[i][0] - WINDOW[j][0]), abs(OWN[i][1] - WINDOW[j][1])) <= 1
 )
-EARLY = SELF + PAIRED + CROSS[:6]
+HALF = 256
+PACKED = 3
+EARLY = PAIRED + CROSS[:6]
 LATE = CROSS[6:]
 BLOCK = 512
 RHS = 16
@@ -121,13 +122,16 @@
     return feature_rows(place)
 
 
-def sweep(lefts, rights, buffers, use):
-    count = len(lefts)
+def sweep(lefts, rights, buffers, use, fills=()):
+    count = len(fills) + len(lefts)
 
     def distances(step):
-        buffers[step % 2][...] = jnp.dot(
-            lefts[step](), rights[step](), preferred_element_type=f32
-        )
+        buffer = buffers[step % 2]
+        if step < len(fills):
+            fills[step](buffer)
+        else:
+            place = step - len(fills)
+            buffer[...] = jnp.dot(lefts[place](), rights[place](), preferred_element_type=f32)
 
     distances(0)
     for step in range(count):
@@ -152,19 +156,45 @@
 
 def within_layer(sent, left, right, totals, tiles, *buffers):
     totals[...] = jnp.zeros_like(totals)
-    pairs = EARLY
+
+    def upper_halves(first, buffer):
+        for place in range(2):
+            i = first + place
+            buffer[place * HALF:(place + 1) * HALF, :] = jnp.dot(
+                left[i, 0:HALF, :], right[i], preferred_element_type=f32
+            )
+
+    def last_quarters(buffer):
+        for i in range(4):
+            down, along = i // 2 * HALF, i % 2 * HALF
+            buffer[down:down + HALF, along:along + HALF] = jnp.dot(
+                left[i, HALF:BLOCK, :], right[i, :, HALF:BLOCK], preferred_element_type=f32
+            )
 
     def use(step, tile):
-        i, j = pairs[step]
         tiles[step] = tile
-        totals[i] += times(sent[j, 0:16, :], tile)
-        if i != j and j < 4:
-            totals[j] += times_transposed(sent[i, 0:16, :], tile)
+        if step < 2:
+            for place in range(2):
+                i = 2 * step + place
+                part = tile[place * HALF:(place + 1) * HALF, :]
+                totals[i] += times(sent[i, 0:16, 0:HALF], part)
+                totals[i, :, 0:HALF] += times_transposed(sent[i, 0:16, HALF:BLOCK], part[:, HALF:BLOCK])
+        elif step == 2:
+            for i in range(4):
+                down, along = i // 2 * HALF, i % 2 * HALF
+                part = tile[down:down + HALF, along:along + HALF]
+                totals[i, :, HALF:BLOCK] += times(sent[i, 0:16, HALF:BLOCK], part)
+        else:
+            i, j = EARLY[step - PACKED]
+            totals[i] += times(sent[j, 0:16, :], tile)
+            if j < 4:
+                totals[j] += times_transposed(sent[i, 0:16, :], tile)
 
     sweep(
-        [lambda j=j: left[j] for i, j in pairs],
-        [lambda i=i: right[i] for i, j in pairs],
+        [lambda j=j: left[j] for i, j in EARLY],
+        [lambda i=i: right[i] for i, j in EARLY],
         buffers, use,
+        [functools.partial(upper_halves, 0), functools.partial(upper_halves, 2), last_quarters],
     )
 
 
@@ -245,12 +275,16 @@
         axis=0,
     )
     products[...] = gram(both, both)
-    single = [times(rounded[i], tiles[i]) for i in range(4)]
     double = [jnp.zeros((RHS, BLOCK), f32)] * 4
     for step, (i, j) in enumerate(PAIRED):
-        double[i] += times(rounded[j], tiles[4 + step])
+        double[i] += times(rounded[j], tiles[PACKED + step])
     for i in range(4):
-        partial[i] = own_noise[i] * image[i] * 256.0 + single[i] + 2.0 * double[i]
+        start = i % 2 * HALF
+        upper = times(rounded[i, :, 0:HALF], tiles[i // 2, start:start + HALF, :])
+        down = i // 2 * HALF
+        last = times(rounded[i, :, HALF:BLOCK], tiles[2, down:down + HALF, start:start + HALF])
+        single = jnp.concatenate([upper[:, 0:HALF], 2.0 * upper[:, HALF:BLOCK] + last], axis=1)
+        partial[i] = own_noise[i] * image[i] * 256.0 + single + 2.0 * double[i]
 
 
 def upward(upper, tiles, before, partial):
@@ -261,36 +295,35 @@
         partial[i] = before[i] + 2.0 * double[i]
 
 
-def cross_tile(step, tiles_early, tiles_late):
+def cross_products(border, tiles_early, tiles_late, tiles_up, single, raised):
     first = len(CROSS) - len(LATE)
-    return tiles_early[10 + step] if step < first else tiles_late[step - first]
-
-
-def by_column(from_column, tiles_early, tiles_late, tiles_up, before, partial, raised):
+    for step, (i, j) in enumerate(CROSS):
+        if j in border:
+            tile = tiles_early[PACKED + 6 + step] if step < first else tiles_late[step - first]
+            single[i] += times(border[j], tile)
+            raised[i] += times(border[j], tiles_up[16 + step])
+
+
+def by_row(from_row, from_corner, upper, tiles_early, tiles_late, tiles_up, before, image, third):
+    border = {6: from_row[0], 7: from_row[1], 8: from_corner[0]}
+    single = [before[i] for i in range(4)]
+    raised = [jnp.zeros((RHS, BLOCK), f32)] * 4
+    cross_products(border, tiles_early, tiles_late, tiles_up, single, raised)
+    third[...] = gram(
+        side_by_side([image[i] for i in range(4)] + [upper[i].astype(f32) for i in range(4)]),
+        side_by_side(single + [2.0 * raised[i] for i in range(4)]),
+    )
+
+
+def by_column(from_column, upper, tiles_early, tiles_late, tiles_up, so_far, image, products, copies):
     border = {4: from_column[0], 5: from_column[1]}
     single = [jnp.zeros((RHS, BLOCK), f32)] * 4
-    lifted = [jnp.zeros((RHS, BLOCK), f32)] * 4
-    for step, (i, j) in enumerate(CROSS):
-        if j in border:
-            single[i] += times(border[j], cross_tile(step, tiles_early, tiles_late))
-            lifted[i] += times(border[j], tiles_up[16 + step])
-    for i in range(4):
-        partial[i] = before[i] + single[i]
-        raised[i] = lifted[i]
-
-
-def outside(from_row, from_corner, upper, tiles_early, tiles_late, tiles_up, before, lifted, image, products, copies):
-    border = {6: from_row[0], 7: from_row[1], 8: from_corner[0]}
-    single = [jnp.zeros((RHS, BLOCK), f32)] * 4
-    raised = [lifted[i] for i in range(4)]
-    for step, (i, j) in enumerate(CROSS):
-        if j in border:
-            single[i] += times(border[j], cross_tile(step, tiles_early, tiles_late))
-            raised[i] += times(border[j], tiles_up[16 + step])
-    third = gram(
-        side_by_side([image[i] for i in range(4)] + [upper[i].astype(f32) for i in range(4)]),
-        side_by_side([before[i] + single[i] for i in range(4)] + [2.0 * raised[i] for i in range(4)]),
-    ) * (1.0 / 256.0)
+    raised = [jnp.zeros((RHS, BLOCK), f32)] * 4
+    cross_products(border, tiles_early, tiles_late, tiles_up, single, raised)
+    third = (so_far[...] + gram(
+        side_by_side([image[i] for i in (1, 3)] + [upper[i].astype(f32) for i in (1, 3)]),
+        side_by_side([single[i] for i in (1, 3)] + [2.0 * raised[i] for i in (1, 3)]),
+    )) * (1.0 / 256.0)
     known = products[...]
     ordered = jnp.concatenate(
         [known[16:32, 16:32], known[16:32, 0:16], known[0:16, 0:16], third], axis=1
@@ -416,8 +449,8 @@
     )
     above = from_region(sent, 1)
     totals, tiles_early = call(
-        within_layer, "within_layer", (shape(*field), held(len(EARLY), BLOCK, BLOCK)),
-        (sent, left, right), len(EARLY) * 4 * tile_flops, buffers,
+        within_layer, "within_layer", (shape(*field), held(PACKED + len(EARLY), BLOCK, BLOCK)),
+        (sent, left, right), (PACKED + len(EARLY)) * 4 * tile_flops, buffers,
     )
     totals, passed, tiles_up = call(
         above_own, "above_own",
@@ -447,16 +480,16 @@
     partial = call(
         upward, "upward", shape(*field), (upper, tiles_up, partial), 16 * 2 * tile_flops,
     )
-    partial, raised = call(
-        by_column, "by_column", (shape(*field), shape(*field)),
-        (from_column, tiles_early, tiles_late, tiles_up, partial), 8 * 2 * tile_flops,
+    third = call(
+        by_row, "by_row", shape(RHS, RHS),
+        (from_row, from_corner, upper, tiles_early, tiles_late, tiles_up, partial, image),
+        10 * 2 * tile_flops,
     )
     plane = 8 * members
     copies = call(
-        outside, "outside", shape(plane, 8, 128),
-        (from_row, from_corner, upper, tiles_early, tiles_late, tiles_up, partial, raised, image,
-         products),
-        10 * 2 * tile_flops,
+        by_column, "by_column", shape(plane, 8, 128),
+        (from_column, upper, tiles_early, tiles_late, tiles_up, third, image, products),
+        8 * 2 * tile_flops,
     )
     arrived = swap(copies, 1)
     copies = call(add_up, "add_up", shape(everyone // plane, 8, 128), (arrived,), 1024)

time: 77.4 us -> 76.8 us (level)
  transfers between devices with their start and end apart: 6 -> 6, of which waited for: 2 -> 1; matrix products, arithmetic and copies ran while one was open for 0% -> 0% of each run, Pallas kernels for 20% -> 20%
where the time goes in v7:
time: 76.8 us; the launch traced here: 75.8 us
  blocking collectives  33.7 us (44%)
  Pallas kernels  31 us (40%)
  starting transfers between devices  9.98 us (13%)
  waiting for transfers between devices  1.1 us (1%)
    all_to_all x2, blocking collectives, swap(): lax.all_to_all(copies, ('region', 'sub'), 0, 0, axis_index_groups=groups,...  33.7 us
    pallas_call x11, Pallas kernels, call(): pl.pallas_call(kernel, name=name, out_shape=out_shape, in_specs=[pl.Block...  31 us
    ppermute x3, starting transfers between devices, from_region(): return lax.ppermute(value, 'region', pairs)  5.61 us
    ppermute x3, starting transfers between devices, from_member(): lax.ppermute(value, 'sub', [(source, source ^ mask) for source in range(m...  4.37 us
  transfers between devices with their start and end apart: 6, of which 1 were waited for; matrix products, arithmetic and copies ran while one was open for 0% of the time, Pallas kernels for 20%

profile of v7, /device:TPU:8, one launch (start us, length us, event | category | flops | bytes accessed | tf_op | source)
XLA Modules:
  0.0 75.8 jit_solution(8845003794163390684)
XLA Ops:
  0.0 1.4 %prepare.1 = (bf16[9,32,512]{2,1,0:T(8,128)(2,1)S(1)}, bf16[9,512,64]{2,1,0:T(8,128)(2,1)S(1)}, bf16[4,64,512]{2,1,0:T(8,128)(2,1)S(1)}, f32[4,16,512]{2,1,0:T(8,128)S(1)}, f32[4,1,512]{2,1,0:T(1,128)S(1)}) custom-call(f32[3,16,512]{2,1,0:T(8,128)} %points_far.1, f32[16,512]{1,0:T(8,128)} %noise_far.1, f32[16,16,512]{2,1,0:T(8,128)} %sides_far.1), custom_call_target="tpu_custom_call" | custom-call | flops 134217728 | bytes 1048576 | tf_op jit(solution)/shard_map/prepare/pallas_call | solution.py:31
  1.4 1.3 %collective-permute-start = (bf16[9,32,512]{2,1,0:T(8,128)(2,1)S(1)}, bf16[9,32,512]{2,1,0:T(8,128)(2,1)S(1)}, u32[]{:S(2)}, u32[]{:S(2)}) collective-permute-start(bf16[9,32,512]{2,1,0:T(8,128)(2,1)S(1)} %get-tuple-element.21.sent), channel_id=1, source_target_pairs={{4,0},{8,4},{12,8},{16,12},{20,16},{24,20},{28,24},{32,28},{36,32}... | collective-permute-start | bytes 884744 | tf_op jit(solution)/shard_map/ppermute | solution.py:415
  2.7 6.2 %within_layer.1 = (f32[4,16,512]{2,1,0:T(8,128)S(1)}, bf16[15,512,512]{2,1,0:T(8,128)(2,1)S(1)}) custom-call(bf16[9,32,512]{2,1,0:T(8,128)(2,1)S(1)} %get-tuple-element.21.sent, bf16[9,512,64]{2,1,0:T(8,128)(2,1)S(1)} %get-tuple-element.22.left, bf16[4,64,512]{2,1,0:T(8,128)(2,1)S(1)} %get-tuple-element.23.right), custom_call_target="tpu_custom_call" | custom-call | flops 8053063680 | bytes 1048576 | tf_op jit(solution)/shard_map/within_layer/pallas_call | solution.py:31
  8.9 0.0 collective-permute-done.above
  8.9 11.1 %above_own.1 = (f32[4,16,512]{2,1,0:T(8,128)S(1)}, bf16[4,16,512]{2,1,0:T(8,128)(2,1)S(1)}, bf16[25,512,512]{2,1,0:T(8,128)(2,1)S(1)}) custom-call(bf16[9,32,512]{2,1,0:T(8,128)(2,1)S(1)} %get-tuple-element.21.sent, bf16[9,512,64]{2,1,0:T(8,128)(2,1)S(1)} %get-tuple-element.22.left, bf16[4,64,512]{2,1,0:T(8,128)(2,1)S(1)} %get-tuple-element.23.right, ...), custom_call_target="tpu_custom_call" | custom-call | flops 13421772800 | bytes 1048576 | tf_op jit(solution)/shard_map/above_own/pallas_call | solution.py:31
  20.0 3.0 %collective-permute-start.1 = (bf16[4,16,512]{2,1,0:T(8,128)(2,1)S(1)}, bf16[4,16,512]{2,1,0:T(8,128)(2,1)S(1)}, u32[]{:S(2)}, u32[]{:S(2)}) collective-permute-start(bf16[4,16,512]{2,1,0:T(8,128)(2,1)S(1)} %get-tuple-element.27), channel_id=1, source_target_pairs={{0,4},{4,8},{8,12},{12,16},{16,20},{20,24},{24,28},{28,32},{32,36}... | collective-permute-start | bytes 196616 | tf_op jit(solution)/shard_map/ppermute | solution.py:415
  23.0 5.2 %borders.1 = (f32[4,16,512]{2,1,0:T(8,128)S(1)}, bf16[3,512,512]{2,1,0:T(8,128)(2,1)S(1)}) custom-call(bf16[9,32,512]{2,1,0:T(8,128)(2,1)S(1)} %get-tuple-element.21.sent, bf16[9,512,64]{2,1,0:T(8,128)(2,1)S(1)} %get-tuple-element.22.left, bf16[4,64,512]{2,1,0:T(8,128)(2,1)S(1)} %get-tuple-element.23.right, ...), custom_call_target="tpu_custom_call" | custom-call | flops 8589934592 | bytes 1048576 | tf_op jit(solution)/shard_map/borders/pallas_call | solution.py:31
  28.2 0.0 collective-permute-done.1.arrived
  28.3 1.3 %collective-permute-start.3 = (bf16[4,16,512]{2,1,0:T(8,128)(2,1)S(1)}, bf16[4,16,512]{2,1,0:T(8,128)(2,1)S(1)}, u32[]{:S(2)}, u32[]{:S(2)}) collective-permute-start(bf16[4,16,512]{2,1,0:T(8,128)(2,1)S(1)} %get-tuple-element.30.rounded), channel_id=1, source_target_pairs={{4,0},{8,4},{12,8},{16,12},{20,16},{24,20},{28,24},{32,28},{36,32}... | collective-permute-start | bytes 196616 | tf_op jit(solution)/shard_map/ppermute | solution.py:415
  29.6 1.7 %collective-permute-start.5 = (bf16[1,16,512]{2,1,0:T(8,128)(2,1)S(1)}, bf16[1,16,512]{2,1,0:T(8,128)(2,1)S(1)}, u32[]{:S(2)}, u32[]{:S(2)}) collective-permute-start(bf16[1,16,512]{2,1,0:T(8,128)(2,1)S(1)} %slice.11), channel_id=1, source_target_pairs={{0,3},{1,2},{2,1},{3,0},{4,7},{5,6},{6,5},{7,4},{8,11},{9,10},{10,... | collective-permute-start | bytes 49160 | tf_op jit(solution)/shard_map/ppermute | solution.py:418
  31.2 1.9 %collective-permute-start.4 = (bf16[2,16,512]{2,1,0:T(8,128)(2,1)S(1)}, bf16[2,16,512]{2,1,0:T(8,128)(2,1)S(1)}, u32[]{:S(2)}, u32[]{:S(2)}) collective-permute-start(bf16[2,16,512]{2,1,0:T(8,128)(2,1)S(1)} %get-tuple-element.37), channel_id=1, source_target_pairs={{0,1},{1,0},{2,3},{3,2},{4,5},{5,4},{6,7},{7,6},{8,9},{9,8},{10,11... | collective-permute-start | bytes 98312 | tf_op jit(solution)/shard_map/ppermute | solution.py:418
  33.1 0.8 %collective-permute-start.2 = (bf16[2,16,512]{2,1,0:T(8,128)(2,1)S(1)}, bf16[2,16,512]{2,1,0:T(8,128)(2,1)S(1)}, u32[]{:S(2)}, u32[]{:S(2)}) collective-permute-start(bf16[2,16,512]{2,1,0:T(8,128)(2,1)S(1)} %get-tuple-element.38), channel_id=1, source_target_pairs={{0,2},{1,3},{2,0},{3,1},{4,6},{5,7},{6,4},{7,5},{8,10},{9,11},{10,... | collective-permute-start | bytes 98312 | tf_op jit(solution)/shard_map/ppermute | solution.py:418
  33.9 0.9 %inside.1 = (f32[32,32]{1,0:T(8,128)S(1)}, f32[4,16,512]{2,1,0:T(8,128)S(1)}) custom-call(f32[4,16,512]{2,1,0:T(8,128)S(1)} %get-tuple-element.29.own_sides, f32[4,16,512]{2,1,0:T(8,128)S(1)} %get-tuple-element.34.image, bf16[4,16,512]{2,1,0:T(8,128)(2,1)S(1)} %get-tuple-element.30.rounded, f32[4,1,512]{2,1,0:T(1,128)S(1)} %get-tuple-element.28.own_noise, ...), custom_call_target="tpu_custom_call" | custom-call | flops 2684354560 | bytes 1048576 | tf_op jit(solution)/shard_map/inside/pallas_call | solution.py:31
  34.9 0.0 collective-permute-done.3.upper
  34.9 1.2 %upward.1.before = f32[4,16,512]{2,1,0:T(8,128)S(1)} custom-call(bf16[4,16,512]{2,1,0:T(8,128)(2,1)S(1)} %collective-permute-done.3.upper, bf16[25,512,512]{2,1,0:T(8,128)(2,1)S(1)} %get-tuple-element.33.tiles.tiles_up, f32[4,16,512]{2,1,0:T(8,128)S(1)} %get-tuple-element.35.before), custom_call_target="tpu_custom_call" | custom-call | flops 4294967296 | bytes 1048576 | tf_op jit(solution)/shard_map/upward/pallas_call | solution.py:31
  36.1 0.0 collective-permute-done.5.from_corner
  36.1 0.0 collective-permute-done.4.from_row
  36.1 1.5 %by_row.1.so_far = f32[16,16]{1,0:T(8,128)S(1)} custom-call(bf16[2,16,512]{2,1,0:T(8,128)(2,1)S(1)} %collective-permute-done.4.from_row, bf16[1,16,512]{2,1,0:T(8,128)(2,1)S(1)} %collective-permute-done.5.from_corner, bf16[4,16,512]{2,1,0:T(8,128)(2,1)S(1)} %collective-permute-done.3.upper, bf16[15,512,512]{2,1,0:T(8,128)(2,1)S(1)} %get-tuple-element.31.tiles.tiles_early, ...), custom_call_target="tpu_custom_call" | custom-call | flops 2684354560 | bytes 1048576 | tf_op jit(solution)/shard_map/by_row/pallas_call | solution.py:31
  37.6 1.1 %collective-permute-done.2.from_column = bf16[2,16,512]{2,1,0:T(8,128)(2,1)S(1)} collective-permute-done((bf16[2,16,512]{2,1,0:T(8,128)(2,1)S(1)}, bf16[2,16,512]{2,1,0:T(8,128)(2,1)S(1)}, u32[]{:S(2)}, u32[]{:S(2)}) %collective-permute-start.2) | collective-permute-done | bytes 32800 | tf_op jit(solution)/shard_map/ppermute | solution.py:418
  38.7 1.0 %by_column.1 = f32[32,8,128]{2,1,0:T(8,128)S(1)} custom-call(bf16[2,16,512]{2,1,0:T(8,128)(2,1)S(1)} %collective-permute-done.2.from_column, bf16[4,16,512]{2,1,0:T(8,128)(2,1)S(1)} %collective-permute-done.3.upper, bf16[15,512,512]{2,1,0:T(8,128)(2,1)S(1)} %get-tuple-element.31.tiles.tiles_early, bf16[3,512,512]{2,1,0:T(8,128)(2,1)S(1)} %get-tuple-element.32.tiles_late, ...), custom_call_target="tpu_custom_call" | custom-call | flops 2147483648 | bytes 1048576 | tf_op jit(solution)/shard_map/by_column/pallas_call | solution.py:31
  39.7 16.3 %all_to_all.10.arrived = f32[32,8,128]{2,1,0:T(8,128)S(1)} all-to-all(f32[32,8,128]{2,1,0:T(8,128)S(1)} %by_column.1), channel_id=1, replica_groups={{0,1,2,3,4,5,6,7,8,9,10,11,12,13,14,15,16,17,18,19,20,21,22,23,24,25,26..., dimensions={0} | all-to-all | bytes 262144 | tf_op jit(solution)/shard_map/all_to_all | solution.py:427
  56.0 17.4 %all_to_all.11.arrived = f32[8,8,128]{2,1,0:T(8,128)S(1)} all-to-all(f32[8,8,128]{2,1,0:T(8,128)S(1)} %add_up.1), channel_id=1, replica_groups={{0,32,64,96,128,160,192,224},{1,33,65,97,129,161,193,225},{2,34,66,98,1..., dimensions={0} | all-to-all | bytes 65536 | tf_op jit(solution)/shard_map/all_to_all | solution.py:427
  73.4 2.4 %conclude.1 = f32[4,16,512]{2,1,0:T(8,128)} custom-call(f32[8,8,128]{2,1,0:T(8,128)S(1)} %all_to_all.11.arrived, f32[4,16,512]{2,1,0:T(8,128)S(1)} %get-tuple-element.29.own_sides, f32[4,16,512]{2,1,0:T(8,128)S(1)} %get-tuple-element.34.image), custom_call_target="tpu_custom_call" | custom-call | flops 134217728 | bytes 1048576 | tf_op jit(solution)/shard_map/conclude/pallas_call | solution.py:31
  (4 shorter events, 0.1 us)
Async XLA Ops:
  1.4 7.5 %collective-permute-start = (bf16[9,32,512]{2,1,0:T(8,128)(2,1)S(1)}, bf16[9,32,512]{2,1,0:T(8,128)(2,1)S(1)}, u32[]{:S(2)}, u32[]{:S(2)}) collective-permute-start(bf16[9,32,512]{2,1,0:T(8,128)(2,1)S(1)} %get-tuple-element.21.sent), channel_id=1, source_target_pairs={{4,0},{8,4},{12,8},{16,12},{20,16},{24,20},{28,24},{32,28},{36,32}... | collective-permute-start | bytes 884744 | tf_op jit(solution)/shard_map/ppermute | solution.py:415
  20.0 8.2 %collective-permute-start.1 = (bf16[4,16,512]{2,1,0:T(8,128)(2,1)S(1)}, bf16[4,16,512]{2,1,0:T(8,128)(2,1)S(1)}, u32[]{:S(2)}, u32[]{:S(2)}) collective-permute-start(bf16[4,16,512]{2,1,0:T(8,128)(2,1)S(1)} %get-tuple-element.27), channel_id=1, source_target_pairs={{0,4},{4,8},{8,12},{12,16},{16,20},{20,24},{24,28},{28,32},{32,36}... | collective-permute-start | bytes 196616 | tf_op jit(solution)/shard_map/ppermute | solution.py:415
  28.3 6.6 %collective-permute-start.3 = (bf16[4,16,512]{2,1,0:T(8,128)(2,1)S(1)}, bf16[4,16,512]{2,1,0:T(8,128)(2,1)S(1)}, u32[]{:S(2)}, u32[]{:S(2)}) collective-permute-start(bf16[4,16,512]{2,1,0:T(8,128)(2,1)S(1)} %get-tuple-element.30.rounded), channel_id=1, source_target_pairs={{4,0},{8,4},{12,8},{16,12},{20,16},{24,20},{28,24},{32,28},{36,32}... | collective-permute-start | bytes 196616 | tf_op jit(solution)/shard_map/ppermute | solution.py:415
  29.6 6.5 %collective-permute-start.5 = (bf16[1,16,512]{2,1,0:T(8,128)(2,1)S(1)}, bf16[1,16,512]{2,1,0:T(8,128)(2,1)S(1)}, u32[]{:S(2)}, u32[]{:S(2)}) collective-permute-start(bf16[1,16,512]{2,1,0:T(8,128)(2,1)S(1)} %slice.11), channel_id=1, source_target_pairs={{0,3},{1,2},{2,1},{3,0},{4,7},{5,6},{6,5},{7,4},{8,11},{9,10},{10,... | collective-permute-start | bytes 49160 | tf_op jit(solution)/shard_map/ppermute | solution.py:418
  31.2 4.8 %collective-permute-start.4 = (bf16[2,16,512]{2,1,0:T(8,128)(2,1)S(1)}, bf16[2,16,512]{2,1,0:T(8,128)(2,1)S(1)}, u32[]{:S(2)}, u32[]{:S(2)}) collective-permute-start(bf16[2,16,512]{2,1,0:T(8,128)(2,1)S(1)} %get-tuple-element.37), channel_id=1, source_target_pairs={{0,1},{1,0},{2,3},{3,2},{4,5},{5,4},{6,7},{7,6},{8,9},{9,8},{10,11... | collective-permute-start | bytes 98312 | tf_op jit(solution)/shard_map/ppermute | solution.py:418
  33.1 5.6 %collective-permute-start.2 = (bf16[2,16,512]{2,1,0:T(8,128)(2,1)S(1)}, bf16[2,16,512]{2,1,0:T(8,128)(2,1)S(1)}, u32[]{:S(2)}, u32[]{:S(2)}) collective-permute-start(bf16[2,16,512]{2,1,0:T(8,128)(2,1)S(1)} %get-tuple-element.38), channel_id=1, source_target_pairs={{0,2},{1,3},{2,0},{3,1},{4,6},{5,7},{6,4},{7,5},{8,10},{9,11},{10,... | collective-permute-start | bytes 98312 | tf_op jit(solution)/shard_map/ppermute | solution.py:418

commit v8 on v7

--- a/solution.py
+++ b/solution.py
@@ -269,7 +269,8 @@
     return jnp.concatenate(blocks, axis=1)
 
 
-def inside(own_sides, image, rounded, own_noise, tiles, products, partial):
+def inside(own_sides, image, rounded, own_noise, tiles, products, partial, for_row):
+    for_row[...] = rounded[2:4]
     both = jnp.concatenate(
         [side_by_side([image[i] for i in range(4)]), side_by_side([own_sides[i] for i in range(4)])],
         axis=0,
@@ -470,13 +471,13 @@
         (totals, arrived, own_noise, own_sides), tile_flops // 8,
     )
     upper = from_region(rounded, 1)
-    from_row = from_member(rounded[2:4], 1)
     from_column = from_member(rounded[1::2], 2)
     from_corner = from_member(rounded[3:4], 3)
-    products, partial = call(
-        inside, "inside", (shape(32, 32), shape(*field)),
+    products, partial, for_row = call(
+        inside, "inside", (shape(32, 32), shape(*field), shape(2, RHS, BLOCK, dtype=bf16)),
         (own_sides, image, rounded, own_noise, tiles_early), 10 * 2 * tile_flops,
     )
+    from_row = from_member(for_row, 1)
     partial = call(
         upward, "upward", shape(*field), (upper, tiles_up, partial), 16 * 2 * tile_flops,
     )

time: 76.8 us -> 78.7 us (1.025)
  waiting for transfers between devices: 1.1 us -> 2.71 us
    ppermute x3, waiting for transfers between devices: 1.08 us -> 2.71 us  [from_member(): lax.ppermute(value, 'sub', [(source, source ^ mask) for source in range(m...]
  transfers between devices with their start and end apart: 6 -> 6, of which waited for: 1 -> 1; matrix products, arithmetic and copies ran while one was open for 0% -> 0% of each run, Pallas kernels for 20% -> 19%
where the time goes in v8:
time: 78.7 us; the launch traced here: 77.7 us
  blocking collectives  33.6 us (43%)
  Pallas kernels  31.1 us (40%)
  starting transfers between devices  10.2 us (13%)
  waiting for transfers between devices  2.71 us (3%)
    all_to_all x2, blocking collectives, swap(): lax.all_to_all(copies, ('region', 'sub'), 0, 0, axis_index_groups=groups,...  33.6 us
    pallas_call x11, Pallas kernels, call(): pl.pallas_call(kernel, name=name, out_shape=out_shape, in_specs=[pl.Block...  31.1 us
    ppermute x3, starting transfers between devices, from_region(): return lax.ppermute(value, 'region', pairs)  5.61 us
    ppermute x3, starting transfers between devices, from_member(): lax.ppermute(value, 'sub', [(source, source ^ mask) for source in range(m...  4.64 us
    ppermute x3, waiting for transfers between devices, from_member(): lax.ppermute(value, 'sub', [(source, source ^ mask) for source in range(m...  2.71 us
  transfers between devices with their start and end apart: 6, of which 1 were waited for; matrix products, arithmetic and copies ran while one was open for 0% of the time, Pallas kernels for 19%

profile of v8, /device:TPU:8, one launch (start us, length us, event | category | flops | bytes accessed | tf_op | source)
XLA Modules:
  0.0 77.7 jit_solution(3990250534638759107)
XLA Ops:
  0.0 1.4 %prepare.1 = (bf16[9,32,512]{2,1,0:T(8,128)(2,1)S(1)}, bf16[9,512,64]{2,1,0:T(8,128)(2,1)S(1)}, bf16[4,64,512]{2,1,0:T(8,128)(2,1)S(1)}, f32[4,16,512]{2,1,0:T(8,128)S(1)}, f32[4,1,512]{2,1,0:T(1,128)S(1)}) custom-call(f32[3,16,512]{2,1,0:T(8,128)} %points_far.1, f32[16,512]{1,0:T(8,128)} %noise_far.1, f32[16,16,512]{2,1,0:T(8,128)} %sides_far.1), custom_call_target="tpu_custom_call" | custom-call | flops 134217728 | bytes 1048576 | tf_op jit(solution)/shard_map/prepare/pallas_call | solution.py:31
  1.4 1.3 %collective-permute-start = (bf16[9,32,512]{2,1,0:T(8,128)(2,1)S(1)}, bf16[9,32,512]{2,1,0:T(8,128)(2,1)S(1)}, u32[]{:S(2)}, u32[]{:S(2)}) collective-permute-start(bf16[9,32,512]{2,1,0:T(8,128)(2,1)S(1)} %get-tuple-element.22.sent), channel_id=1, source_target_pairs={{4,0},{8,4},{12,8},{16,12},{20,16},{24,20},{28,24},{32,28},{36,32}... | collective-permute-start | bytes 884744 | tf_op jit(solution)/shard_map/ppermute | solution.py:416
  2.7 6.2 %within_layer.1 = (f32[4,16,512]{2,1,0:T(8,128)S(1)}, bf16[15,512,512]{2,1,0:T(8,128)(2,1)S(1)}) custom-call(bf16[9,32,512]{2,1,0:T(8,128)(2,1)S(1)} %get-tuple-element.22.sent, bf16[9,512,64]{2,1,0:T(8,128)(2,1)S(1)} %get-tuple-element.23.left, bf16[4,64,512]{2,1,0:T(8,128)(2,1)S(1)} %get-tuple-element.24.right), custom_call_target="tpu_custom_call" | custom-call | flops 8053063680 | bytes 1048576 | tf_op jit(solution)/shard_map/within_layer/pallas_call | solution.py:31
  8.9 0.0 collective-permute-done.above
  8.9 11.1 %above_own.1 = (f32[4,16,512]{2,1,0:T(8,128)S(1)}, bf16[4,16,512]{2,1,0:T(8,128)(2,1)S(1)}, bf16[25,512,512]{2,1,0:T(8,128)(2,1)S(1)}) custom-call(bf16[9,32,512]{2,1,0:T(8,128)(2,1)S(1)} %get-tuple-element.22.sent, bf16[9,512,64]{2,1,0:T(8,128)(2,1)S(1)} %get-tuple-element.23.left, bf16[4,64,512]{2,1,0:T(8,128)(2,1)S(1)} %get-tuple-element.24.right, ...), custom_call_target="tpu_custom_call" | custom-call | flops 13421772800 | bytes 1048576 | tf_op jit(solution)/shard_map/above_own/pallas_call | solution.py:31
  20.1 3.0 %collective-permute-start.1 = (bf16[4,16,512]{2,1,0:T(8,128)(2,1)S(1)}, bf16[4,16,512]{2,1,0:T(8,128)(2,1)S(1)}, u32[]{:S(2)}, u32[]{:S(2)}) collective-permute-start(bf16[4,16,512]{2,1,0:T(8,128)(2,1)S(1)} %get-tuple-element.28), channel_id=1, source_target_pairs={{0,4},{4,8},{8,12},{12,16},{16,20},{20,24},{24,28},{28,32},{32,36}... | collective-permute-start | bytes 196616 | tf_op jit(solution)/shard_map/ppermute | solution.py:416
  23.1 5.2 %borders.1 = (f32[4,16,512]{2,1,0:T(8,128)S(1)}, bf16[3,512,512]{2,1,0:T(8,128)(2,1)S(1)}) custom-call(bf16[9,32,512]{2,1,0:T(8,128)(2,1)S(1)} %get-tuple-element.22.sent, bf16[9,512,64]{2,1,0:T(8,128)(2,1)S(1)} %get-tuple-element.23.left, bf16[4,64,512]{2,1,0:T(8,128)(2,1)S(1)} %get-tuple-element.24.right, ...), custom_call_target="tpu_custom_call" | custom-call | flops 8589934592 | bytes 1048576 | tf_op jit(solution)/shard_map/borders/pallas_call | solution.py:31
  28.3 0.0 collective-permute-done.1.arrived
  28.4 1.3 %collective-permute-start.3 = (bf16[4,16,512]{2,1,0:T(8,128)(2,1)S(1)}, bf16[4,16,512]{2,1,0:T(8,128)(2,1)S(1)}, u32[]{:S(2)}, u32[]{:S(2)}) collective-permute-start(bf16[4,16,512]{2,1,0:T(8,128)(2,1)S(1)} %get-tuple-element.31.rounded), channel_id=1, source_target_pairs={{4,0},{8,4},{12,8},{16,12},{20,16},{24,20},{28,24},{32,28},{36,32}... | collective-permute-start | bytes 196616 | tf_op jit(solution)/shard_map/ppermute | solution.py:416
  29.7 1.7 %collective-permute-start.5 = (bf16[1,16,512]{2,1,0:T(8,128)(2,1)S(1)}, bf16[1,16,512]{2,1,0:T(8,128)(2,1)S(1)}, u32[]{:S(2)}, u32[]{:S(2)}) collective-permute-start(bf16[1,16,512]{2,1,0:T(8,128)(2,1)S(1)} %slice.7), channel_id=1, source_target_pairs={{0,3},{1,2},{2,1},{3,0},{4,7},{5,6},{6,5},{7,4},{8,11},{9,10},{10,... | collective-permute-start | bytes 49160 | tf_op jit(solution)/shard_map/ppermute | solution.py:419
  31.3 2.7 %collective-permute-start.2 = (bf16[2,16,512]{2,1,0:T(8,128)(2,1)S(1)}, bf16[2,16,512]{2,1,0:T(8,128)(2,1)S(1)}, u32[]{:S(2)}, u32[]{:S(2)}) collective-permute-start(bf16[2,16,512]{2,1,0:T(8,128)(2,1)S(1)} %slice.6), channel_id=1, source_target_pairs={{0,2},{1,3},{2,0},{3,1},{4,6},{5,7},{6,4},{7,5},{8,10},{9,11},{10,... | collective-permute-start | bytes 98312 | tf_op jit(solution)/shard_map/ppermute | solution.py:419
  34.0 0.9 %inside.1 = (f32[32,32]{1,0:T(8,128)S(1)}, f32[4,16,512]{2,1,0:T(8,128)S(1)}, bf16[2,16,512]{2,1,0:T(8,128)(2,1)S(1)}) custom-call(f32[4,16,512]{2,1,0:T(8,128)S(1)} %get-tuple-element.30.own_sides, f32[4,16,512]{2,1,0:T(8,128)S(1)} %get-tuple-element.35.image, bf16[4,16,512]{2,1,0:T(8,128)(2,1)S(1)} %get-tuple-element.31.rounded, ...), custom_call_target="tpu_custom_call" | custom-call | flops 2684354560 | bytes 1048576 | tf_op jit(solution)/shard_map/inside/pallas_call | solution.py:31
  34.9 0.3 collective-permute-start.4
  35.2 0.0 collective-permute-done.3.upper
  35.2 1.2 %upward.1.before = f32[4,16,512]{2,1,0:T(8,128)S(1)} custom-call(bf16[4,16,512]{2,1,0:T(8,128)(2,1)S(1)} %collective-permute-done.3.upper, bf16[25,512,512]{2,1,0:T(8,128)(2,1)S(1)} %get-tuple-element.34.tiles.tiles_up, f32[4,16,512]{2,1,0:T(8,128)S(1)} %get-tuple-element.37.before), custom_call_target="tpu_custom_call" | custom-call | flops 4294967296 | bytes 1048576 | tf_op jit(solution)/shard_map/upward/pallas_call | solution.py:31
  36.4 0.0 collective-permute-done.5.from_corner
  36.4 2.7 %collective-permute-done.4.from_row = bf16[2,16,512]{2,1,0:T(8,128)(2,1)S(1)} collective-permute-done((bf16[2,16,512]{2,1,0:T(8,128)(2,1)S(1)}, bf16[2,16,512]{2,1,0:T(8,128)(2,1)S(1)}, u32[]{:S(2)}, u32[]{:S(2)}) %collective-permute-start.4) | collective-permute-done | bytes 32800 | tf_op jit(solution)/shard_map/ppermute | solution.py:419
  39.1 1.5 %by_row.1.so_far = f32[16,16]{1,0:T(8,128)S(1)} custom-call(bf16[2,16,512]{2,1,0:T(8,128)(2,1)S(1)} %collective-permute-done.4.from_row, bf16[1,16,512]{2,1,0:T(8,128)(2,1)S(1)} %collective-permute-done.5.from_corner, bf16[4,16,512]{2,1,0:T(8,128)(2,1)S(1)} %collective-permute-done.3.upper, bf16[15,512,512]{2,1,0:T(8,128)(2,1)S(1)} %get-tuple-element.32.tiles.tiles_early, ...), custom_call_target="tpu_custom_call" | custom-call | flops 2684354560 | bytes 1048576 | tf_op jit(solution)/shard_map/by_row/pallas_call | solution.py:31
  40.7 0.0 collective-permute-done.2.from_column
  40.7 1.0 %by_column.1 = f32[32,8,128]{2,1,0:T(8,128)S(1)} custom-call(bf16[2,16,512]{2,1,0:T(8,128)(2,1)S(1)} %collective-permute-done.2.from_column, bf16[4,16,512]{2,1,0:T(8,128)(2,1)S(1)} %collective-permute-done.3.upper, bf16[15,512,512]{2,1,0:T(8,128)(2,1)S(1)} %get-tuple-element.32.tiles.tiles_early, bf16[3,512,512]{2,1,0:T(8,128)(2,1)S(1)} %get-tuple-element.33.tiles_late, ...), custom_call_target="tpu_custom_call" | custom-call | flops 2147483648 | bytes 1048576 | tf_op jit(solution)/shard_map/by_column/pallas_call | solution.py:31
  41.7 14.9 %all_to_all.10.arrived = f32[32,8,128]{2,1,0:T(8,128)S(1)} all-to-all(f32[32,8,128]{2,1,0:T(8,128)S(1)} %by_column.1), channel_id=1, replica_groups={{0,1,2,3,4,5,6,7,8,9,10,11,12,13,14,15,16,17,18,19,20,21,22,23,24,25,26..., dimensions={0} | all-to-all | bytes 262144 | tf_op jit(solution)/shard_map/all_to_all | solution.py:428
  56.6 18.7 %all_to_all.11.arrived = f32[8,8,128]{2,1,0:T(8,128)S(1)} all-to-all(f32[8,8,128]{2,1,0:T(8,128)S(1)} %add_up.1), channel_id=1, replica_groups={{0,32,64,96,128,160,192,224},{1,33,65,97,129,161,193,225},{2,34,66,98,1..., dimensions={0} | all-to-all | bytes 65536 | tf_op jit(solution)/shard_map/all_to_all | solution.py:428
  75.3 2.5 %conclude.1 = f32[4,16,512]{2,1,0:T(8,128)} custom-call(f32[8,8,128]{2,1,0:T(8,128)S(1)} %all_to_all.11.arrived, f32[4,16,512]{2,1,0:T(8,128)S(1)} %get-tuple-element.30.own_sides, f32[4,16,512]{2,1,0:T(8,128)S(1)} %get-tuple-element.35.image), custom_call_target="tpu_custom_call" | custom-call | flops 134217728 | bytes 1048576 | tf_op jit(solution)/shard_map/conclude/pallas_call | solution.py:31
  (4 shorter events, 0.1 us)
Async XLA Ops:
  1.4 7.5 %collective-permute-start = (bf16[9,32,512]{2,1,0:T(8,128)(2,1)S(1)}, bf16[9,32,512]{2,1,0:T(8,128)(2,1)S(1)}, u32[]{:S(2)}, u32[]{:S(2)}) collective-permute-start(bf16[9,32,512]{2,1,0:T(8,128)(2,1)S(1)} %get-tuple-element.22.sent), channel_id=1, source_target_pairs={{4,0},{8,4},{12,8},{16,12},{20,16},{24,20},{28,24},{32,28},{36,32}... | collective-permute-start | bytes 884744 | tf_op jit(solution)/shard_map/ppermute | solution.py:416
  20.1 8.2 %collective-permute-start.1 = (bf16[4,16,512]{2,1,0:T(8,128)(2,1)S(1)}, bf16[4,16,512]{2,1,0:T(8,128)(2,1)S(1)}, u32[]{:S(2)}, u32[]{:S(2)}) collective-permute-start(bf16[4,16,512]{2,1,0:T(8,128)(2,1)S(1)} %get-tuple-element.28), channel_id=1, source_target_pairs={{0,4},{4,8},{8,12},{12,16},{16,20},{20,24},{24,28},{28,32},{32,36}... | collective-permute-start | bytes 196616 | tf_op jit(solution)/shard_map/ppermute | solution.py:416
  28.4 6.9 %collective-permute-start.3 = (bf16[4,16,512]{2,1,0:T(8,128)(2,1)S(1)}, bf16[4,16,512]{2,1,0:T(8,128)(2,1)S(1)}, u32[]{:S(2)}, u32[]{:S(2)}) collective-permute-start(bf16[4,16,512]{2,1,0:T(8,128)(2,1)S(1)} %get-tuple-element.31.rounded), channel_id=1, source_target_pairs={{4,0},{8,4},{12,8},{16,12},{20,16},{24,20},{28,24},{32,28},{36,32}... | collective-permute-start | bytes 196616 | tf_op jit(solution)/shard_map/ppermute | solution.py:416
  29.7 6.8 %collective-permute-start.5 = (bf16[1,16,512]{2,1,0:T(8,128)(2,1)S(1)}, bf16[1,16,512]{2,1,0:T(8,128)(2,1)S(1)}, u32[]{:S(2)}, u32[]{:S(2)}) collective-permute-start(bf16[1,16,512]{2,1,0:T(8,128)(2,1)S(1)} %slice.7), channel_id=1, source_target_pairs={{0,3},{1,2},{2,1},{3,0},{4,7},{5,6},{6,5},{7,4},{8,11},{9,10},{10,... | collective-permute-start | bytes 49160 | tf_op jit(solution)/shard_map/ppermute | solution.py:419
  31.3 9.3 %collective-permute-start.2 = (bf16[2,16,512]{2,1,0:T(8,128)(2,1)S(1)}, bf16[2,16,512]{2,1,0:T(8,128)(2,1)S(1)}, u32[]{:S(2)}, u32[]{:S(2)}) collective-permute-start(bf16[2,16,512]{2,1,0:T(8,128)(2,1)S(1)} %slice.6), channel_id=1, source_target_pairs={{0,2},{1,3},{2,0},{3,1},{4,6},{5,7},{6,4},{7,5},{8,10},{9,11},{10,... | collective-permute-start | bytes 98312 | tf_op jit(solution)/shard_map/ppermute | solution.py:419
  34.9 4.2 %collective-permute-start.4 = (bf16[2,16,512]{2,1,0:T(8,128)(2,1)S(1)}, bf16[2,16,512]{2,1,0:T(8,128)(2,1)S(1)}, u32[]{:S(2)}, u32[]{:S(2)}) collective-permute-start(bf16[2,16,512]{2,1,0:T(8,128)(2,1)S(1)} %get-tuple-element.36), channel_id=1, source_target_pairs={{0,1},{1,0},{2,3},{3,2},{4,5},{5,4},{6,7},{7,6},{8,9},{9,8},{10,11... | collective-permute-start | bytes 98312 | tf_op jit(solution)/shard_map/ppermute | solution.py:419

commit v9 on v7

--- a/solution.py
+++ b/solution.py
@@ -287,12 +287,14 @@
         partial[i] = own_noise[i] * image[i] * 256.0 + single + 2.0 * double[i]
 
 
-def upward(upper, tiles, before, partial):
+def upward(upper, tiles, before, image, third):
     double = [jnp.zeros((RHS, BLOCK), f32)] * 4
     for step in range(16):
         double[step % 4] += times(upper[step // 4], tiles[step])
-    for i in range(4):
-        partial[i] = before[i] + 2.0 * double[i]
+    third[...] = gram(
+        side_by_side([image[i] for i in range(4)]),
+        side_by_side([before[i] + 2.0 * double[i] for i in range(4)]),
+    )
 
 
 def cross_products(border, tiles_early, tiles_late, tiles_up, single, raised):
@@ -304,25 +306,27 @@
             raised[i] += times(border[j], tiles_up[16 + step])
 
 
-def by_row(from_row, from_corner, upper, tiles_early, tiles_late, tiles_up, before, image, third):
-    border = {6: from_row[0], 7: from_row[1], 8: from_corner[0]}
-    single = [before[i] for i in range(4)]
-    raised = [jnp.zeros((RHS, BLOCK), f32)] * 4
-    cross_products(border, tiles_early, tiles_late, tiles_up, single, raised)
-    third[...] = gram(
-        side_by_side([image[i] for i in range(4)] + [upper[i].astype(f32) for i in range(4)]),
-        side_by_side(single + [2.0 * raised[i] for i in range(4)]),
-    )
-
-
-def by_column(from_column, upper, tiles_early, tiles_late, tiles_up, so_far, image, products, copies):
+def by_column(from_column, so_far, tiles_early, tiles_late, tiles_up, single_out, raised_out):
     border = {4: from_column[0], 5: from_column[1]}
     single = [jnp.zeros((RHS, BLOCK), f32)] * 4
     raised = [jnp.zeros((RHS, BLOCK), f32)] * 4
     cross_products(border, tiles_early, tiles_late, tiles_up, single, raised)
+    for i in range(4):
+        single_out[i] = single[i]
+        raised_out[i] = raised[i]
+
+
+def by_row(
+    from_row, from_corner, upper, tiles_early, tiles_late, tiles_up, single_in, raised_in,
+    so_far, image, products, copies,
+):
+    border = {6: from_row[0], 7: from_row[1], 8: from_corner[0]}
+    single = [single_in[i] for i in range(4)]
+    raised = [raised_in[i] for i in range(4)]
+    cross_products(border, tiles_early, tiles_late, tiles_up, single, raised)
     third = (so_far[...] + gram(
-        side_by_side([image[i] for i in (1, 3)] + [upper[i].astype(f32) for i in (1, 3)]),
-        side_by_side([single[i] for i in (1, 3)] + [2.0 * raised[i] for i in (1, 3)]),
+        side_by_side([image[i] for i in range(1, 4)] + [upper[i].astype(f32) for i in range(1, 4)]),
+        side_by_side([single[i] for i in range(1, 4)] + [2.0 * raised[i] for i in range(1, 4)]),
     )) * (1.0 / 256.0)
     known = products[...]
     ordered = jnp.concatenate(
@@ -477,19 +481,19 @@
         inside, "inside", (shape(32, 32), shape(*field)),
         (own_sides, image, rounded, own_noise, tiles_early), 10 * 2 * tile_flops,
     )
-    partial = call(
-        upward, "upward", shape(*field), (upper, tiles_up, partial), 16 * 2 * tile_flops,
-    )
     third = call(
-        by_row, "by_row", shape(RHS, RHS),
-        (from_row, from_corner, upper, tiles_early, tiles_late, tiles_up, partial, image),
-        10 * 2 * tile_flops,
+        upward, "upward", shape(RHS, RHS), (upper, tiles_up, partial, image), 16 * 2 * tile_flops,
+    )
+    single, raised = call(
+        by_column, "by_column", (shape(*field), shape(*field)),
+        (from_column, third, tiles_early, tiles_late, tiles_up), 8 * 2 * tile_flops,
     )
     plane = 8 * members
     copies = call(
-        by_column, "by_column", shape(plane, 8, 128),
-        (from_column, upper, tiles_early, tiles_late, tiles_up, third, image, products),
-        8 * 2 * tile_flops,
+        by_row, "by_row", shape(plane, 8, 128),
+        (from_row, from_corner, upper, tiles_early, tiles_late, tiles_up, single, raised,
+         third, image, products),
+        10 * 2 * tile_flops,
     )
     arrived = swap(copies, 1)
     copies = call(add_up, "add_up", shape(everyone // plane, 8, 128), (arrived,), 1024)

time: 76.8 us -> 76.2 us (level)
  transfers between devices with their start and end apart: 6 -> 6, of which waited for: 1 -> 2; matrix products, arithmetic and copies ran while one was open for 0% -> 0% of each run, Pallas kernels for 20% -> 19%
where the time goes in v9:
time: 76.2 us; the launch traced here: 75.1 us
  blocking collectives  33.7 us (44%)
  Pallas kernels  30.6 us (40%)
  starting transfers between devices  9.96 us (13%)
  waiting for transfers between devices  0.8 us (1%)
    all_to_all x2, blocking collectives, swap(): lax.all_to_all(copies, ('region', 'sub'), 0, 0, axis_index_groups=groups,...  33.7 us
    pallas_call x11, Pallas kernels, call(): pl.pallas_call(kernel, name=name, out_shape=out_shape, in_specs=[pl.Block...  30.6 us
    ppermute x3, starting transfers between devices, from_region(): return lax.ppermute(value, 'region', pairs)  5.61 us
    ppermute x3, starting transfers between devices, from_member(): lax.ppermute(value, 'sub', [(source, source ^ mask) for source in range(m...  4.35 us
  transfers between devices with their start and end apart: 6, of which 2 were waited for; matrix products, arithmetic and copies ran while one was open for 0% of the time, Pallas kernels for 19%

profile of v9, /device:TPU:8, one launch (start us, length us, event | category | flops | bytes accessed | tf_op | source)
XLA Modules:
  0.0 75.1 jit_solution(14846933433887305452)
XLA Ops:
  0.0 1.4 %prepare.1 = (bf16[9,32,512]{2,1,0:T(8,128)(2,1)S(1)}, bf16[9,512,64]{2,1,0:T(8,128)(2,1)S(1)}, bf16[4,64,512]{2,1,0:T(8,128)(2,1)S(1)}, f32[4,16,512]{2,1,0:T(8,128)S(1)}, f32[4,1,512]{2,1,0:T(1,128)S(1)}) custom-call(f32[3,16,512]{2,1,0:T(8,128)} %points_far.1, f32[16,512]{1,0:T(8,128)} %noise_far.1, f32[16,16,512]{2,1,0:T(8,128)} %sides_far.1), custom_call_target="tpu_custom_call" | custom-call | flops 134217728 | bytes 1048576 | tf_op jit(solution)/shard_map/prepare/pallas_call | solution.py:31
  1.4 1.3 %collective-permute-start = (bf16[9,32,512]{2,1,0:T(8,128)(2,1)S(1)}, bf16[9,32,512]{2,1,0:T(8,128)(2,1)S(1)}, u32[]{:S(2)}, u32[]{:S(2)}) collective-permute-start(bf16[9,32,512]{2,1,0:T(8,128)(2,1)S(1)} %get-tuple-element.23.sent), channel_id=1, source_target_pairs={{4,0},{8,4},{12,8},{16,12},{20,16},{24,20},{28,24},{32,28},{36,32}... | collective-permute-start | bytes 884744 | tf_op jit(solution)/shard_map/ppermute | solution.py:419
  2.7 6.2 %within_layer.1 = (f32[4,16,512]{2,1,0:T(8,128)S(1)}, bf16[15,512,512]{2,1,0:T(8,128)(2,1)S(1)}) custom-call(bf16[9,32,512]{2,1,0:T(8,128)(2,1)S(1)} %get-tuple-element.23.sent, bf16[9,512,64]{2,1,0:T(8,128)(2,1)S(1)} %get-tuple-element.24.left, bf16[4,64,512]{2,1,0:T(8,128)(2,1)S(1)} %get-tuple-element.25.right), custom_call_target="tpu_custom_call" | custom-call | flops 8053063680 | bytes 1048576 | tf_op jit(solution)/shard_map/within_layer/pallas_call | solution.py:31
  8.9 0.0 collective-permute-done.above
  8.9 11.1 %above_own.1 = (f32[4,16,512]{2,1,0:T(8,128)S(1)}, bf16[4,16,512]{2,1,0:T(8,128)(2,1)S(1)}, bf16[25,512,512]{2,1,0:T(8,128)(2,1)S(1)}) custom-call(bf16[9,32,512]{2,1,0:T(8,128)(2,1)S(1)} %get-tuple-element.23.sent, bf16[9,512,64]{2,1,0:T(8,128)(2,1)S(1)} %get-tuple-element.24.left, bf16[4,64,512]{2,1,0:T(8,128)(2,1)S(1)} %get-tuple-element.25.right, ...), custom_call_target="tpu_custom_call" | custom-call | flops 13421772800 | bytes 1048576 | tf_op jit(solution)/shard_map/above_own/pallas_call | solution.py:31
  20.0 3.0 %collective-permute-start.1 = (bf16[4,16,512]{2,1,0:T(8,128)(2,1)S(1)}, bf16[4,16,512]{2,1,0:T(8,128)(2,1)S(1)}, u32[]{:S(2)}, u32[]{:S(2)}) collective-permute-start(bf16[4,16,512]{2,1,0:T(8,128)(2,1)S(1)} %get-tuple-element.29), channel_id=1, source_target_pairs={{0,4},{4,8},{8,12},{12,16},{16,20},{20,24},{24,28},{28,32},{32,36}... | collective-permute-start | bytes 196616 | tf_op jit(solution)/shard_map/ppermute | solution.py:419
  23.0 5.2 %borders.1 = (f32[4,16,512]{2,1,0:T(8,128)S(1)}, bf16[3,512,512]{2,1,0:T(8,128)(2,1)S(1)}) custom-call(bf16[9,32,512]{2,1,0:T(8,128)(2,1)S(1)} %get-tuple-element.23.sent, bf16[9,512,64]{2,1,0:T(8,128)(2,1)S(1)} %get-tuple-element.24.left, bf16[4,64,512]{2,1,0:T(8,128)(2,1)S(1)} %get-tuple-element.25.right, ...), custom_call_target="tpu_custom_call" | custom-call | flops 8589934592 | bytes 1048576 | tf_op jit(solution)/shard_map/borders/pallas_call | solution.py:31
  28.2 0.0 collective-permute-done.1.arrived
  28.3 1.3 %collective-permute-start.4 = (bf16[4,16,512]{2,1,0:T(8,128)(2,1)S(1)}, bf16[4,16,512]{2,1,0:T(8,128)(2,1)S(1)}, u32[]{:S(2)}, u32[]{:S(2)}) collective-permute-start(bf16[4,16,512]{2,1,0:T(8,128)(2,1)S(1)} %get-tuple-element.32.rounded), channel_id=1, source_target_pairs={{4,0},{8,4},{12,8},{16,12},{20,16},{24,20},{28,24},{32,28},{36,32}... | collective-permute-start | bytes 196616 | tf_op jit(solution)/shard_map/ppermute | solution.py:419
  29.6 1.7 %collective-permute-start.3 = (bf16[1,16,512]{2,1,0:T(8,128)(2,1)S(1)}, bf16[1,16,512]{2,1,0:T(8,128)(2,1)S(1)}, u32[]{:S(2)}, u32[]{:S(2)}) collective-permute-start(bf16[1,16,512]{2,1,0:T(8,128)(2,1)S(1)} %slice.10), channel_id=1, source_target_pairs={{0,3},{1,2},{2,1},{3,0},{4,7},{5,6},{6,5},{7,4},{8,11},{9,10},{10,... | collective-permute-start | bytes 49160 | tf_op jit(solution)/shard_map/ppermute | solution.py:422
  31.3 2.7 %collective-permute-start.5 = (bf16[2,16,512]{2,1,0:T(8,128)(2,1)S(1)}, bf16[2,16,512]{2,1,0:T(8,128)(2,1)S(1)}, u32[]{:S(2)}, u32[]{:S(2)}) collective-permute-start(bf16[2,16,512]{2,1,0:T(8,128)(2,1)S(1)} %get-tuple-element.41), channel_id=1, source_target_pairs={{0,2},{1,3},{2,0},{3,1},{4,6},{5,7},{6,4},{7,5},{8,10},{9,11},{10,... | collective-permute-start | bytes 98312 | tf_op jit(solution)/shard_map/ppermute | solution.py:422
  33.9 0.0 collective-permute-start.2
  33.9 0.9 %inside.1 = (f32[32,32]{1,0:T(8,128)S(1)}, f32[4,16,512]{2,1,0:T(8,128)S(1)}) custom-call(f32[4,16,512]{2,1,0:T(8,128)S(1)} %get-tuple-element.31.own_sides, f32[4,16,512]{2,1,0:T(8,128)S(1)} %get-tuple-element.36.image, bf16[4,16,512]{2,1,0:T(8,128)(2,1)S(1)} %get-tuple-element.32.rounded, f32[4,1,512]{2,1,0:T(1,128)S(1)} %get-tuple-element.30.own_noise, ...), custom_call_target="tpu_custom_call" | custom-call | flops 2684354560 | bytes 1048576 | tf_op jit(solution)/shard_map/inside/pallas_call | solution.py:31
  34.9 0.0 collective-permute-done.4.upper
  34.9 1.5 %upward.1.so_far = f32[16,16]{1,0:T(8,128)S(1)} custom-call(bf16[4,16,512]{2,1,0:T(8,128)(2,1)S(1)} %collective-permute-done.4.upper, bf16[25,512,512]{2,1,0:T(8,128)(2,1)S(1)} %get-tuple-element.35.tiles.tiles_up, f32[4,16,512]{2,1,0:T(8,128)S(1)} %get-tuple-element.37.before, f32[4,16,512]{2,1,0:T(8,128)S(1)} %get-tuple-element.36.image), custom_call_target="tpu_custom_call" | custom-call | flops 4294967296 | bytes 1048576 | tf_op jit(solution)/shard_map/upward/pallas_call | solution.py:31
  36.4 0.2 collective-permute-done.5.from_column
  36.7 0.6 by_column.1
  37.3 0.0 collective-permute-done.3.from_corner
  37.3 0.5 collective-permute-done.2.from_row
  37.9 1.1 %by_row.1 = f32[32,8,128]{2,1,0:T(8,128)S(1)} custom-call(bf16[2,16,512]{2,1,0:T(8,128)(2,1)S(1)} %collective-permute-done.2.from_row, bf16[1,16,512]{2,1,0:T(8,128)(2,1)S(1)} %collective-permute-done.3.from_corner, bf16[4,16,512]{2,1,0:T(8,128)(2,1)S(1)} %collective-permute-done.4.upper, bf16[15,512,512]{2,1,0:T(8,128)(2,1)S(1)} %get-tuple-element.33.tiles.tiles_early, ...), custom_call_target="tpu_custom_call" | custom-call | flops 2684354560 | bytes 1048576 | tf_op jit(solution)/shard_map/by_row/pallas_call | solution.py:31
  39.0 16.6 %all_to_all.10.arrived = f32[32,8,128]{2,1,0:T(8,128)S(1)} all-to-all(f32[32,8,128]{2,1,0:T(8,128)S(1)} %by_row.1), channel_id=1, replica_groups={{0,1,2,3,4,5,6,7,8,9,10,11,12,13,14,15,16,17,18,19,20,21,22,23,24,25,26..., dimensions={0} | all-to-all | bytes 262144 | tf_op jit(solution)/shard_map/all_to_all | solution.py:431
  55.6 17.1 %all_to_all.11.arrived = f32[8,8,128]{2,1,0:T(8,128)S(1)} all-to-all(f32[8,8,128]{2,1,0:T(8,128)S(1)} %add_up.1), channel_id=1, replica_groups={{0,32,64,96,128,160,192,224},{1,33,65,97,129,161,193,225},{2,34,66,98,1..., dimensions={0} | all-to-all | bytes 65536 | tf_op jit(solution)/shard_map/all_to_all | solution.py:431
  72.7 2.4 %conclude.1 = f32[4,16,512]{2,1,0:T(8,128)} custom-call(f32[8,8,128]{2,1,0:T(8,128)S(1)} %all_to_all.11.arrived, f32[4,16,512]{2,1,0:T(8,128)S(1)} %get-tuple-element.31.own_sides, f32[4,16,512]{2,1,0:T(8,128)S(1)} %get-tuple-element.36.image), custom_call_target="tpu_custom_call" | custom-call | flops 134217728 | bytes 1048576 | tf_op jit(solution)/shard_map/conclude/pallas_call | solution.py:31
  (4 shorter events, 0.1 us)
Async XLA Ops:
  1.4 7.5 %collective-permute-start = (bf16[9,32,512]{2,1,0:T(8,128)(2,1)S(1)}, bf16[9,32,512]{2,1,0:T(8,128)(2,1)S(1)}, u32[]{:S(2)}, u32[]{:S(2)}) collective-permute-start(bf16[9,32,512]{2,1,0:T(8,128)(2,1)S(1)} %get-tuple-element.23.sent), channel_id=1, source_target_pairs={{4,0},{8,4},{12,8},{16,12},{20,16},{24,20},{28,24},{32,28},{36,32}... | collective-permute-start | bytes 884744 | tf_op jit(solution)/shard_map/ppermute | solution.py:419
  20.0 8.2 %collective-permute-start.1 = (bf16[4,16,512]{2,1,0:T(8,128)(2,1)S(1)}, bf16[4,16,512]{2,1,0:T(8,128)(2,1)S(1)}, u32[]{:S(2)}, u32[]{:S(2)}) collective-permute-start(bf16[4,16,512]{2,1,0:T(8,128)(2,1)S(1)} %get-tuple-element.29), channel_id=1, source_target_pairs={{0,4},{4,8},{8,12},{12,16},{16,20},{20,24},{24,28},{28,32},{32,36}... | collective-permute-start | bytes 196616 | tf_op jit(solution)/shard_map/ppermute | solution.py:419
  28.3 6.6 %collective-permute-start.4 = (bf16[4,16,512]{2,1,0:T(8,128)(2,1)S(1)}, bf16[4,16,512]{2,1,0:T(8,128)(2,1)S(1)}, u32[]{:S(2)}, u32[]{:S(2)}) collective-permute-start(bf16[4,16,512]{2,1,0:T(8,128)(2,1)S(1)} %get-tuple-element.32.rounded), channel_id=1, source_target_pairs={{4,0},{8,4},{12,8},{16,12},{20,16},{24,20},{28,24},{32,28},{36,32}... | collective-permute-start | bytes 196616 | tf_op jit(solution)/shard_map/ppermute | solution.py:419
  29.6 7.7 %collective-permute-start.3 = (bf16[1,16,512]{2,1,0:T(8,128)(2,1)S(1)}, bf16[1,16,512]{2,1,0:T(8,128)(2,1)S(1)}, u32[]{:S(2)}, u32[]{:S(2)}) collective-permute-start(bf16[1,16,512]{2,1,0:T(8,128)(2,1)S(1)} %slice.10), channel_id=1, source_target_pairs={{0,3},{1,2},{2,1},{3,0},{4,7},{5,6},{6,5},{7,4},{8,11},{9,10},{10,... | collective-permute-start | bytes 49160 | tf_op jit(solution)/shard_map/ppermute | solution.py:422
  31.3 5.4 %collective-permute-start.5 = (bf16[2,16,512]{2,1,0:T(8,128)(2,1)S(1)}, bf16[2,16,512]{2,1,0:T(8,128)(2,1)S(1)}, u32[]{:S(2)}, u32[]{:S(2)}) collective-permute-start(bf16[2,16,512]{2,1,0:T(8,128)(2,1)S(1)} %get-tuple-element.41), channel_id=1, source_target_pairs={{0,2},{1,3},{2,0},{3,1},{4,6},{5,7},{6,4},{7,5},{8,10},{9,11},{10,... | collective-permute-start | bytes 98312 | tf_op jit(solution)/shard_map/ppermute | solution.py:422
  33.9 3.9 %collective-permute-start.2 = (bf16[2,16,512]{2,1,0:T(8,128)(2,1)S(1)}, bf16[2,16,512]{2,1,0:T(8,128)(2,1)S(1)}, u32[]{:S(2)}, u32[]{:S(2)}) collective-permute-start(bf16[2,16,512]{2,1,0:T(8,128)(2,1)S(1)} %get-tuple-element.42), channel_id=1, source_target_pairs={{0,1},{1,0},{2,3},{3,2},{4,5},{5,4},{6,7},{7,6},{8,9},{9,8},{10,11... | collective-permute-start | bytes 98312 | tf_op jit(solution)/shard_map/ppermute | solution.py:422
